TPU v7x, 128 devices: a whole 4x4x4 slice. The times are simulated.
128 devices in a mesh: adapter: 16 (over x, z), tensor: 8 (over y, core).
Axes of the slice: x: 4, y: 4, z: 4, core: 2. Of those that a mesh axis runs over, the one named last changes fastest.
Arguments:
- tokens: bfloat16 [8192, 8192], P(('adapter', 'tensor')), may hold values from -6 to 6
- token_adapter_index: int32 [8192], P(('adapter', 'tensor')), may hold values from 0 to 1023, as said below
- joined_weight_matrix: bfloat16 [8192, 10240], P(None, 'tensor'), may hold values from -0.0625 to 0.0625
- adapter_down_weight: bfloat16 [1024, 16, 8192], P('adapter', None, 'tensor'), may hold values from -0.0625 to 0.0625
- adapter_up_weight: bfloat16 [1024, 16, 10240], P('adapter', None, 'tensor'), may hold values from -0.75 to 0.75
Outputs:
- projected: bfloat16 [8192, 10240], P('adapter', 'tensor')
Inputs may be any that keep to these rules, and one draw needn't show every extreme that they name: `token_adapter_index`: in every aligned block of 512 rows, at most 128 rows name adapters of one owner, owner o holding adapters o * 64 to (o + 1) * 64 - 1; one owner gets exactly 128 rows of every block.
All inputs are finite; a program needn't handle non-finite values.
Results may differ from a plain program's by a relative error of at most 0.0049.
Values may be sent and summed in bfloat16 or wider, within the bound.
No kernel may reach another device: no remote copies, remote signals or barrier semaphores. Data moves between devices by JAX's collectives and lax.ppermute only.
A program may use at most 128 MiB of HBM per device.

v0:
```python
import jax
import jax.numpy as jnp
from jax import lax
from jax.sharding import PartitionSpec as P


def per_device(
    tokens, token_adapter_index, joined_weight_matrix, adapter_down_weight, adapter_up_weight
):
    gathered, group_ids = (
        lax.all_gather(tokens, "tensor", axis=0, tiled=True),
        lax.all_gather(token_adapter_index, "tensor", axis=0, tiled=True),
    )
    owners = lax.axis_size("adapter")
    group = gathered.shape[0]
    held_rows = adapter_down_weight.shape[0]
    rank_value = adapter_down_weight.shape[1]
    slice_column_width = adapter_down_weight.shape[2]
    column_width = adapter_up_weight.shape[2]
    capacity = 4 * group // owners
    slots = owners * capacity
    owner_of = group_ids // held_rows
    local_of = group_ids % held_rows
    owner_hot = (owner_of[:, None] == jnp.arange(owners, dtype=jnp.int32)[None, :]).astype(
        jnp.int32
    )
    rank_in = jnp.sum((jnp.cumsum(owner_hot, axis=0) - 1) * owner_hot, axis=1)
    target = owner_of * capacity + rank_in
    placing = target[None, :] == jnp.arange(slots, dtype=jnp.int32)[:, None]
    dispatch = placing.astype(jnp.bfloat16)
    start_col = lax.axis_index("tensor") * slice_column_width
    feature_part = lax.dynamic_slice_in_dim(gathered, start_col, slice_column_width, 1)
    send_rows = jnp.dot(dispatch, feature_part, preferred_element_type=jnp.float32).astype(
        jnp.bfloat16
    )
    send_local = jnp.sum(placing.astype(jnp.int32) * (local_of + 1)[None, :], axis=1) - 1
    send_rows = send_rows.reshape(owners, capacity, slice_column_width)
    send_local = send_local.reshape(owners, capacity)
    flattened_down = adapter_down_weight.reshape(held_rows * rank_value, slice_column_width)
    flattened_up = adapter_up_weight.reshape(held_rows * rank_value, column_width)
    recv_rows, recv_local = (
        lax.all_to_all(send_rows, "adapter", split_axis=0, concat_axis=0, tiled=True),
        lax.all_to_all(send_local, "adapter", split_axis=0, concat_axis=0, tiled=True),
    )
    first = recv_rows.shape[0]
    items = recv_rows.shape[1]
    count = first * items
    rows = recv_rows.reshape(count, slice_column_width)
    select = (
        recv_local.reshape(count)[:, None] == jnp.arange(held_rows, dtype=jnp.int32)[None, :]
    ).astype(jnp.float32)
    partial_low = jnp.einsum("sd,kd->sk", rows, flattened_down, preferred_element_type=jnp.float32)
    partial_low = jnp.sum(
        partial_low.reshape(count, held_rows, rank_value) * select[:, :, None], axis=1
    )
    low = lax.psum(partial_low, "tensor")
    low_rounded = low.astype(jnp.bfloat16)
    expanded = (select.astype(jnp.bfloat16)[:, :, None] * low_rounded[:, None, :]).reshape(
        count, held_rows * rank_value
    )
    delta = (2.0 * jnp.dot(expanded, flattened_up, preferred_element_type=jnp.float32)).astype(
        jnp.bfloat16
    )
    returned = lax.all_to_all(
        delta.reshape(first, items, column_width),
        "adapter",
        split_axis=0,
        concat_axis=0,
        tiled=True,
    )
    base = jnp.dot(gathered, joined_weight_matrix, preferred_element_type=jnp.float32)
    delta_rows = jnp.einsum(
        "sg,sc->gc",
        dispatch,
        returned.reshape(slots, column_width),
        preferred_element_type=jnp.float32,
    )
    return (base + delta_rows).astype(jnp.bfloat16)


def solution(mesh):
    return jax.shard_map(
        per_device,
        mesh=mesh,
        in_specs=(
            P(("adapter", "tensor"), None),
            P(("adapter", "tensor")),
            P(None, "tensor"),
            P("adapter", None, "tensor"),
            P("adapter", None, "tensor"),
        ),
        out_specs=P("adapter", "tensor"),
        check_vma=False,
    )
```

profile of v0, /device:TPU:2, one launch (start us, length us, event | category | flops | bytes accessed | tf_op | source)
XLA Modules:
  0.0 267.1 jit_solution(6267148403461118507)
XLA Ops:
  6.5 0.0 copy-start
  6.5 0.0 all-gather.2.cloned.1.call-start
  6.5 0.7 all-gather.2.cloned.1.call-update
  7.3 1.3 dynamic-slice
  9.2 0.9 dynamic-update-slice
  10.1 9.5 %all-reduce = s32[512]{0:T(512)S(1)} all-reduce(s32[512]{0:T(512)S(1)} %dynamic-update-slice), channel_id=1, replica_groups=mesh['adapter'=16,'tensor'=8] {'tensor'}, use_global_device_ids=true, to_apply=%add | all-reduce | flops 512 | bytes 4096
  19.6 1.2 reduce-window.6
  20.7 0.2 slice_reduce_fusion
  21.0 0.1 fusion.16
  21.1 0.5 select_reduce_fusion
  21.6 0.6 broadcast_add_fusion
  22.2 8.3 %all-to-all-start = ((s32[16,1,128]{2,1,0:T(1,128)}), s32[16,1,128]{2,1,0:T(1,128)S(1)}, u32[]{:S(2)}, u32[]{:S(2)}) async-start(s32[16,1,128]{2,1,0:T(1,128)} %bitcast.3), calls=%async_computation | async-start | bytes 16384 | tf_op jit(solution)/shard_map/all_to_all | solution.py:43
  30.6 30.6 %all-gather.2.cloned.1.call-done = bf16[512,8192]{1,0:T(8,128)(2,1)} async-done(((bf16[64,8192]{1,0:T(8,128)(2,1)}), bf16[512,8192]{1,0:T(8,128)(2,1)}) %all-gather.2.cloned.1.call-update) | async-done | bytes 8388624 | tf_op jit(solution)/shard_map/all_gather | solution.py:11
  61.2 5.5 %fusion.4 = bf16[2048,1024]{1,0:T(8,128)(2,1)} fusion(s32[512]{0:T(512)S(1)} %multiply_add_fusion, bf16[512,8192]{1,0:T(8,128)(2,1)} %all-gather.2.cloned.1.call-done, s32[]{:T(128)S(6)} %select_n.17), kind=kOutput, calls=%fused_computation.8 | convolution fusion | flops 2150629376 | bytes 5244932 | tf_op jit(solution)/shard_map/dot_general | solution.py:33
  66.7 0.0 all-to-all-done
  66.7 7.4 %all-to-all-start.1 = ((bf16[16,128,1024]{2,1,0:T(8,128)(2,1)}), bf16[16,128,1024]{2,1,0:T(8,128)(2,1)}, u32[]{:S(2)}, u32[]{:S(2)}) async-start(bf16[16,128,1024]{2,1,0:T(8,128)(2,1)} %bitcast.35), calls=%async_computation.1 | async-start | bytes 8388608 | tf_op jit(solution)/shard_map/all_to_all | solution.py:42
  74.1 0.1 fusion.14
  74.2 54.8 %all-to-all-done.1 = bf16[16,128,1024]{2,1,0:T(8,128)(2,1)} async-done(((bf16[16,128,1024]{2,1,0:T(8,128)(2,1)}), bf16[16,128,1024]{2,1,0:T(8,128)(2,1)}, u32[]{:S(2)}, u32[]{:S(2)}) %all-to-all-start.1) | async-done | bytes 4194336 | tf_op jit(solution)/shard_map/all_to_all | solution.py:42
  129.0 7.9 %multiply_reduce_fusion = f32[2048,16]{0,1:T(8,128)S(1)} fusion(f32[2048,64]{0,1:T(8,128)S(1)} %get-tuple-element.6, bf16[2048,1024,1]{1,0,2:T(8,128)(2,1)} %bitcast.7, bf16[64,16,1024]{2,1,0:T(8,128)(2,1)} %param.8), kind=kOutput, calls=%fused_computation.2 | convolution fusion | flops 4299128832 | bytes 6946816 | tf_op jit(solution)/shard_map/sd,kd->sk/dot_general | solution.py:52
  136.9 24.7 %all-reduce.2 = bf16[2048,16]{0,1:T(8,128)(2,1)S(1)} all-reduce(f32[2048,16]{0,1:T(8,128)S(1)} %multiply_reduce_fusion), channel_id=1, replica_groups=mesh['adapter'=16,'tensor'=8] {'tensor'}, use_global_device_ids=true, to_apply=%region_5.6 | all-reduce | flops 32768 | bytes 196608 | tf_op jit(solution)/shard_map/psum | solution.py:56
  161.7 0.0 copy-done
  161.7 6.4 %fusion = bf16[2048,1280]{1,0:T(8,128)(2,1)S(1)} fusion(bf16[64,16,1280]{2,1,0:T(8,128)(2,1)S(1)} %copy-done, bf16[2048,16]{0,1:T(8,128)(2,1)S(1)} %all-reduce.2, bf16[2048,64]{0,1:T(8,128)(2,1)S(1)} %get-tuple-element.5), kind=kOutput, calls=%fused_computation.1 | convolution fusion | flops 5376049152 | bytes 8192000 | tf_op jit(solution)/shard_map/dot_general | solution.py:61
  168.1 0.0 slice-start
  168.1 73.3 %all_to_all.16 = bf16[16,128,1280]{2,1,0:T(8,128)(2,1)S(1)} all-to-all(bf16[16,128,1280]{2,1,0:T(8,128)(2,1)S(1)} %bitcast.33), channel_id=1, replica_groups=mesh['adapter'=16,'tensor'=8] {'adapter'}, dimensions={0} | all-to-all | bytes 10485760 | tf_op jit(solution)/shard_map/all_to_all | solution.py:64
  241.4 0.0 slice-start.1
  241.4 3.3 %fusion.2 = f32[512,1280]{1,0:T(8,128)S(1)} fusion(bf16[2048,1280]{1,0:T(8,128)(2,1)S(1)} %bitcast.34, s32[512]{0:T(512)S(1)} %multiply_add_fusion), kind=kOutput, calls=%fused_computation.6 | convolution fusion | flops 2685403136 | bytes 7866368 | tf_op jit(solution)/shard_map/sg,sc->gc/dot_general | solution.py:72
  244.7 0.0 slice-done
  244.7 0.0 slice-done.1
  244.7 15.5 %fusion.5 = bf16[512,1280]{1,0:T(8,128)(2,1)} fusion(f32[512,1280]{1,0:T(8,128)S(1)} %fusion.2, bf16[512,8192]{1,0:T(8,128)(2,1)S(1)} %bitcast.39, bf16[8192,1280]{1,0:T(8,128)(2,1)} %param.7), kind=kOutput, calls=%fused_computation.10 | convolution fusion | flops 10738728960 | bytes 33292288 | tf_op jit(solution)/shard_map/dot_general | solution.py:71
  (7 shorter events, 0.1 us)
Async XLA Ops:
  6.5 155.1 %copy-start = (bf16[64,16,1280]{2,1,0:T(8,128)(2,1)S(1)}, bf16[64,16,1280]{2,1,0:T(8,128)(2,1)}, u32[]{:S(2)}) copy-start(bf16[64,16,1280]{2,1,0:T(8,128)(2,1)} %param.9) | copy-start | bytes 7864324
  6.5 54.7 %all-gather.2.cloned.1.call-start = ((), (), s32[]{:S(2)}) async-start(), calls=%async_computation.3 | async-start | bytes 9437184 | tf_op jit(solution)/shard_map/all_gather | solution.py:11
  22.2 44.5 %all-to-all-start = ((s32[16,1,128]{2,1,0:T(1,128)}), s32[16,1,128]{2,1,0:T(1,128)S(1)}, u32[]{:S(2)}, u32[]{:S(2)}) async-start(s32[16,1,128]{2,1,0:T(1,128)} %bitcast.3), calls=%async_computation | async-start | bytes 16384 | tf_op jit(solution)/shard_map/all_to_all | solution.py:43
  66.7 62.3 %all-to-all-start.1 = ((bf16[16,128,1024]{2,1,0:T(8,128)(2,1)}), bf16[16,128,1024]{2,1,0:T(8,128)(2,1)}, u32[]{:S(2)}, u32[]{:S(2)}) async-start(bf16[16,128,1024]{2,1,0:T(8,128)(2,1)} %bitcast.35), calls=%async_computation.1 | async-start | bytes 8388608 | tf_op jit(solution)/shard_map/all_to_all | solution.py:42
  168.1 76.6 %slice-start = ((s8[8388608]{0:T(1024)(128)(4,1)}), s8[4194304]{0:T(1024)(128)(4,1)S(1)}, s32[]{:S(2)}) async-start(s8[8388608]{0:T(1024)(128)(4,1)} %bitcast.38), calls=%async_computation.4 | async-start | bytes 8388608
  241.4 3.3 %slice-start.1 = ((s8[8388608]{0:T(1024)(128)(4,1)}), s8[4194304]{0:T(1024)(128)(4,1)S(1)}, s32[]{:S(2)}) async-start(s8[8388608]{0:T(1024)(128)(4,1)} %bitcast.38), calls=%async_computation.5 | async-start | bytes 8388608
Sparse Core Ops, SparseCore 0:
  9.1 52.0 all-gather.1
where the time goes:
time: 269 us; the launch traced here: 267 us
  blocking collectives  107 us (40%)
  waiting for transfers between devices  86.2 us (32%)
  matrix products  38.7 us (14%)
  starting transfers between devices  15.7 us (6%)
  between operations  14.2 us (5%)
    all_to_all x1, blocking collectives, per_device(): lax.all_to_all(delta.reshape(first, items, column_width), 'adapter', spli...  73.3 us
    all_to_all x1, waiting for transfers between devices, per_device(): lax.all_to_all(send_rows, 'adapter', split_axis=0, concat_axis=0, tiled=T...  54.8 us
    all_gather x1, waiting for transfers between devices, per_device(): lax.all_gather(tokens, 'tensor', axis=0, tiled=True)  30.6 us
    psum x1, blocking collectives, per_device(): low = lax.psum(partial_low, 'tensor')  24.7 us
    dot_general x1, matrix products, per_device(): jnp.dot(gathered, joined_weight_matrix, preferred_element_type=jnp.float32)  15.5 us
    unnamed x1, blocking collectives  9.48 us
    all_to_all x1, starting transfers between devices, per_device(): lax.all_to_all(send_local, 'adapter', split_axis=0, concat_axis=0, tiled=...  8.32 us
    dot_general x1, matrix products, per_device(): jnp.einsum('sd,kd->sk', rows, flattened_down, preferred_element_type=jnp....  7.91 us
  transfers between devices with their start and end apart: 3, of which 2 were waited for; matrix products, arithmetic and copies ran while one was open for 4% of the time, Pallas kernels for 0%

commit v1 on v0

v1 whole, which is shorter than its diff:
```python
import functools

import jax
import jax.numpy as jnp
from jax import lax
from jax.experimental import pallas as pl
from jax.experimental.pallas import tpu as pltpu
from jax.sharding import PartitionSpec as P

BF16, F32, I32 = jnp.bfloat16, jnp.float32, jnp.int32
LANES = 128
VMEM = pl.BlockSpec(memory_space=pltpu.VMEM)
LIMIT = 48 * 1024 * 1024


def iota(shape, dim):
    return lax.broadcasted_iota(I32, shape, dim)


def rows_by_rows(a, b):
    return lax.dot_general(a, b, (((1,), (1,)), ((), ())), preferred_element_type=F32)


def columns_by_columns(a, b):
    return lax.dot_general(a, b, (((0,), (0,)), ((), ())), preferred_element_type=F32)


def lane_as_row(extra, lane):
    pick = (iota((8, LANES), 1) == lane).astype(BF16)
    return rows_by_rows(pick, extra).astype(I32)


def route_kernel(owners, even, rest, slab_ref, main_ref, rest_ref, info_ref, rows_ref):
    members, local_rows, wide = slab_ref.shape
    group = members * local_rows
    for i in range(members):
        rows_ref[pl.ds(i * local_rows, local_rows), :] = slab_ref[i]
    extra = rows_ref[:, wide - LANES :]
    owner = lane_as_row(extra, 0)
    local = lane_as_row(extra, 1)
    hot = iota((owners, group), 0) == owner[0:1]
    hot16 = hot.astype(BF16)
    earlier = (iota((group, group), 0) < iota((group, group), 1)).astype(BF16)
    before = jnp.dot(hot16, earlier, preferred_element_type=F32)
    place = jnp.sum(jnp.where(hot, before, 0.0), axis=0, keepdims=True).astype(I32)
    counts = jnp.sum(jnp.where(hot, 1, 0), axis=1, keepdims=True)
    most = jnp.max(counts, axis=0, keepdims=True)
    number = iota((owners, 1), 0)
    full = jnp.min(jnp.where(counts == most, number, owners), axis=0, keepdims=True)
    others = jnp.max(jnp.where(number == full, 0, counts), axis=0, keepdims=True)

    target = jnp.where(place < even, owner[0:1] * even + place, -1)
    send = jnp.dot(
        (iota((owners * even, group), 0) == target).astype(BF16),
        rows_ref[...],
        preferred_element_type=F32,
    )
    tail = send[:, wide - LANES :]
    lane = iota(tail.shape, 1)
    tail = jnp.where(lane == 2, full.astype(F32), tail)
    tail = jnp.where(lane == 3, others.astype(F32), tail)
    tail = jnp.where(lane == 4, most.astype(F32), tail)
    main_ref[:, : wide - LANES] = send[:, : wide - LANES].astype(BF16)
    main_ref[:, wide - LANES :] = tail.astype(BF16)

    spare = jnp.where((owner[0:1] == full) & (place >= even), place - even, -1)
    rest_ref[...] = jnp.dot(
        (iota((rest, group), 0) == spare).astype(BF16), rows_ref[...], preferred_element_type=F32
    ).astype(BF16)
    line = iota((8, group), 0)
    info_ref[...] = jnp.where(line == 0, owner, jnp.where(line == 1, local, place))


def route(slab, owners, even, rest):
    members, local_rows, wide = slab.shape
    group = members * local_rows
    return pl.pallas_call(
        functools.partial(route_kernel, owners, even, rest),
        out_shape=(
            jax.ShapeDtypeStruct((owners * even, wide), BF16),
            jax.ShapeDtypeStruct((rest, wide), BF16),
            jax.ShapeDtypeStruct((8, group), I32),
        ),
        in_specs=[VMEM],
        out_specs=(VMEM, VMEM, VMEM),
        scratch_shapes=[pltpu.VMEM((group, wide), BF16)],
        compiler_params=pltpu.CompilerParams(vmem_limit_bytes=LIMIT),
        name="route",
    )(slab)


def low_kernel(rank, rows_ref, down_ref, low_ref, local_ref):
    features = down_ref.shape[1]
    held = down_ref.shape[0] // rank
    wide = rows_by_rows(down_ref[...], rows_ref[:, :features])
    local = lane_as_row(rows_ref[:, features:], 1)
    local_ref[...] = local
    total = jnp.zeros(low_ref.shape, F32)
    for i in range(held):
        total += jnp.where(local[0:1] == i, wide[i * rank : (i + 1) * rank], 0.0)
    low_ref[...] = total


def low_part(rows, down, rank, tile):
    count, wide = rows.shape
    return pl.pallas_call(
        functools.partial(low_kernel, rank),
        grid=(count // tile,),
        in_specs=[
            pl.BlockSpec((tile, wide), lambda i: (i, 0)),
            pl.BlockSpec(down.shape, lambda i: (0, 0)),
        ],
        out_specs=(
            pl.BlockSpec((rank, tile), lambda i: (0, i)),
            pl.BlockSpec((8, tile), lambda i: (0, i)),
        ),
        out_shape=(
            jax.ShapeDtypeStruct((rank, count), F32),
            jax.ShapeDtypeStruct((8, count), I32),
        ),
        compiler_params=pltpu.CompilerParams(vmem_limit_bytes=LIMIT),
        cost_estimate=pl.CostEstimate(
            flops=2 * count * down.shape[0] * down.shape[1],
            bytes_accessed=2 * (rows.size + down.size),
            transcendentals=0,
        ),
        name="low",
    )(rows, down)


def spread(low, local, held):
    none = jnp.zeros_like(low)
    return jnp.concatenate([jnp.where(local == i, low, none) for i in range(held)], axis=0)


def delta_kernel(low_ref, local_ref, up_ref, out_ref):
    held = up_ref.shape[0] // low_ref.shape[0]
    chosen = spread(low_ref[...], local_ref[0:1], held)
    out_ref[...] = (2.0 * columns_by_columns(chosen, up_ref[...])).astype(BF16)


def delta_of(low, local, up):
    count, columns = low.shape[1], up.shape[1]
    return pl.pallas_call(
        delta_kernel,
        out_shape=jax.ShapeDtypeStruct((count, columns), BF16),
        in_specs=[VMEM] * 3,
        out_specs=VMEM,
        compiler_params=pltpu.CompilerParams(vmem_limit_bytes=LIMIT),
        cost_estimate=pl.CostEstimate(
            flops=2 * count * up.size, bytes_accessed=2 * (up.size + count * columns), transcendentals=0
        ),
        name="delta",
    )(low, local, up)


def finish_kernel(even, full_ref, info_ref, low_ref, base_ref, back_ref, up_ref, out_ref):
    slots = back_ref.shape[0]
    rank, spare_slots = low_ref.shape
    held = up_ref.shape[0] // rank
    group = info_ref.shape[1]
    owner, local, place = info_ref[0:1], info_ref[1:2], info_ref[2:3]
    target = jnp.where(place < even, owner * even + place, -1)
    chosen = (iota((slots, group), 0) == target).astype(BF16)
    spare = jnp.where((owner == full_ref[0]) & (place >= even), place - even, -1)
    chosen_spare = (iota((spare_slots, group), 0) == spare).astype(BF16)
    local_rows = jnp.broadcast_to(local, (8, group)).astype(F32).astype(BF16)
    local_spare = rows_by_rows(local_rows, chosen_spare).astype(I32)
    wide = spread(low_ref[...], local_spare[0:1], held)
    delta = (2.0 * columns_by_columns(wide, up_ref[...])).astype(BF16)
    total = base_ref[...] + columns_by_columns(chosen, back_ref[...])
    out_ref[...] = (total + columns_by_columns(chosen_spare, delta)).astype(BF16)


def finish(full, info, low, base, back, up, even, tile):
    group, columns = base.shape
    whole = lambda a: pl.BlockSpec(a.shape, lambda i: (0, 0))
    cut = lambda a: pl.BlockSpec((a.shape[0], tile), lambda i: (0, i))
    return pl.pallas_call(
        functools.partial(finish_kernel, even),
        grid=(columns // tile,),
        in_specs=[
            pl.BlockSpec(memory_space=pltpu.SMEM),
            whole(info),
            whole(low),
            cut(base),
            cut(back),
            cut(up),
        ],
        out_specs=pl.BlockSpec((group, tile), lambda i: (0, i)),
        out_shape=jax.ShapeDtypeStruct((group, columns), BF16),
        compiler_params=pltpu.CompilerParams(vmem_limit_bytes=LIMIT),
        name="finish",
    )(full, info, low, base, back, up)


def exchange(block, axis):
    return lax.all_to_all(block, axis, split_axis=0, concat_axis=0, tiled=True)


def shifted(block, step):
    members = lax.axis_size("tensor")
    return lax.ppermute(block, "tensor", [(i, (i + step) % members) for i in range(members)])


def swapped(block, bit):
    members = lax.axis_size("tensor")
    return lax.ppermute(block, "tensor", [(i, i ^ bit) for i in range(members)])


def total_over_tensor(part):
    for bit in (1, 2, 4):
        part = part + swapped(part, bit)
    return part


def gather_rows(own):
    rows = own.shape[0]
    half = rows // 2
    before = shifted(own, 2)
    after = shifted(own, -2)
    across = jnp.concatenate([shifted(before[:half], 2), shifted(after[half:], -2)], axis=0)
    here = lax.axis_index("tensor")
    chip, core = here // 2, here % 2
    full = jnp.zeros((8 * rows, own.shape[1]), own.dtype)
    for away, block in ((0, own), (3, before), (1, after), (2, across)):
        other = swapped(block, 1)
        start = ((chip + away) % 4) * 2 * rows
        full = lax.dynamic_update_slice(full, block, (start + core * rows, 0))
        full = lax.dynamic_update_slice(full, other, (start + (1 - core) * rows, 0))
    return full


def per_device(
    tokens, token_adapter_index, joined_weight_matrix, adapter_down_weight, adapter_up_weight
):
    owners = lax.axis_size("adapter")
    members = lax.axis_size("tensor")
    local_rows, width = tokens.shape
    group = members * local_rows
    held, rank, features = adapter_down_weight.shape
    columns = adapter_up_weight.shape[2]
    capacity = 4 * group // owners
    even = group // owners
    rest = capacity - even
    down = adapter_down_weight.reshape(held * rank, features)
    up = adapter_up_weight.reshape(held * rank, columns)
    wide = features + LANES

    numbers = jnp.stack([token_adapter_index // held, token_adapter_index % held], axis=1)
    numbers = jnp.pad(numbers.astype(BF16), ((0, 0), (0, LANES - 2)))
    blocks = tokens.reshape(local_rows, members, features).transpose(1, 0, 2)
    numbers = jnp.broadcast_to(numbers[None], (members, local_rows, LANES))
    slab = exchange(jnp.concatenate([blocks, numbers], axis=2), "tensor")

    send, send_rest, info = route(slab, owners, even, rest)
    rest_rows = lax.all_gather(send_rest, "adapter", axis=0, tiled=True)
    rows = exchange(send.reshape(owners, even, wide), "adapter")

    said = rows[:, 0, features + 2 : features + 5].astype(I32)
    same = jnp.all(said[:, 0] == said[0, 0])
    full = jnp.where(same, said[0, 0], -1)
    largest = jnp.where(same, jnp.max(said[:, 1]), jnp.max(said[:, 2]))
    turns = (largest + even - 1) // even

    pieces = exchange(up.reshape(owners, up.shape[0] // owners, columns), "adapter")
    piece = lax.dynamic_index_in_dim(pieces, jnp.maximum(full, 0), 0, keepdims=False)
    up_full = lax.all_gather(piece, "adapter", axis=0, tiled=True)

    part, local = low_part(rows.reshape(owners * even, wide), down, rank, owners * even)
    low = total_over_tensor(part).astype(BF16)
    delta = delta_of(low, local, up)
    back = exchange(delta.reshape(owners, even, columns), "adapter").reshape(owners * even, columns)

    rest_part, _ = low_part(rest_rows, down, rank, owners * rest // 3)
    rest_low = total_over_tensor(rest_part).astype(BF16).reshape(rank, owners, rest)
    rest_low = jnp.pad(rest_low.transpose(1, 0, 2), ((0, 0), (0, 0), (0, capacity - rest)))
    low_back = exchange(rest_low, "adapter")
    low_full = lax.dynamic_index_in_dim(low_back, jnp.maximum(full, 0), 0, keepdims=False)

    ready, _ = lax.optimization_barrier((tokens, send))
    base = jnp.dot(gather_rows(ready), joined_weight_matrix, preferred_element_type=F32)

    owner, place = info[0], info[2]
    flat = slab.reshape(group, wide)

    def more(carry):
        turn, total = carry
        wanted = (owner != full) & (place // even == turn)
        slot = jnp.where(wanted, owner * even + place % even, -1)
        chosen = (slot[None, :] == jnp.arange(owners * even, dtype=I32)[:, None]).astype(BF16)
        moved = jnp.dot(chosen, flat, preferred_element_type=F32).astype(BF16)
        moved = exchange(moved.reshape(owners, even, wide), "adapter").reshape(owners * even, wide)
        more_part, more_local = low_part(moved, down, rank, owners * even)
        more_low = total_over_tensor(more_part).astype(BF16)
        more_delta = delta_of(more_low, more_local, up).reshape(owners, even, columns)
        more_back = exchange(more_delta, "adapter").reshape(owners * even, columns)
        return turn + 1, total + jnp.dot(chosen.T, more_back, preferred_element_type=F32)

    _, base = lax.while_loop(lambda carry: carry[0] < turns, more, (jnp.int32(1), base))
    return finish(full.reshape(1), info, low_full, base, back, up_full, even, 256)


def solution(mesh):
    return jax.shard_map(
        per_device,
        mesh=mesh,
        in_specs=(
            P(("adapter", "tensor"), None),
            P(("adapter", "tensor")),
            P(None, "tensor"),
            P("adapter", None, "tensor"),
            P("adapter", None, "tensor"),
        ),
        out_specs=P("adapter", "tensor"),
        check_vma=False,
    )
```

time: 269 us -> 206 us (0.77)
  blocking collectives: 107 us -> 22 us
  waiting for transfers between devices: 86.2 us -> 49.8 us
  local copies, waits for them, and re-layouts: 2.38 us -> 30.8 us
  starting transfers between devices: 15.7 us -> 40.4 us
  Pallas kernels: 0 us -> 24.4 us
  matrix products: 38.7 us -> 18 us
  between operations: 14.2 us -> 16.9 us
    all_to_all x1, blocking collectives: 73.3 us -> 22 us  [exchange(): return lax.all_to_all(block, axis, split_axis=0, concat_axis=0, tiled=True)]
    all_gather x1 -> x2, waiting for transfers between devices: 30.6 us -> 0.02 us  [the longest x1 0.02 us: per_device(): up_full = lax.all_gather(piece, 'adapter', axis=0, tiled=True)]
    all_to_all x2 -> x4, waiting for transfers between devices: 54.8 us -> 29.2 us  [exchange(): return lax.all_to_all(block, axis, split_axis=0, concat_axis=0, tiled=True)]
    psum x1 -> x0, blocking collectives: 24.7 us -> none  [per_device(): low = lax.psum(partial_low, 'tensor')]
    pallas_call x0 -> x5, Pallas kernels: none -> 24.4 us  [the longest x2 10.1 us: low_part(): pl.pallas_call(functools.partial(low_kernel, rank), grid=(count // tile,)...]
    dot_general x5 -> x1, matrix products: 38.7 us -> 18 us  [per_device(): jnp.dot(gather_rows(ready), joined_weight_matrix, preferred_element_type=...]
    ppermute x0 -> x14, waiting for transfers between devices: none -> 20.6 us  [the longest x10 10.6 us: swapped(): return lax.ppermute(block, 'tensor', [(i, i ^ bit) for i in range(members)])]
    all_to_all x2 -> x4, starting transfers between devices: 15.7 us -> 30.8 us  [exchange(): return lax.all_to_all(block, axis, split_axis=0, concat_axis=0, tiled=True)]
  transfers between devices with their start and end apart: 3 -> 20, of which waited for: 2 -> 7; matrix products, arithmetic and copies ran while one was open for 4% -> 22% of each run, Pallas kernels for 0% -> 7%
where the time goes in v1:
time: 206 us; the launch traced here: 205 us
  waiting for transfers between devices  49.8 us (24%)
  starting transfers between devices  40.4 us (20%)
  local copies, waits for them, and re-layouts  30.8 us (15%)
  Pallas kernels  24.4 us (12%)
  blocking collectives  22 us (11%)
  matrix products  18 us (9%)
  between operations  16.9 us (8%)
  other arithmetic  2.85 us (1%)
    all_to_all x4, starting transfers between devices, exchange(): return lax.all_to_all(block, axis, split_axis=0, concat_axis=0, tiled=True)  30.8 us
    all_to_all x4, waiting for transfers between devices, exchange(): return lax.all_to_all(block, axis, split_axis=0, concat_axis=0, tiled=True)  29.2 us
    all_to_all x1, blocking collectives, exchange(): return lax.all_to_all(block, axis, split_axis=0, concat_axis=0, tiled=True)  22 us
    dot_general x1, matrix products, per_device(): jnp.dot(gather_rows(ready), joined_weight_matrix, preferred_element_type=...  18 us
    ppermute x10, waiting for transfers between devices, swapped(): return lax.ppermute(block, 'tensor', [(i, i ^ bit) for i in range(members)])  10.6 us
    pallas_call x2, Pallas kernels, low_part(): pl.pallas_call(functools.partial(low_kernel, rank), grid=(count // tile,)...  10.1 us
    ppermute x4, waiting for transfers between devices, shifted(): lax.ppermute(block, 'tensor', [(i, (i + step) % members) for i in range(m...  9.94 us
    dynamic_update_slice x4, local copies, waits for them, and re-layouts, gather_rows(): full = lax.dynamic_update_slice(full, other, (start + (1 - core) * rows, 0))  7.99 us
  transfers between devices with their start and end apart: 20, of which 7 were waited for; matrix products, arithmetic and copies ran while one was open for 22% of the time, Pallas kernels for 7%

profile of v1, /device:TPU:2, one launch (start us, length us, event | category | flops | bytes accessed | tf_op | source)
XLA Modules:
  0.0 205.1 jit_solution(1550501262231772685)
XLA Ops:
  6.5 0.7 convert_bitcast_fusion
  7.2 0.1 copy.25
  7.3 1.3 copy.30
  8.7 0.0 copy-start.2
  8.7 0.1 pad_maximum_fusion
  8.8 22.0 %all_to_all.47.slab_ref = bf16[8,64,1152]{2,1,0:T(8,128)(2,1)} all-to-all(bf16[8,64,1152]{2,1,0:T(8,128)(2,1)S(1)} %pad_maximum_fusion), channel_id=1, replica_groups=mesh['adapter'=16,'tensor'=8] {'tensor'}, dimensions={0} | all-to-all | bytes 2359296 | tf_op jit(solution)/shard_map/all_to_all | solution.py:198
  30.8 3.7 %route.1 = (bf16[512,1152]{1,0:T(8,128)(2,1)}, bf16[96,1152]{1,0:T(8,128)(2,1)}, s32[8,512]{1,0:T(8,128)S(1)}) custom-call(bf16[8,64,1152]{2,1,0:T(8,128)(2,1)} %all_to_all.47.slab_ref), custom_call_target="tpu_custom_call" | custom-call | tf_op jit(solution)/shard_map/route/pallas_call | solution.py:77
  34.5 0.0 all-gather.4.cloned.1.call-update
  34.7 0.1 collective-permute-start.6
  34.8 0.6 collective-permute-start.7
  35.4 2.7 %collective-permute-start.9 = (bf16[64,8192]{1,0:T(8,128)(2,1)S(1)}, bf16[64,8192]{1,0:T(8,128)(2,1)S(1)}, u32[]{:S(2)}, u32[]{:S(2)}) collective-permute-start(bf16[64,8192]{1,0:T(8,128)(2,1)S(1)} %copy-done.2), channel_id=1, source_target_pairs={{0,6},{1,7},{2,0},{3,1},{4,2},{5,3},{6,4},{7,5},{8,14},{9,15},{10,... | collective-permute-start | bytes 3145736 | tf_op jit(solution)/shard_map/ppermute | solution.py:203
  38.1 8.3 %all-to-all-start.3 = ((bf16[16,32,1152]{2,1,0:T(8,128)(2,1)}), bf16[16,32,1152]{2,1,0:T(8,128)(2,1)S(1)}, u32[]{:S(2)}, u32[]{:S(2)}) async-start(bf16[16,32,1152]{2,1,0:T(8,128)(2,1)} %bitcast.8), calls=%async_computation.3 | async-start | bytes 2359296 | tf_op jit(solution)/shard_map/all_to_all | solution.py:198
  46.4 4.3 %broadcast_in_dim.7 = bf16[512,8192]{1,0:T(8,128)(2,1)} broadcast(bf16[]{:T(256)} %constant.176.clone.1), dimensions={} | broadcast | bytes 8388610 | tf_op jit(solution)/shard_map/broadcast_in_dim | solution.py:225
  50.7 1.0 constant_dynamic-update-slice_fusion.9
  51.7 9.9 %collective-permute-done.7 = bf16[64,8192]{1,0:T(8,128)(2,1)} collective-permute-done((bf16[64,8192]{1,0:T(8,128)(2,1)S(1)}, bf16[64,8192]{1,0:T(8,128)(2,1)}, u32[]{:S(2)}, u32[]{:S(2)}) %collective-permute-start.7) | collective-permute-done | bytes 1048608 | tf_op jit(solution)/shard_map/ppermute | solution.py:203
  61.6 1.9 slice.38
  63.5 0.8 slice.39
  64.4 3.2 %collective-permute-start.12 = (bf16[32,8192]{1,0:T(8,128)(2,1)}, bf16[32,8192]{1,0:T(8,128)(2,1)}, u32[]{:S(2)}, u32[]{:S(2)}) collective-permute-start(bf16[32,8192]{1,0:T(8,128)(2,1)} %slice.39), channel_id=1, source_target_pairs={{0,6},{1,7},{2,0},{3,1},{4,2},{5,3},{6,4},{7,5},{8,14},{9,15},{10,... | collective-permute-start | bytes 1572872 | tf_op jit(solution)/shard_map/ppermute | solution.py:203
  67.6 0.0 collective-permute-start.8
  67.6 0.0 all-to-all-done.3
  67.6 8.3 %all-to-all-start.6 = ((bf16[16,64,1280]{2,1,0:T(8,128)(2,1)}), bf16[16,64,1280]{2,1,0:T(8,128)(2,1)}, u32[]{:S(2)}, u32[]{:S(2)}) async-start(bf16[16,64,1280]{2,1,0:T(8,128)(2,1)} %bitcast.63), calls=%async_computation.6 | async-start | bytes 5242880 | tf_op jit(solution)/shard_map/all_to_all | solution.py:198
  75.9 0.0 all-gather.6.cloned.1.call-start
  76.0 2.3 %constant_dynamic-update-slice_fusion.8 = bf16[512,8192]{1,0:T(8,128)(2,1)} fusion(bf16[512,8192]{1,0:T(8,128)(2,1)} %constant_dynamic-update-slice_fusion.9, bf16[64,8192]{1,0:T(8,128)(2,1)} %collective-permute-done.6, s32[]{:T(128)S(6)} %select_n.128), kind=kLoop, calls=%fused_computation.32 | loop fusion | bytes 2097156 | tf_op jit(solution)/shard_map/dynamic_update_slice | solution.py:230
  78.2 3.1 %low.9 = (f32[16,512]{1,0:T(8,128)S(1)}, s32[8,512]{1,0:T(8,128)S(1)}) custom-call(bf16[512,1152]{1,0:T(8,128)(2,1)S(1)} %bitcast.58, bf16[1024,1024]{1,0:T(8,128)(2,1)} %bitcast.11.down_ref), custom_call_target="tpu_custom_call" | custom-call | flops 1073741824 | bytes 3276800 | tf_op jit(solution)/shard_map/low/pallas_call | solution.py:106
  81.4 0.1 collective-permute-start.14
  81.5 2.3 %constant_dynamic-update-slice_fusion.7 = bf16[512,8192]{1,0:T(8,128)(2,1)} fusion(bf16[512,8192]{1,0:T(8,128)(2,1)} %constant_dynamic-update-slice_fusion.8, bf16[64,8192]{1,0:T(8,128)(2,1)} %collective-permute-done.7, s32[]{:T(128)S(6)} %select_n.130), kind=kLoop, calls=%fused_computation.31 | loop fusion | bytes 2097156 | tf_op jit(solution)/shard_map/dynamic_update_slice | solution.py:229
  83.7 0.1 slice.37
  83.8 0.1 copy.24
  84.0 0.1 collective-permute-start.15
  84.1 0.6 slice_reduce_fusion
  84.7 0.5 slice.30
  85.2 2.7 %collective-permute-done.15 = f32[16,512]{1,0:T(8,128)S(1)} collective-permute-done((f32[16,512]{1,0:T(8,128)S(1)}, f32[16,512]{1,0:T(8,128)S(1)}, u32[]{:S(2)}, u32[]{:S(2)}) %collective-permute-start.15) | collective-permute-done | bytes 32800 | tf_op jit(solution)/shard_map/ppermute | solution.py:208
  88.0 0.0 collective-permute-start.16
  88.0 1.3 compare_reduce_fusion.1
  92.4 0.1 collective-permute-start.10
  92.5 0.9 collective-permute-done.16
  93.4 4.4 %delta.7 = bf16[512,1280]{1,0:T(8,128)(2,1)} custom-call(bf16[16,512]{1,0:T(8,128)(2,1)S(1)} %add_convert_fusion.2.low_ref, s32[8,512]{1,0:T(8,128)S(1)} %get-tuple-element.234.local_ref, bf16[1024,1280]{1,0:T(8,128)(2,1)} %bitcast.64), custom_call_target="tpu_custom_call" | custom-call | flops 1342177280 | bytes 3932160 | tf_op jit(solution)/shard_map/delta/pallas_call | solution.py:144
  97.8 25.0 %all-to-all-done.6 = bf16[16,64,1280]{2,1,0:T(8,128)(2,1)} async-done(((bf16[16,64,1280]{2,1,0:T(8,128)(2,1)}), bf16[16,64,1280]{2,1,0:T(8,128)(2,1)}, u32[]{:S(2)}, u32[]{:S(2)}) %all-to-all-start.6) | async-done | bytes 2621472 | tf_op jit(solution)/shard_map/all_to_all | solution.py:198
  122.7 1.6 constant_dynamic-slice_fusion
  124.3 0.0 all-gather.6.cloned.1.call-update
  124.4 1.1 constant_dynamic-update-slice_fusion.1
  125.5 1.1 constant_dynamic-update-slice_fusion
  126.5 0.1 collective-permute-start.13
  126.6 2.4 %constant_dynamic-update-slice_fusion.6 = bf16[512,8192]{1,0:T(8,128)(2,1)} fusion(bf16[512,8192]{1,0:T(8,128)(2,1)} %constant_dynamic-update-slice_fusion.7, bf16[64,8192]{1,0:T(8,128)(2,1)} %collective-permute-done.8, s32[]{:T(128)S(6)} %select_n.131), kind=kLoop, calls=%fused_computation.30 | loop fusion | bytes 2097156 | tf_op jit(solution)/shard_map/dynamic_update_slice | solution.py:230
  129.0 2.0 copy-done.1
  131.0 6.9 %low.8 = (f32[16,1536]{1,0:T(8,128)S(1)}, s32[8,1536]{1,0:T(8,128)}) custom-call(bf16[1536,1152]{1,0:T(8,128)(2,1)S(1)} %copy-done.1, bf16[1024,1024]{1,0:T(8,128)(2,1)} %bitcast.11.down_ref), custom_call_target="tpu_custom_call" | custom-call | flops 3221225472 | bytes 5636096 | tf_op jit(solution)/shard_map/low/pallas_call | solution.py:106
  137.9 0.4 collective-permute-start.3
  138.3 1.1 constant_dynamic-update-slice_fusion.5
  139.4 0.6 collective-permute-start.4
  140.0 1.0 constant_dynamic-update-slice_fusion.4
  141.0 3.3 %collective-permute-done.4 = f32[16,1536]{1,0:T(8,128)S(1)} collective-permute-done((f32[16,1536]{1,0:T(8,128)S(1)}, f32[16,1536]{1,0:T(8,128)S(1)}, u32[]{:S(2)}, u32[]{:S(2)}) %collective-permute-start.4) | collective-permute-done | bytes 98336 | tf_op jit(solution)/shard_map/ppermute | solution.py:208
  144.4 1.6 collective-permute-start.5
  146.0 1.1 constant_dynamic-update-slice_fusion.3
  147.1 3.6 %collective-permute-done.5 = f32[16,1536]{1,0:T(8,128)S(1)} collective-permute-done((f32[16,1536]{1,0:T(8,128)S(1)}, f32[16,1536]{1,0:T(8,128)S(1)}, u32[]{:S(2)}, u32[]{:S(2)}) %collective-permute-start.5) | collective-permute-done | bytes 98336 | tf_op jit(solution)/shard_map/ppermute | solution.py:208
  150.8 0.1 reshape.118
  151.0 0.6 pad.9
  151.6 9.0 %all-to-all-start.4 = ((bf16[16,16,128]{2,1,0:T(8,128)(2,1)}), bf16[16,16,128]{2,1,0:T(8,128)(2,1)S(1)}, u32[]{:S(2)}, u32[]{:S(2)}) async-start(bf16[16,16,128]{2,1,0:T(8,128)(2,1)} %pad.9), calls=%async_computation.4 | async-start | bytes 131072 | tf_op jit(solution)/shard_map/all_to_all | solution.py:198
  160.6 2.3 %constant_dynamic-update-slice_fusion.2 = bf16[512,8192]{1,0:T(8,128)(2,1)} fusion(bf16[512,8192]{1,0:T(8,128)(2,1)} %constant_dynamic-update-slice_fusion.3, bf16[64,8192]{1,0:T(8,128)(2,1)} %collective-permute-done.13, s32[]{:T(128)S(6)} %select_n.137), kind=kLoop, calls=%fused_computation.26 | loop fusion | bytes 2097156 | tf_op jit(solution)/shard_map/dynamic_update_slice | solution.py:230
  162.8 4.3 %all-to-all-done.4 = bf16[16,16,128]{2,1,0:T(8,128)(2,1)S(1)} async-done(((bf16[16,16,128]{2,1,0:T(8,128)(2,1)}), bf16[16,16,128]{2,1,0:T(8,128)(2,1)S(1)}, u32[]{:S(2)}, u32[]{:S(2)}) %all-to-all-start.4) | async-done | bytes 65568 | tf_op jit(solution)/shard_map/all_to_all | solution.py:198
  167.1 5.2 %all-to-all-start.5 = ((bf16[16,32,1280]{2,1,0:T(8,128)(2,1)}), bf16[16,32,1280]{2,1,0:T(8,128)(2,1)S(1)}, u32[]{:S(2)}, u32[]{:S(2)}) async-start(bf16[16,32,1280]{2,1,0:T(8,128)(2,1)} %bitcast.19), calls=%async_computation.5 | async-start | bytes 2621440 | tf_op jit(solution)/shard_map/all_to_all | solution.py:198
  172.3 18.0 %fusion.8 = f32[512,1280]{1,0:T(8,128)} fusion(bf16[512,8192]{1,0:T(8,128)(2,1)} %constant_dynamic-update-slice_fusion.2, bf16[8192,1280]{1,0:T(8,128)(2,1)} %param.9), kind=kOutput, calls=%fused_computation.49 | convolution fusion | flops 10737418240 | bytes 31981568 | tf_op jit(solution)/shard_map/dot_general | solution.py:282
  190.3 0.0 all-gather.6.cloned.1.call-done
  190.3 1.7 copy-done
  192.1 6.2 %finish.1 = bf16[512,1280]{1,0:T(8,128)(2,1)} custom-call(s32[1]{0:T(128)} %bitcast.10.full_ref, s32[8,512]{1,0:T(8,128)S(1)} %get-tuple-element.228.info_ref, bf16[16,128]{1,0:T(8,128)(2,1)S(1)} %dynamic-slice_bitcast_fusion.low_ref, f32[512,1280]{1,0:T(8,128)} %get-tuple-element.232.base_ref, bf16[512,1280]{1,0:T(8,128)(2,1)S(1)} %bitcast.56, ...), custom_call_target="tpu_custom_call" | custom-call | tf_op jit(solution)/shard_map/finish/pallas_call | solution.py:179
  (32 shorter events, 0.2 us)
Async XLA Ops:
  6.5 122.5 %all-gather.4.cloned.1.call-start = ((), (), s32[]{:S(2)}) async-start(), calls=%async_computation.7 | async-start | bytes 3760128 | tf_op jit(solution)/shard_map/all_gather | solution.py:257
  8.7 26.0 %copy-start.2 = (bf16[64,8192]{1,0:T(8,128)(2,1)S(1)}, bf16[64,8192]{1,0:T(8,128)(2,1)}, u32[]{:S(2)}) copy-start(bf16[64,8192]{1,0:T(8,128)(2,1)} %param.7) | copy-start | bytes 3145732
  34.7 41.3 %collective-permute-start.6 = (bf16[64,8192]{1,0:T(8,128)(2,1)S(1)}, bf16[64,8192]{1,0:T(8,128)(2,1)}, u32[]{:S(2)}, u32[]{:S(2)}) collective-permute-start(bf16[64,8192]{1,0:T(8,128)(2,1)S(1)} %copy-done.2), channel_id=1, source_target_pairs={{0,1},{1,0},{2,3},{3,2},{4,5},{5,4},{6,7},{7,6},{8,9},{9,8},{10,11... | collective-permute-start | bytes 3145736 | tf_op jit(solution)/shard_map/ppermute | solution.py:208
  34.8 26.9 %collective-permute-start.7 = (bf16[64,8192]{1,0:T(8,128)(2,1)S(1)}, bf16[64,8192]{1,0:T(8,128)(2,1)}, u32[]{:S(2)}, u32[]{:S(2)}) collective-permute-start(bf16[64,8192]{1,0:T(8,128)(2,1)S(1)} %copy-done.2), channel_id=1, source_target_pairs={{0,2},{1,3},{2,4},{3,5},{4,6},{5,7},{6,0},{7,1},{8,10},{9,11},{10,... | collective-permute-start | bytes 3145736 | tf_op jit(solution)/shard_map/ppermute | solution.py:203
  35.4 28.2 %collective-permute-start.9 = (bf16[64,8192]{1,0:T(8,128)(2,1)S(1)}, bf16[64,8192]{1,0:T(8,128)(2,1)S(1)}, u32[]{:S(2)}, u32[]{:S(2)}) collective-permute-start(bf16[64,8192]{1,0:T(8,128)(2,1)S(1)} %copy-done.2), channel_id=1, source_target_pairs={{0,6},{1,7},{2,0},{3,1},{4,2},{5,3},{6,4},{7,5},{8,14},{9,15},{10,... | collective-permute-start | bytes 3145736 | tf_op jit(solution)/shard_map/ppermute | solution.py:203
  38.1 29.6 %all-to-all-start.3 = ((bf16[16,32,1152]{2,1,0:T(8,128)(2,1)}), bf16[16,32,1152]{2,1,0:T(8,128)(2,1)S(1)}, u32[]{:S(2)}, u32[]{:S(2)}) async-start(bf16[16,32,1152]{2,1,0:T(8,128)(2,1)} %bitcast.8), calls=%async_computation.3 | async-start | bytes 2359296 | tf_op jit(solution)/shard_map/all_to_all | solution.py:198
  63.5 60.8 %collective-permute-start.11 = (bf16[32,8192]{1,0:T(8,128)(2,1)}, bf16[32,8192]{1,0:T(8,128)(2,1)}, u32[]{:S(2)}, u32[]{:S(2)}) collective-permute-start(bf16[32,8192]{1,0:T(8,128)(2,1)} %slice.38), channel_id=1, source_target_pairs={{0,2},{1,3},{2,4},{3,5},{4,6},{5,7},{6,0},{7,1},{8,10},{9,11},{10,... | collective-permute-start | bytes 1572872 | tf_op jit(solution)/shard_map/ppermute | solution.py:203
  64.4 61.1 %collective-permute-start.12 = (bf16[32,8192]{1,0:T(8,128)(2,1)}, bf16[32,8192]{1,0:T(8,128)(2,1)}, u32[]{:S(2)}, u32[]{:S(2)}) collective-permute-start(bf16[32,8192]{1,0:T(8,128)(2,1)} %slice.39), channel_id=1, source_target_pairs={{0,6},{1,7},{2,0},{3,1},{4,2},{5,3},{6,4},{7,5},{8,14},{9,15},{10,... | collective-permute-start | bytes 1572872 | tf_op jit(solution)/shard_map/ppermute | solution.py:203
  67.6 59.0 %collective-permute-start.8 = (bf16[64,8192]{1,0:T(8,128)(2,1)}, bf16[64,8192]{1,0:T(8,128)(2,1)}, u32[]{:S(2)}, u32[]{:S(2)}) collective-permute-start(bf16[64,8192]{1,0:T(8,128)(2,1)} %collective-permute-done.7), channel_id=1, source_target_pairs={{0,1},{1,0},{2,3},{3,2},{4,5},{5,4},{6,7},{7,6},{8,9},{9,8},{10,11... | collective-permute-start | bytes 3145736 | tf_op jit(solution)/shard_map/ppermute | solution.py:208
  67.6 55.1 %all-to-all-start.6 = ((bf16[16,64,1280]{2,1,0:T(8,128)(2,1)}), bf16[16,64,1280]{2,1,0:T(8,128)(2,1)}, u32[]{:S(2)}, u32[]{:S(2)}) async-start(bf16[16,64,1280]{2,1,0:T(8,128)(2,1)} %bitcast.63), calls=%async_computation.6 | async-start | bytes 5242880 | tf_op jit(solution)/shard_map/all_to_all | solution.py:198
  75.9 114.4 %all-gather.6.cloned.1.call-start = ((), (), s32[]{:S(2)}) async-start(), calls=%async_computation.8 | async-start | bytes 2785280 | tf_op jit(solution)/shard_map/all_gather | solution.py:268
  81.4 2.5 %collective-permute-start.14 = (f32[16,512]{1,0:T(8,128)S(1)}, f32[16,512]{1,0:T(8,128)S(1)}, u32[]{:S(2)}, u32[]{:S(2)}) collective-permute-start(f32[16,512]{1,0:T(8,128)S(1)} %get-tuple-element.233), channel_id=1, source_target_pairs={{0,1},{1,0},{2,3},{3,2},{4,5},{5,4},{6,7},{7,6},{8,9},{9,8},{10,11... | collective-permute-start | bytes 98312 | tf_op jit(solution)/shard_map/ppermute | solution.py:208
  84.0 4.0 %collective-permute-start.15 = (f32[16,512]{1,0:T(8,128)S(1)}, f32[16,512]{1,0:T(8,128)S(1)}, u32[]{:S(2)}, u32[]{:S(2)}) collective-permute-start(f32[16,512]{1,0:T(8,128)S(1)} %add.217), channel_id=1, source_target_pairs={{0,2},{1,3},{2,0},{3,1},{4,6},{5,7},{6,4},{7,5},{8,10},{9,11},{10,... | collective-permute-start | bytes 98312 | tf_op jit(solution)/shard_map/ppermute | solution.py:208
  88.0 5.4 %collective-permute-start.16 = (f32[16,512]{1,0:T(8,128)S(1)}, f32[16,512]{1,0:T(8,128)S(1)}, u32[]{:S(2)}, u32[]{:S(2)}) collective-permute-start(f32[16,512]{1,0:T(8,128)S(1)} %add.218), channel_id=1, source_target_pairs={{0,4},{1,5},{2,6},{3,7},{4,0},{5,1},{6,2},{7,3},{8,12},{9,13},{10,... | collective-permute-start | bytes 98312 | tf_op jit(solution)/shard_map/ppermute | solution.py:208
  92.4 47.6 %collective-permute-start.10 = (bf16[64,8192]{1,0:T(8,128)(2,1)S(1)}, bf16[64,8192]{1,0:T(8,128)(2,1)S(1)}, u32[]{:S(2)}, u32[]{:S(2)}) collective-permute-start(bf16[64,8192]{1,0:T(8,128)(2,1)S(1)} %collective-permute-done.9), channel_id=1, source_target_pairs={{0,1},{1,0},{2,3},{3,2},{4,5},{5,4},{6,7},{7,6},{8,9},{9,8},{10,11... | collective-permute-start | bytes 3145736 | tf_op jit(solution)/shard_map/ppermute | solution.py:208
  126.5 34.0 %collective-permute-start.13 = (bf16[64,8192]{1,0:T(8,128)(2,1)S(1)}, bf16[64,8192]{1,0:T(8,128)(2,1)}, u32[]{:S(2)}, u32[]{:S(2)}) collective-permute-start(bf16[64,8192]{1,0:T(8,128)(2,1)S(1)} %constant_dynamic-update-slice_fusion), channel_id=1, source_target_pairs={{0,1},{1,0},{2,3},{3,2},{4,5},{5,4},{6,7},{7,6},{8,9},{9,8},{10,11... | collective-permute-start | bytes 3145736 | tf_op jit(solution)/shard_map/ppermute | solution.py:208
  129.0 2.0 copy-start.1
  137.9 1.4 collective-permute-start.3
  139.4 5.0 %collective-permute-start.4 = (f32[16,1536]{1,0:T(8,128)S(1)}, f32[16,1536]{1,0:T(8,128)S(1)}, u32[]{:S(2)}, u32[]{:S(2)}) collective-permute-start(f32[16,1536]{1,0:T(8,128)S(1)} %add.190), channel_id=1, source_target_pairs={{0,2},{1,3},{2,0},{3,1},{4,6},{5,7},{6,4},{7,5},{8,10},{9,11},{10,... | collective-permute-start | bytes 294920 | tf_op jit(solution)/shard_map/ppermute | solution.py:208
  144.4 6.4 %collective-permute-start.5 = (f32[16,1536]{1,0:T(8,128)S(1)}, f32[16,1536]{1,0:T(8,128)S(1)}, u32[]{:S(2)}, u32[]{:S(2)}) collective-permute-start(f32[16,1536]{1,0:T(8,128)S(1)} %add.191), channel_id=1, source_target_pairs={{0,4},{1,5},{2,6},{3,7},{4,0},{5,1},{6,2},{7,3},{8,12},{9,13},{10,... | collective-permute-start | bytes 294920 | tf_op jit(solution)/shard_map/ppermute | solution.py:208
  151.6 15.5 %all-to-all-start.4 = ((bf16[16,16,128]{2,1,0:T(8,128)(2,1)}), bf16[16,16,128]{2,1,0:T(8,128)(2,1)S(1)}, u32[]{:S(2)}, u32[]{:S(2)}) async-start(bf16[16,16,128]{2,1,0:T(8,128)(2,1)} %pad.9), calls=%async_computation.4 | async-start | bytes 131072 | tf_op jit(solution)/shard_map/all_to_all | solution.py:198
  167.1 23.2 %all-to-all-start.5 = ((bf16[16,32,1280]{2,1,0:T(8,128)(2,1)}), bf16[16,32,1280]{2,1,0:T(8,128)(2,1)S(1)}, u32[]{:S(2)}, u32[]{:S(2)}) async-start(bf16[16,32,1280]{2,1,0:T(8,128)(2,1)} %bitcast.19), calls=%async_computation.5 | async-start | bytes 2621440 | tf_op jit(solution)/shard_map/all_to_all | solution.py:198
  190.3 1.7 copy-start
Sparse Core Ops, SparseCore 0:
  34.6 85.5 all-gather.3
  124.5 50.5 all-gather.5

commit v2 on v1

v2 whole, which is shorter than its diff:
```python
import functools

import jax
import jax.numpy as jnp
from jax import lax
from jax.experimental import pallas as pl
from jax.experimental.pallas import tpu as pltpu
from jax.sharding import PartitionSpec as P

BF16, F32, I32 = jnp.bfloat16, jnp.float32, jnp.int32
LANES = 128
VMEM = pl.BlockSpec(memory_space=pltpu.VMEM)
LIMIT = 60 * 1024 * 1024
SMALL = 24 * 1024 * 1024


def iota(shape, dim):
    return lax.broadcasted_iota(I32, shape, dim)


def rows_by_rows(a, b):
    return lax.dot_general(a, b, (((1,), (1,)), ((), ())), preferred_element_type=F32)


def columns_by_columns(a, b):
    return lax.dot_general(a, b, (((0,), (0,)), ((), ())), preferred_element_type=F32)


def lane_as_row(extra, lane):
    pick = (iota((8, LANES), 1) == lane).astype(BF16)
    return rows_by_rows(pick, extra).astype(I32)


def plan_kernel(owners, held, even, ids_ref, info_ref, down_ref):
    group = ids_ref.shape[1]
    ids = ids_ref[...]
    owner = ids // held
    hot = iota((owners, group), 0) == owner[0:1]
    earlier = (iota((group, group), 0) < iota((group, group), 1)).astype(BF16)
    before = jnp.dot(hot.astype(BF16), earlier, preferred_element_type=F32)
    place = jnp.sum(jnp.where(hot, before, 0.0), axis=0, keepdims=True).astype(I32)
    counts = jnp.sum(jnp.where(hot, 1, 0), axis=1, keepdims=True)
    most = jnp.max(counts, axis=0, keepdims=True)
    number = iota((owners, 1), 0)
    full = jnp.min(jnp.where(counts == most, number, owners), axis=0, keepdims=True)
    others = jnp.max(jnp.where(number == full, 0, counts), axis=0, keepdims=True)
    info = jnp.broadcast_to(most, (8, group))
    line = iota((8, group), 0)
    for i, value in enumerate((owner, ids - owner * held, place, full, others)):
        info = jnp.where(line == i, value, info)
    info_ref[...] = info
    tall = jnp.concatenate([info.astype(F32), jnp.zeros((LANES - 8, group), F32)], axis=0)
    down_ref[...] = tall.T.astype(I32)


def plan(ids, owners, held, even):
    return pl.pallas_call(
        functools.partial(plan_kernel, owners, held, even),
        out_shape=(
            jax.ShapeDtypeStruct((8, ids.shape[0]), I32),
            jax.ShapeDtypeStruct((ids.shape[0], LANES), I32),
        ),
        in_specs=[VMEM],
        out_specs=(VMEM, VMEM),
        compiler_params=pltpu.CompilerParams(vmem_limit_bytes=SMALL),
        name="plan",
    )(jnp.broadcast_to(ids[None], (8, ids.shape[0])))


def route_kernel(owners, even, at_ref, info_ref, rows_ref, main_ref, rest_ref):
    group, features = rows_ref.shape
    slots, spare_slots = main_ref.shape[0], rest_ref.shape[0]
    info = info_ref[...]
    owner, local, place, full = info[0:1], info[1:2], info[2:3], info[3:4]
    rows = rows_ref[...]
    numbers = jnp.where(iota((LANES, group), 0) == 1, local, 0).astype(F32).astype(BF16)

    target = jnp.where(place < even, owner * even + place, -1)
    chosen = (iota((slots, group), 0) == target).astype(BF16)
    main_ref[:, :features] = jnp.dot(chosen, rows, preferred_element_type=F32).astype(BF16)
    tail = rows_by_rows(chosen, numbers)
    lane = iota(tail.shape, 1)
    for i in (3, 4, 5):
        tail = jnp.where(lane == i, info[i : i + 1, 0:1].astype(F32), tail)
    main_ref[:, features:] = tail.astype(BF16)

    spare = jnp.where((owner == full) & (place >= even), place - even, -1)
    chosen = (iota((spare_slots, group), 0) == spare).astype(BF16)
    rest_ref[:, :features] = jnp.dot(chosen, rows, preferred_element_type=F32).astype(BF16)
    rest_ref[:, features:] = rows_by_rows(chosen, numbers).astype(BF16)


def route(at, info, gathered, features, owners, even, spare_slots):
    group = gathered.shape[0]
    wide = features + LANES
    return pl.pallas_call(
        functools.partial(route_kernel, owners, even),
        grid_spec=pltpu.PrefetchScalarGridSpec(
            num_scalar_prefetch=1,
            grid=(1,),
            in_specs=[
                pl.BlockSpec((8, group), lambda i, at: (0, 0)),
                pl.BlockSpec((group, features), lambda i, at: (0, at[0])),
            ],
            out_specs=(
                pl.BlockSpec((owners * even, wide), lambda i, at: (0, 0)),
                pl.BlockSpec((spare_slots, wide), lambda i, at: (0, 0)),
            ),
        ),
        out_shape=(
            jax.ShapeDtypeStruct((owners * even, wide), BF16),
            jax.ShapeDtypeStruct((spare_slots, wide), BF16),
        ),
        compiler_params=pltpu.CompilerParams(vmem_limit_bytes=SMALL),
        name="route",
    )(at, info, gathered)


def low_kernel(rank, labels_ref, rows_ref, extra_ref, down_ref, low_ref, local_ref):
    step = pl.program_id(0)
    some = down_ref.shape[0] // rank
    local = lane_as_row(extra_ref[...], 1)
    wide = rows_by_rows(down_ref[...], rows_ref[...])
    total = jnp.zeros(low_ref.shape, F32)
    for i in range(some):
        label = labels_ref[step * some + i]
        total += jnp.where(local[0:1] == label, wide[i * rank : (i + 1) * rank], 0.0)

    @pl.when(step == 0)
    def _():
        local_ref[...] = local
        low_ref[...] = total

    @pl.when(step != 0)
    def _():
        low_ref[...] += total


def low_part(labels, rows, down, rank, limit):
    count, wide = rows.shape
    features = wide - LANES
    steps = 4
    return pl.pallas_call(
        functools.partial(low_kernel, rank),
        grid=(steps,),
        in_specs=[
            pl.BlockSpec(memory_space=pltpu.SMEM),
            pl.BlockSpec((count, features), lambda i: (0, 0)),
            pl.BlockSpec((count, LANES), lambda i: (0, features // LANES)),
            pl.BlockSpec((down.shape[0] // steps, features), lambda i: (i, 0)),
        ],
        out_specs=(
            pl.BlockSpec((rank, count), lambda i: (0, 0)),
            pl.BlockSpec((8, count), lambda i: (0, 0)),
        ),
        out_shape=(
            jax.ShapeDtypeStruct((rank, count), F32),
            jax.ShapeDtypeStruct((8, count), I32),
        ),
        compiler_params=pltpu.CompilerParams(vmem_limit_bytes=limit),
        cost_estimate=pl.CostEstimate(
            flops=2 * count * down.shape[0] * features,
            bytes_accessed=2 * features * (count + down.shape[0]),
            transcendentals=0,
        ),
        name="low",
    )(labels, rows, rows, down)


def spread(low, local, labels):
    rank, places = low.shape[0], labels.shape[1]
    repeat = (iota((rank, places), 1) % rank == iota((rank, places), 0)).astype(BF16)
    values = columns_by_columns(low, repeat)
    return jnp.where(local == labels, values, 0.0).astype(BF16)


def delta_kernel(low_ref, extra_ref, up_ref, out_ref, wide_ref):
    rank, places = low_ref.shape[0], up_ref.shape[0]

    @pl.when(pl.program_id(0) == 0)
    def _():
        local = extra_ref[:, 1:2].astype(F32).astype(I32)
        wide_ref[...] = spread(low_ref[...], local, iota((1, places), 1) // rank)

    out_ref[...] = (2.0 * jnp.dot(wide_ref[...], up_ref[...], preferred_element_type=F32)).astype(BF16)


def delta_of(low, rows, up, tile):
    count, wide = rows.shape
    places, columns = up.shape
    return pl.pallas_call(
        delta_kernel,
        grid=(columns // tile,),
        in_specs=[
            pl.BlockSpec(low.shape, lambda i: (0, 0)),
            pl.BlockSpec((count, LANES), lambda i: (0, wide // LANES - 1)),
            pl.BlockSpec((places, tile), lambda i: (0, i)),
        ],
        out_specs=pl.BlockSpec((count, tile), lambda i: (0, i)),
        out_shape=jax.ShapeDtypeStruct((count, columns), BF16),
        scratch_shapes=[pltpu.VMEM((count, places), BF16)],
        compiler_params=pltpu.CompilerParams(vmem_limit_bytes=SMALL),
        cost_estimate=pl.CostEstimate(
            flops=2 * count * up.size, bytes_accessed=2 * (up.size + count * columns), transcendentals=0
        ),
        name="delta",
    )(low, rows, up)


def finish_kernel(
    even,
    full_ref,
    labels_ref,
    tall_ref,
    low_ref,
    extra_ref,
    base_ref,
    back_ref,
    up_ref,
    out_ref,
    wide_ref,
    main_ref,
    rest_ref,
):
    @pl.when(pl.program_id(0) == 0)
    def _():
        owner, place = tall_ref[:, 0:1], tall_ref[:, 2:3]
        target = jnp.where(place < even, owner * even + place, -1)
        main_ref[...] = (iota(main_ref.shape, 1) == target).astype(BF16)
        spare = jnp.where((owner == full_ref[0]) & (place >= even), place - even, -1)
        rest_ref[...] = (iota(rest_ref.shape, 1) == spare).astype(BF16)
        local = extra_ref[:, 1:2].astype(F32).astype(I32)
        wide_ref[...] = spread(low_ref[...], local, labels_ref[0:1])

    delta = (2.0 * jnp.dot(wide_ref[...], up_ref[...], preferred_element_type=F32)).astype(BF16)
    total = base_ref[...] + jnp.dot(main_ref[...], back_ref[...], preferred_element_type=F32)
    total += jnp.dot(rest_ref[...], delta, preferred_element_type=F32)
    out_ref[...] = total.astype(BF16)


def finish(full, labels, tall, low, rows, base, back, weights, even, tile):
    group, columns = base.shape
    skip = (weights.shape[1] - columns) // tile
    whole = lambda a: pl.BlockSpec(a.shape, lambda i: (0, 0))
    cut = lambda a: pl.BlockSpec((a.shape[0], tile), lambda i: (0, i))
    return pl.pallas_call(
        functools.partial(finish_kernel, even),
        grid=(columns // tile,),
        in_specs=[
            pl.BlockSpec(memory_space=pltpu.SMEM),
            whole(labels),
            whole(tall),
            whole(low),
            pl.BlockSpec((rows.shape[0], LANES), lambda i: (0, rows.shape[1] // LANES - 1)),
            cut(base),
            cut(back),
            pl.BlockSpec((weights.shape[0], tile), lambda i: (0, i + skip)),
        ],
        out_specs=pl.BlockSpec((group, tile), lambda i: (0, i)),
        out_shape=jax.ShapeDtypeStruct((group, columns), BF16),
        scratch_shapes=[
            pltpu.VMEM((low.shape[1], weights.shape[0]), BF16),
            pltpu.VMEM((group, back.shape[0]), BF16),
            pltpu.VMEM((group, low.shape[1]), BF16),
        ],
        compiler_params=pltpu.CompilerParams(vmem_limit_bytes=LIMIT),
        name="finish",
    )(full, labels, tall, low, rows, base, back, weights)


def exchange(block, axis):
    return lax.all_to_all(block, axis, split_axis=0, concat_axis=0, tiled=True)


SIDE = 4


def neighbour(block, dim, step):
    def to(i):
        at = [i // SIDE, i % SIDE]
        at[dim] = (at[dim] + step) % SIDE
        return at[0] * SIDE + at[1]

    return lax.ppermute(block, "adapter", [(i, to(i)) for i in range(SIDE * SIDE)])


def send_ring(block, dim):
    quarter = block.shape[0] // SIDE
    parts = [block[i * quarter : (i + 1) * quarter] for i in range(SIDE)]
    return [parts[0]] + [neighbour(parts[i], dim, i) for i in range(1, SIDE)]


def keep(got, away):
    return jnp.where(
        away == 0, got[0], jnp.where(away == 1, got[1], jnp.where(away == 2, got[2], got[3]))
    )


def scatter_start(matrix):
    half = matrix.shape[0] // 2
    return [send_ring(matrix[:half], 0), send_ring(matrix[half:], 1)]


def scatter_end(started, root):
    me = lax.axis_index("adapter").astype(I32)
    away = ((me // SIDE - root // SIDE) % SIDE, (me % SIDE - root % SIDE) % SIDE)
    parts = []
    for first, got in enumerate(started):
        second = 1 - first
        parts.append(keep(send_ring(keep(got, away[first]), second), away[second]))
    return jnp.concatenate(parts, axis=0)


def scattered_order(root, held):
    member, slot = jnp.arange(held) // 4, jnp.arange(held) % 4
    x, z = (member // SIDE - root // SIDE) % SIDE, (member % SIDE - root % SIDE) % SIDE
    quarter = held // 2 // SIDE
    sixteenth = quarter // SIDE
    one = x * quarter + z * sixteenth + slot
    other = held // 2 + z * quarter + x * sixteenth + slot - 2
    return jnp.where(slot < 2, one, other).astype(I32)


def swapped(block, bit):
    members = lax.axis_size("tensor")
    return lax.ppermute(block, "tensor", [(i, i ^ bit) for i in range(members)])


def total_over_tensor(part):
    part = part + swapped(part, 1)
    others = [swapped(part, bit) for bit in (2, 4, 6)]
    return (part + others[0]) + (others[1] + others[2])


def per_device(
    tokens, token_adapter_index, joined_weight_matrix, adapter_down_weight, adapter_up_weight
):
    owners = lax.axis_size("adapter")
    members = lax.axis_size("tensor")
    local_rows, width = tokens.shape
    group = members * local_rows
    held, rank, features = adapter_down_weight.shape
    columns = adapter_up_weight.shape[2]
    capacity = 4 * group // owners
    even = group // owners
    down = adapter_down_weight.reshape(held * rank, features)
    up = adapter_up_weight.reshape(held * rank, columns)
    wide = features + LANES

    order = jnp.arange(held, dtype=I32)
    gathered = lax.all_gather(tokens, "tensor", axis=0, tiled=True)
    started = scatter_start(jnp.concatenate([down, up], axis=1))
    ids = lax.all_gather(token_adapter_index, "tensor", axis=0, tiled=True)
    started, ids = lax.optimization_barrier((started, ids))
    info, tall = plan(ids, owners, held, even)

    named = info[3, 0]
    piece = scatter_end(started, named)
    weights = lax.all_gather(piece, "adapter", axis=0, tiled=True)
    labels = scattered_order(named, held)

    here = lax.axis_index("tensor").astype(I32).reshape(1)
    send, rest_rows = route(here, info, gathered, features, owners, even, capacity)
    rows = exchange(send.reshape(owners, even, wide), "adapter")

    said = rows[:, 0, features + 3 : features + 6].astype(I32)
    same = jnp.all(said[:, 0] == said[0, 0])
    full = jnp.where(same, said[0, 0], -1)
    largest = jnp.where(same, jnp.max(said[:, 1]), jnp.max(said[:, 2]))
    turns = (largest + even - 1) // even

    base = jnp.dot(gathered, joined_weight_matrix, preferred_element_type=F32)
    rows, base = lax.optimization_barrier((rows, base))

    rows = rows.reshape(owners * even, wide)
    part, _ = low_part(order, rows, down, rank, SMALL)
    low = total_over_tensor(part).astype(BF16)
    delta = delta_of(low, rows, up, 256)
    rest_rows, delta, full, turns, labels = lax.optimization_barrier(
        (rest_rows, delta, full, turns, labels)
    )
    back = exchange(delta.reshape(owners, even, columns), "adapter").reshape(owners * even, columns)

    owner, place = info[0], info[2]

    def more(carry):
        turn, total = carry
        turn, source = lax.optimization_barrier((turn, gathered))
        wanted = (owner != full) & (place // even == turn)
        slot = jnp.where(wanted, owner * even + place % even, -1)
        chosen = (slot[None, :] == jnp.arange(owners * even, dtype=I32)[:, None]).astype(BF16)
        mine = lax.dynamic_slice_in_dim(source, here[0] * features, features, 1)
        numbers = jnp.pad(info[1][:, None].astype(BF16), ((0, 0), (1, LANES - 2)))
        mine = jnp.concatenate([mine, numbers], axis=1)
        moved = jnp.dot(chosen, mine, preferred_element_type=F32).astype(BF16)
        moved = exchange(moved.reshape(owners, even, wide), "adapter").reshape(owners * even, wide)
        more_part, _ = low_part(order, moved, down, rank, SMALL)
        more_low = total_over_tensor(more_part).astype(BF16)
        more_delta = delta_of(more_low, moved, up, 256).reshape(owners, even, columns)
        more_back = exchange(more_delta, "adapter").reshape(owners * even, columns)
        return turn + 1, total + jnp.dot(chosen.T, more_back, preferred_element_type=F32)

    _, base = lax.while_loop(lambda carry: carry[0] < turns, more, (jnp.int32(1), base))

    rest_part, _ = low_part(labels, rest_rows, weights, rank, LIMIT)
    rest_low = total_over_tensor(rest_part).astype(BF16)
    places = jnp.broadcast_to(jnp.repeat(labels, rank)[None], (8, held * rank))
    return finish(full.reshape(1), places, tall, rest_low, rest_rows, base, back, weights, even, 256)


def solution(mesh):
    return jax.shard_map(
        per_device,
        mesh=mesh,
        in_specs=(
            P(("adapter", "tensor"), None),
            P(("adapter", "tensor")),
            P(None, "tensor"),
            P("adapter", None, "tensor"),
            P("adapter", None, "tensor"),
        ),
        out_specs=P("adapter", "tensor"),
        check_vma=False,
    )
```

time: 206 us -> 169 us (0.82)
  local copies, waits for them, and re-layouts: 30.8 us -> 4.48 us
  blocking collectives: 22 us -> 9.6 us
  other arithmetic: 2.85 us -> 11 us
  waiting for transfers between devices: 49.8 us -> 43.5 us
  between operations: 16.9 us -> 19.9 us
  starting transfers between devices: 40.4 us -> 37.9 us
    all_to_all x4 -> x2, waiting for transfers between devices: 29.2 us -> 0.01 us  [exchange(): return lax.all_to_all(block, axis, split_axis=0, concat_axis=0, tiled=True)]
    all_to_all x1 -> x0, blocking collectives: 22 us -> none  [exchange(): return lax.all_to_all(block, axis, split_axis=0, concat_axis=0, tiled=True)]
    all_to_all x4 -> x2, starting transfers between devices: 30.8 us -> 12.9 us  [exchange(): return lax.all_to_all(block, axis, split_axis=0, concat_axis=0, tiled=True)]
    all_gather x2, waiting for transfers between devices: 0.02 us -> 16.1 us  [the longest x1 16.1 us: per_device(): weights = lax.all_gather(piece, 'adapter', axis=0, tiled=True)]
    dynamic_update_slice x8 -> x0, local copies, waits for them, and re-layouts: 13.4 us -> none  [the longest x4 7.99 us: gather_rows(): full = lax.dynamic_update_slice(full, other, (start + (1 - core) * rows, 0))]
    ppermute x4 -> x12, waiting for transfers between devices: 9.94 us -> 21.7 us  [neighbour(): lax.ppermute(block, 'adapter', [(i, to(i)) for i in range(SIDE * SIDE)])]
    ppermute x4 -> x12, starting transfers between devices: 6.54 us -> 16.6 us  [neighbour(): lax.ppermute(block, 'adapter', [(i, to(i)) for i in range(SIDE * SIDE)])]
    optimization_barrier x0 -> x1, blocking collectives: none -> 9.6 us  [per_device(): started, ids = lax.optimization_barrier((started, ids))]
  transfers between devices with their start and end apart: 20 -> 24, of which waited for: 7 -> 12; matrix products, arithmetic and copies ran while one was open for 22% -> 19% of each run, Pallas kernels for 7% -> 10%
where the time goes in v2:
time: 169 us; the launch traced here: 168 us
  waiting for transfers between devices  43.5 us (26%)
  starting transfers between devices  37.9 us (22%)
  Pallas kernels  23.2 us (14%)
  between operations  19.9 us (12%)
  matrix products  18.1 us (11%)
  other arithmetic  11 us (7%)
  blocking collectives  9.6 us (6%)
  local copies, waits for them, and re-layouts  4.48 us (3%)
    ppermute x12, waiting for transfers between devices, neighbour(): lax.ppermute(block, 'adapter', [(i, to(i)) for i in range(SIDE * SIDE)])  21.7 us
    dot_general x1, matrix products, per_device(): base = jnp.dot(gathered, joined_weight_matrix, preferred_element_type=F32)  18.1 us
    ppermute x12, starting transfers between devices, neighbour(): lax.ppermute(block, 'adapter', [(i, to(i)) for i in range(SIDE * SIDE)])  16.6 us
    all_gather x1, waiting for transfers between devices, per_device(): weights = lax.all_gather(piece, 'adapter', axis=0, tiled=True)  16.1 us
    all_to_all x2, starting transfers between devices, exchange(): return lax.all_to_all(block, axis, split_axis=0, concat_axis=0, tiled=True)  12.9 us
    optimization_barrier x1, blocking collectives, per_device(): started, ids = lax.optimization_barrier((started, ids))  9.6 us
    ppermute x8, starting transfers between devices, swapped(): return lax.ppermute(block, 'tensor', [(i, i ^ bit) for i in range(members)])  8.27 us
    pallas_call x2, Pallas kernels, low_part(): pl.pallas_call(functools.partial(low_kernel, rank), grid=(steps,), in_spe...  7.11 us
  transfers between devices with their start and end apart: 24, of which 12 were waited for; matrix products, arithmetic and copies ran while one was open for 19% of the time, Pallas kernels for 10%

profile of v2, /device:TPU:2, one launch (start us, length us, event | category | flops | bytes accessed | tf_op | source)
XLA Modules:
  0.0 167.7 jit_solution(8841063757629901008)
XLA Ops:
  6.5 0.7 all-gather.3.cloned.1.call-update
  7.3 0.0 all-gather.5.cloned.1.call-start
  7.3 3.4 %pad_maximum_fusion = (bf16[128,2304]{1,0:T(8,128)(2,1)S(1)}, bf16[128,2304]{1,0:T(8,128)(2,1)S(1)}, bf16[128,2304]{1,0:T(8,128)(2,1)}, bf16[128,2304]{1,0:T(8,1...) fusion(bf16[1024,1280]{1,0:T(8,128)(2,1)} %bitcast.45, ...), kind=kLoop, calls=%fused_computation.50 | loop fusion | flops 9437184 | bytes 9437184 | tf_op jit(solution)/shard_map/concatenate | solution.py:352
  10.7 4.1 %collective-permute-start.9 = (bf16[128,2304]{1,0:T(8,128)(2,1)S(1)}, bf16[128,2304]{1,0:T(8,128)(2,1)S(1)}, u32[]{:S(2)}, u32[]{:S(2)}) collective-permute-start(bf16[128,2304]{1,0:T(8,128)(2,1)S(1)} %get-tuple-element.445), channel_id=1, source_target_pairs={{0,24},{8,0},{16,8},{24,16},{32,56},{40,32},{48,40},{56,48},{64,88... | collective-permute-start | bytes 1769480 | tf_op jit(solution)/shard_map/ppermute | solution.py:284
  14.8 1.5 collective-permute-start.4
  16.3 1.1 collective-permute-start.5
  17.4 2.2 %collective-permute-start.6 = (bf16[128,2304]{1,0:T(8,128)(2,1)S(1)}, bf16[128,2304]{1,0:T(8,128)(2,1)}, u32[]{:S(2)}, u32[]{:S(2)}) collective-permute-start(bf16[128,2304]{1,0:T(8,128)(2,1)S(1)} %get-tuple-element.449), channel_id=1, source_target_pairs={{0,96},{8,104},{16,112},{24,120},{32,0},{40,8},{48,16},{56,24},{64... | collective-permute-start | bytes 1769480 | tf_op jit(solution)/shard_map/ppermute | solution.py:284
  19.6 7.8 %collective-permute-done.9 = bf16[128,2304]{1,0:T(8,128)(2,1)S(1)} collective-permute-done((bf16[128,2304]{1,0:T(8,128)(2,1)S(1)}, bf16[128,2304]{1,0:T(8,128)(2,1)S(1)}, u32[]{:S(2)}, u32[]{:S(2)}) %collective-permute-start.9) | collective-permute-done | bytes 589856 | tf_op jit(solution)/shard_map/ppermute | solution.py:284
  27.4 2.3 %collective-permute-start.8 = (bf16[128,2304]{1,0:T(8,128)(2,1)S(1)}, bf16[128,2304]{1,0:T(8,128)(2,1)}, u32[]{:S(2)}, u32[]{:S(2)}) collective-permute-start(bf16[128,2304]{1,0:T(8,128)(2,1)S(1)} %get-tuple-element.452), channel_id=1, source_target_pairs={{0,16},{8,24},{16,0},{24,8},{32,48},{40,56},{48,32},{56,40},{64,80... | collective-permute-start | bytes 1769480 | tf_op jit(solution)/shard_map/ppermute | solution.py:284
  29.7 0.6 dynamic-slice
  30.9 0.2 dynamic-update-slice
  31.2 9.6 %all-reduce.1 = s32[512]{0:T(512)S(1)} all-reduce(s32[512]{0:T(512)S(1)} %dynamic-update-slice), channel_id=1, replica_groups=mesh['adapter'=16,'tensor'=8] {'tensor'}, use_global_device_ids=true, to_apply=%add.1 | all-reduce | flops 512 | bytes 4096 | tf_op jit(solution)/shard_map/optimization_barrier | solution.py:354
  40.8 3.6 %collective-permute-done.6 = bf16[128,2304]{1,0:T(8,128)(2,1)} collective-permute-done((bf16[128,2304]{1,0:T(8,128)(2,1)S(1)}, bf16[128,2304]{1,0:T(8,128)(2,1)}, u32[]{:S(2)}, u32[]{:S(2)}) %collective-permute-start.6) | collective-permute-done | bytes 589856 | tf_op jit(solution)/shard_map/ppermute | solution.py:284
  44.4 3.1 %collective-permute-done.7 = bf16[128,2304]{1,0:T(8,128)(2,1)} collective-permute-done((bf16[128,2304]{1,0:T(8,128)(2,1)S(1)}, bf16[128,2304]{1,0:T(8,128)(2,1)}, u32[]{:S(2)}, u32[]{:S(2)}) %collective-permute-start.7) | collective-permute-done | bytes 589856 | tf_op jit(solution)/shard_map/ppermute | solution.py:284
  47.5 0.3 plan.1
  47.8 0.7 copy-done.1
  48.5 0.5 slice.102
  51.7 1.3 select_select_fusion
  53.0 1.4 collective-permute-start.19
  54.4 1.7 %collective-permute-start.17 = (bf16[32,2304]{1,0:T(8,128)(2,1)S(1)}, bf16[32,2304]{1,0:T(8,128)(2,1)S(1)}, u32[]{:S(2)}, u32[]{:S(2)}) collective-permute-start(bf16[32,2304]{1,0:T(8,128)(2,1)S(1)} %get-tuple-element.458), channel_id=1, source_target_pairs={{0,32},{8,40},{16,48},{24,56},{32,64},{40,72},{48,80},{56,88},{64,... | collective-permute-start | bytes 442376 | tf_op jit(solution)/shard_map/ppermute | solution.py:284
  56.2 1.2 select_select_fusion.1
  57.4 0.6 fusion.25
  58.0 0.2 copy.14
  58.2 1.2 collective-permute-start.16
  59.3 0.5 compare_select_fusion.5.labels_ref
  59.9 1.1 collective-permute-start.14
  60.9 0.1 collective-permute-done.18
  61.1 0.8 collective-permute-done.17
  61.9 1.5 collective-permute-done.16
  63.4 3.2 %collective-permute-done.15 = bf16[32,2304]{1,0:T(8,128)(2,1)S(1)} collective-permute-done((bf16[32,2304]{1,0:T(8,128)(2,1)S(1)}, bf16[32,2304]{1,0:T(8,128)(2,1)S(1)}, u32[]{:S(2)}, u32[]{:S(2)}) %collective-permute-start.15) | collective-permute-done | bytes 147488 | tf_op jit(solution)/shard_map/ppermute | solution.py:284
  66.6 1.5 collective-permute-done.14
  68.1 0.7 pad_maximum_fusion.1
  68.9 0.0 all-gather.5.cloned.1.call-update
  68.9 0.0 all-gather.3.cloned.1.call-done.rows_ref
  68.9 3.2 %route.1 = (bf16[512,1152]{1,0:T(8,128)(2,1)}, bf16[128,1152]{1,0:T(8,128)(2,1)S(1)}) custom-call(s32[1]{0:T(128)} %bitcast.at_ref, s32[8,512]{1,0:T(8,128)S(1)} %get-tuple-element.317.info_ref, bf16[512,8192]{1,0:T(8,128)(2,1)} %all-gather.3.cloned.1.call-done.rows_ref), custom_call_target="tpu_custom_call" | custom-call | tf_op jit(solution)/shard_map/route/pallas_call | solution.py:96
  72.2 0.7 copy-done
  72.9 5.7 %all-to-all-start.2 = ((bf16[16,32,1152]{2,1,0:T(8,128)(2,1)}), bf16[16,32,1152]{2,1,0:T(8,128)(2,1)S(1)}, u32[]{:S(2)}, u32[]{:S(2)}) async-start(bf16[16,32,1152]{2,1,0:T(8,128)(2,1)} %bitcast.4), calls=%async_computation.2 | async-start | bytes 2359296 | tf_op jit(solution)/shard_map/all_to_all | solution.py:272
  78.5 18.1 %fusion.31 = f32[512,1280]{1,0:T(8,128)} fusion(bf16[512,8192]{1,0:T(8,128)(2,1)} %all-gather.3.cloned.1.call-done.rows_ref, bf16[8192,1280]{1,0:T(8,128)(2,1)} %param.9), kind=kOutput, calls=%fused_computation.87 | convolution fusion | flops 10737418240 | bytes 31981568 | tf_op jit(solution)/shard_map/dot_general | solution.py:372
  96.7 0.1 slice.128
  96.8 0.1 copy.16
  96.9 3.3 %low.8 = (f32[16,512]{1,0:T(8,128)S(1)}, s32[8,512]{1,0:T(8,128)}) custom-call(s32[64]{0:T(128)S(1)} %iota.30.labels_ref, bf16[512,1152]{1,0:T(8,128)(2,1)S(1)} %bitcast.41, bf16[512,1152]{1,0:T(8,128)(2,1)S(1)} %bitcast.42, bf16[1024,1024]{1,0:T(8,128)(2,1)S(1)} %bitcast.49), custom_call_target="tpu_custom_call" | custom-call | flops 1073741824 | bytes 3145728 | tf_op jit(solution)/shard_map/low/pallas_call | solution.py:143
  100.2 0.7 slice_reduce_fusion
  100.9 0.5 slice.99
  101.4 0.0 collective-permute-done.10
  101.4 3.1 %collective-permute-start.13 = (f32[16,512]{1,0:T(8,128)S(1)}, f32[16,512]{1,0:T(8,128)S(1)}, u32[]{:S(2)}, u32[]{:S(2)}) collective-permute-start(f32[16,512]{1,0:T(8,128)S(1)} %add.180), channel_id=1, source_target_pairs={{0,6},{1,7},{2,4},{3,5},{4,2},{5,3},{6,0},{7,1},{8,14},{9,15},{10,... | collective-permute-start | bytes 98312 | tf_op jit(solution)/shard_map/ppermute | solution.py:326
  104.5 0.6 collective-permute-start.12
  105.1 0.5 collective-permute-start.11
  105.6 1.3 compare_reduce_fusion.1
  110.0 5.9 %delta.7 = bf16[512,1280]{1,0:T(8,128)(2,1)} custom-call(bf16[16,512]{1,0:T(8,128)(2,1)S(1)} %add_convert_fusion.1.low_ref, bf16[512,1152]{1,0:T(8,128)(2,1)S(1)} %bitcast.43, bf16[1024,1280]{1,0:T(8,128)(2,1)} %bitcast.46), custom_call_target="tpu_custom_call" | custom-call | flops 1342177280 | bytes 3932160 | tf_op jit(solution)/shard_map/delta/pallas_call | solution.py:191
  115.9 7.3 %all-to-all-start.3 = ((bf16[16,32,1280]{2,1,0:T(8,128)(2,1)}), bf16[16,32,1280]{2,1,0:T(8,128)(2,1)}, u32[]{:S(2)}, u32[]{:S(2)}) async-start(bf16[16,32,1280]{2,1,0:T(8,128)(2,1)} %bitcast.12), calls=%async_computation.3 | async-start | bytes 2621440 | tf_op jit(solution)/shard_map/all_to_all | solution.py:272
  123.2 16.1 %all-gather.5.cloned.1.call-done.down_ref.up_ref = bf16[1024,2304]{1,0:T(8,128)(2,1)} async-done(((bf16[64,2304]{1,0:T(8,128)(2,1)}), bf16[1024,2304]{1,0:T(8,128)(2,1)}) %all-gather.5.cloned.1.call-update) | async-done | bytes 4718608 | tf_op jit(solution)/shard_map/all_gather | solution.py:359
  139.3 3.8 %low.9 = (f32[16,128]{1,0:T(8,128)}, s32[8,128]{1,0:T(8,128)}) custom-call(s32[64]{0:T(128)} %compare_select_fusion.5.labels_ref, bf16[128,1152]{1,0:T(8,128)(2,1)} %copy-done, bf16[128,1152]{1,0:T(8,128)(2,1)} %copy-done, bf16[1024,2304]{1,0:T(8,128)(2,1)} %all-gather.5.cloned.1.call-done.down_ref.up_ref), custom_call_target="tpu_custom_call" | custom-call | flops 268435456 | bytes 2359296 | tf_op jit(solution)/shard_map/low/pallas_call | solution.py:143
  143.1 1.4 collective-permute-done.20
  144.5 0.7 add.198
  145.2 2.6 %collective-permute-start.23 = (f32[16,128]{1,0:T(8,128)S(1)}, f32[16,128]{1,0:T(8,128)S(1)}, u32[]{:S(2)}, u32[]{:S(2)}) collective-permute-start(f32[16,128]{1,0:T(8,128)S(1)} %add.198), channel_id=1, source_target_pairs={{0,6},{1,7},{2,4},{3,5},{4,2},{5,3},{6,0},{7,1},{8,14},{9,15},{10,... | collective-permute-start | bytes 24584 | tf_op jit(solution)/shard_map/ppermute | solution.py:326
  147.8 0.9 collective-permute-start.22
  148.7 0.5 collective-permute-start.21
  149.3 0.1 broadcast_in_dim.13
  149.3 0.1 broadcast_in_dim.22
  149.4 0.6 collective-permute-done.23
  150.0 2.9 %collective-permute-done.22 = f32[16,128]{1,0:T(8,128)S(1)} collective-permute-done((f32[16,128]{1,0:T(8,128)S(1)}, f32[16,128]{1,0:T(8,128)S(1)}, u32[]{:S(2)}, u32[]{:S(2)}) %collective-permute-start.22) | collective-permute-done | bytes 8224 | tf_op jit(solution)/shard_map/ppermute | solution.py:326
  153.0 0.6 add_convert_fusion.2.low_ref
  153.6 0.6 broadcast_in_dim.23.labels_ref
  154.2 6.7 %finish.1 = bf16[512,1280]{1,0:T(8,128)(2,1)} custom-call(s32[1]{0:T(128)} %bitcast.8.full_ref, s32[8,1024]{1,0:T(8,128)} %broadcast_in_dim.23.labels_ref, s32[512,128]{1,0:T(8,128)} %copy-done.1, bf16[16,128]{1,0:T(8,128)(2,1)} %add_convert_fusion.2.low_ref, bf16[128,1152]{1,0:T(8,128)(2,1)} %copy-done, f32[512,1280]{1,0:T(8,128)S(1)} %copy-done.4, ...), custom_call_target="tpu_custom_call" | custom-call | tf_op jit(solution)/shard_map/finish/pallas_call | solution.py:246
  (43 shorter events, 0.3 us)
Async XLA Ops:
  6.5 62.4 %all-gather.3.cloned.1.call-start = ((), (), s32[]{:S(2)}) async-start(), calls=%async_computation.4 | async-start | bytes 9437184 | tf_op jit(solution)/shard_map/all_gather | solution.py:351
  7.3 132.0 %all-gather.5.cloned.1.call-start = ((), (), s32[]{:S(2)}) async-start(), calls=%async_computation.5 | async-start | bytes 5013504 | tf_op jit(solution)/shard_map/all_gather | solution.py:359
  7.3 22.4 %copy-start.8 = (u32[128]{0:T(128)S(1)}, u32[128]{0:T(128)}, u32[]{:S(2)}) copy-start(u32[128]{0:T(128)} %constant.217) | copy-start | bytes 1540
  7.3 23.6 %copy-start.7 = (s32[64]{0:T(128)S(1)}, s32[64]{0:T(128)}, u32[]{:S(2)}) copy-start(s32[64]{0:T(128)} %param.8) | copy-start | bytes 772
  10.7 16.7 %collective-permute-start.9 = (bf16[128,2304]{1,0:T(8,128)(2,1)S(1)}, bf16[128,2304]{1,0:T(8,128)(2,1)S(1)}, u32[]{:S(2)}, u32[]{:S(2)}) collective-permute-start(bf16[128,2304]{1,0:T(8,128)(2,1)S(1)} %get-tuple-element.445), channel_id=1, source_target_pairs={{0,24},{8,0},{16,8},{24,16},{32,56},{40,32},{48,40},{56,48},{64,88... | collective-permute-start | bytes 1769480 | tf_op jit(solution)/shard_map/ppermute | solution.py:284
  14.8 26.0 %collective-permute-start.4 = (bf16[128,2304]{1,0:T(8,128)(2,1)}, bf16[128,2304]{1,0:T(8,128)(2,1)}, u32[]{:S(2)}, u32[]{:S(2)}) collective-permute-start(bf16[128,2304]{1,0:T(8,128)(2,1)} %get-tuple-element.447), channel_id=1, source_target_pairs={{0,32},{8,40},{16,48},{24,56},{32,64},{40,72},{48,80},{56,88},{64,... | collective-permute-start | bytes 1769480 | tf_op jit(solution)/shard_map/ppermute | solution.py:284
  16.3 24.5 %collective-permute-start.5 = (bf16[128,2304]{1,0:T(8,128)(2,1)S(1)}, bf16[128,2304]{1,0:T(8,128)(2,1)}, u32[]{:S(2)}, u32[]{:S(2)}) collective-permute-start(bf16[128,2304]{1,0:T(8,128)(2,1)S(1)} %get-tuple-element.448), channel_id=1, source_target_pairs={{0,64},{8,72},{16,80},{24,88},{32,96},{40,104},{48,112},{56,120},{... | collective-permute-start | bytes 1769480 | tf_op jit(solution)/shard_map/ppermute | solution.py:284
  17.4 27.0 %collective-permute-start.6 = (bf16[128,2304]{1,0:T(8,128)(2,1)S(1)}, bf16[128,2304]{1,0:T(8,128)(2,1)}, u32[]{:S(2)}, u32[]{:S(2)}) collective-permute-start(bf16[128,2304]{1,0:T(8,128)(2,1)S(1)} %get-tuple-element.449), channel_id=1, source_target_pairs={{0,96},{8,104},{16,112},{24,120},{32,0},{40,8},{48,16},{56,24},{64... | collective-permute-start | bytes 1769480 | tf_op jit(solution)/shard_map/ppermute | solution.py:284
  19.6 27.9 %collective-permute-start.7 = (bf16[128,2304]{1,0:T(8,128)(2,1)S(1)}, bf16[128,2304]{1,0:T(8,128)(2,1)}, u32[]{:S(2)}, u32[]{:S(2)}) collective-permute-start(bf16[128,2304]{1,0:T(8,128)(2,1)S(1)} %get-tuple-element.451), channel_id=1, source_target_pairs={{0,8},{8,16},{16,24},{24,0},{32,40},{40,48},{48,56},{56,32},{64,72... | collective-permute-start | bytes 1769480 | tf_op jit(solution)/shard_map/ppermute | solution.py:284
  27.4 2.3 %copy-start.5 = (bf16[128,2304]{1,0:T(8,128)(2,1)}, bf16[128,2304]{1,0:T(8,128)(2,1)S(1)}, u32[]{:S(2)}) copy-start(bf16[128,2304]{1,0:T(8,128)(2,1)S(1)} %collective-permute-done.9) | copy-start | bytes 1769476
  27.4 20.1 %collective-permute-start.8 = (bf16[128,2304]{1,0:T(8,128)(2,1)S(1)}, bf16[128,2304]{1,0:T(8,128)(2,1)}, u32[]{:S(2)}, u32[]{:S(2)}) collective-permute-start(bf16[128,2304]{1,0:T(8,128)(2,1)S(1)} %get-tuple-element.452), channel_id=1, source_target_pairs={{0,16},{8,24},{16,0},{24,8},{32,48},{40,56},{48,32},{56,40},{64,80... | collective-permute-start | bytes 1769480 | tf_op jit(solution)/shard_map/ppermute | solution.py:284
  47.8 0.7 copy-start.1
  53.0 6.9 %collective-permute-start.19 = (bf16[32,2304]{1,0:T(8,128)(2,1)S(1)}, bf16[32,2304]{1,0:T(8,128)(2,1)S(1)}, u32[]{:S(2)}, u32[]{:S(2)}) collective-permute-start(bf16[32,2304]{1,0:T(8,128)(2,1)S(1)} %get-tuple-element.456), channel_id=1, source_target_pairs={{0,96},{8,104},{16,112},{24,120},{32,0},{40,8},{48,16},{56,24},{64... | collective-permute-start | bytes 442376 | tf_op jit(solution)/shard_map/ppermute | solution.py:284
  54.4 6.6 %collective-permute-start.18 = (bf16[32,2304]{1,0:T(8,128)(2,1)S(1)}, bf16[32,2304]{1,0:T(8,128)(2,1)S(1)}, u32[]{:S(2)}, u32[]{:S(2)}) collective-permute-start(bf16[32,2304]{1,0:T(8,128)(2,1)S(1)} %get-tuple-element.457), channel_id=1, source_target_pairs={{0,64},{8,72},{16,80},{24,88},{32,96},{40,104},{48,112},{56,120},{... | collective-permute-start | bytes 442376 | tf_op jit(solution)/shard_map/ppermute | solution.py:284
  54.4 7.5 %collective-permute-start.17 = (bf16[32,2304]{1,0:T(8,128)(2,1)S(1)}, bf16[32,2304]{1,0:T(8,128)(2,1)S(1)}, u32[]{:S(2)}, u32[]{:S(2)}) collective-permute-start(bf16[32,2304]{1,0:T(8,128)(2,1)S(1)} %get-tuple-element.458), channel_id=1, source_target_pairs={{0,32},{8,40},{16,48},{24,56},{32,64},{40,72},{48,80},{56,88},{64,... | collective-permute-start | bytes 442376 | tf_op jit(solution)/shard_map/ppermute | solution.py:284
  58.2 5.2 %collective-permute-start.16 = (bf16[32,2304]{1,0:T(8,128)(2,1)S(1)}, bf16[32,2304]{1,0:T(8,128)(2,1)S(1)}, u32[]{:S(2)}, u32[]{:S(2)}) collective-permute-start(bf16[32,2304]{1,0:T(8,128)(2,1)S(1)} %get-tuple-element.453), channel_id=1, source_target_pairs={{0,24},{8,0},{16,8},{24,16},{32,56},{40,32},{48,40},{56,48},{64,88... | collective-permute-start | bytes 442376 | tf_op jit(solution)/shard_map/ppermute | solution.py:284
  59.9 6.8 %collective-permute-start.15 = (bf16[32,2304]{1,0:T(8,128)(2,1)S(1)}, bf16[32,2304]{1,0:T(8,128)(2,1)S(1)}, u32[]{:S(2)}, u32[]{:S(2)}) collective-permute-start(bf16[32,2304]{1,0:T(8,128)(2,1)S(1)} %get-tuple-element.454), channel_id=1, source_target_pairs={{0,16},{8,24},{16,0},{24,8},{32,48},{40,56},{48,32},{56,40},{64,80... | collective-permute-start | bytes 442376 | tf_op jit(solution)/shard_map/ppermute | solution.py:284
  59.9 8.2 %collective-permute-start.14 = (bf16[32,2304]{1,0:T(8,128)(2,1)S(1)}, bf16[32,2304]{1,0:T(8,128)(2,1)S(1)}, u32[]{:S(2)}, u32[]{:S(2)}) collective-permute-start(bf16[32,2304]{1,0:T(8,128)(2,1)S(1)} %get-tuple-element.455), channel_id=1, source_target_pairs={{0,8},{8,16},{16,24},{24,0},{32,40},{40,48},{48,56},{56,32},{64,72... | collective-permute-start | bytes 442376 | tf_op jit(solution)/shard_map/ppermute | solution.py:284
  72.2 0.7 copy-start
  72.9 23.8 %all-to-all-start.2 = ((bf16[16,32,1152]{2,1,0:T(8,128)(2,1)}), bf16[16,32,1152]{2,1,0:T(8,128)(2,1)S(1)}, u32[]{:S(2)}, u32[]{:S(2)}) async-start(bf16[16,32,1152]{2,1,0:T(8,128)(2,1)} %bitcast.4), calls=%async_computation.2 | async-start | bytes 2359296 | tf_op jit(solution)/shard_map/all_to_all | solution.py:272
  78.5 18.4 %copy-start.3 = (bf16[64,16,1024]{2,1,0:T(8,128)(2,1)S(1)}, bf16[64,16,1024]{2,1,0:T(8,128)(2,1)}, u32[]{:S(2)}) copy-start(bf16[64,16,1024]{2,1,0:T(8,128)(2,1)} %param.10) | copy-start | bytes 6291460
  100.2 1.2 collective-permute-start.10
  101.4 8.5 %collective-permute-start.13 = (f32[16,512]{1,0:T(8,128)S(1)}, f32[16,512]{1,0:T(8,128)S(1)}, u32[]{:S(2)}, u32[]{:S(2)}) collective-permute-start(f32[16,512]{1,0:T(8,128)S(1)} %add.180), channel_id=1, source_target_pairs={{0,6},{1,7},{2,4},{3,5},{4,2},{5,3},{6,0},{7,1},{8,14},{9,15},{10,... | collective-permute-start | bytes 98312 | tf_op jit(solution)/shard_map/ppermute | solution.py:326
  104.5 5.5 %collective-permute-start.12 = (f32[16,512]{1,0:T(8,128)S(1)}, f32[16,512]{1,0:T(8,128)S(1)}, u32[]{:S(2)}, u32[]{:S(2)}) collective-permute-start(f32[16,512]{1,0:T(8,128)S(1)} %add.180), channel_id=1, source_target_pairs={{0,4},{1,5},{2,6},{3,7},{4,0},{5,1},{6,2},{7,3},{8,12},{9,13},{10,... | collective-permute-start | bytes 98312 | tf_op jit(solution)/shard_map/ppermute | solution.py:326
  105.1 4.8 %collective-permute-start.11 = (f32[16,512]{1,0:T(8,128)S(1)}, f32[16,512]{1,0:T(8,128)S(1)}, u32[]{:S(2)}, u32[]{:S(2)}) collective-permute-start(f32[16,512]{1,0:T(8,128)S(1)} %add.180), channel_id=1, source_target_pairs={{0,2},{1,3},{2,0},{3,1},{4,6},{5,7},{6,4},{7,5},{8,10},{9,11},{10,... | collective-permute-start | bytes 98312 | tf_op jit(solution)/shard_map/ppermute | solution.py:326
  115.9 37.7 %all-to-all-start.3 = ((bf16[16,32,1280]{2,1,0:T(8,128)(2,1)}), bf16[16,32,1280]{2,1,0:T(8,128)(2,1)}, u32[]{:S(2)}, u32[]{:S(2)}) async-start(bf16[16,32,1280]{2,1,0:T(8,128)(2,1)} %bitcast.12), calls=%async_computation.3 | async-start | bytes 2621440 | tf_op jit(solution)/shard_map/all_to_all | solution.py:272
  123.1 26.1 %copy-start.6 = (s32[64]{0:T(128)S(1)}, s32[64]{0:T(128)}, u32[]{:S(2)}) copy-start(s32[64]{0:T(128)} %compare_select_fusion.5.labels_ref) | copy-start | bytes 772
  123.1 31.0 %copy-start.4 = (f32[512,1280]{1,0:T(8,128)S(1)}, f32[512,1280]{1,0:T(8,128)}, u32[]{:S(2)}) copy-start(f32[512,1280]{1,0:T(8,128)} %get-tuple-element.337.base_ref) | copy-start | bytes 7864324
  143.1 1.4 collective-permute-start.20
  145.2 4.9 %collective-permute-start.23 = (f32[16,128]{1,0:T(8,128)S(1)}, f32[16,128]{1,0:T(8,128)S(1)}, u32[]{:S(2)}, u32[]{:S(2)}) collective-permute-start(f32[16,128]{1,0:T(8,128)S(1)} %add.198), channel_id=1, source_target_pairs={{0,6},{1,7},{2,4},{3,5},{4,2},{5,3},{6,0},{7,1},{8,14},{9,15},{10,... | collective-permute-start | bytes 24584 | tf_op jit(solution)/shard_map/ppermute | solution.py:326
  147.8 5.2 %collective-permute-start.22 = (f32[16,128]{1,0:T(8,128)S(1)}, f32[16,128]{1,0:T(8,128)S(1)}, u32[]{:S(2)}, u32[]{:S(2)}) collective-permute-start(f32[16,128]{1,0:T(8,128)S(1)} %add.198), channel_id=1, source_target_pairs={{0,4},{1,5},{2,6},{3,7},{4,0},{5,1},{6,2},{7,3},{8,12},{9,13},{10,... | collective-permute-start | bytes 24584 | tf_op jit(solution)/shard_map/ppermute | solution.py:326
  148.7 4.2 %collective-permute-start.21 = (f32[16,128]{1,0:T(8,128)S(1)}, f32[16,128]{1,0:T(8,128)S(1)}, u32[]{:S(2)}, u32[]{:S(2)}) collective-permute-start(f32[16,128]{1,0:T(8,128)S(1)} %add.198), channel_id=1, source_target_pairs={{0,2},{1,3},{2,0},{3,1},{4,6},{5,7},{6,4},{7,5},{8,10},{9,11},{10,... | collective-permute-start | bytes 24584 | tf_op jit(solution)/shard_map/ppermute | solution.py:326
Sparse Core Ops, SparseCore 0:
  9.1 52.1 all-gather.2
  69.0 70.1 all-gather.4

commit v3 on v2

--- a/solution.py
+++ b/solution.py
@@ -10,8 +10,7 @@
 BF16, F32, I32 = jnp.bfloat16, jnp.float32, jnp.int32
 LANES = 128
 VMEM = pl.BlockSpec(memory_space=pltpu.VMEM)
-LIMIT = 60 * 1024 * 1024
-SMALL = 24 * 1024 * 1024
+LIMIT = 24 * 1024 * 1024
 
 
 def iota(shape, dim):
@@ -62,7 +61,7 @@
         ),
         in_specs=[VMEM],
         out_specs=(VMEM, VMEM),
-        compiler_params=pltpu.CompilerParams(vmem_limit_bytes=SMALL),
+        compiler_params=pltpu.CompilerParams(vmem_limit_bytes=LIMIT),
         name="plan",
     )(jnp.broadcast_to(ids[None], (8, ids.shape[0])))
 
@@ -111,60 +110,36 @@
             jax.ShapeDtypeStruct((owners * even, wide), BF16),
             jax.ShapeDtypeStruct((spare_slots, wide), BF16),
         ),
-        compiler_params=pltpu.CompilerParams(vmem_limit_bytes=SMALL),
+        compiler_params=pltpu.CompilerParams(vmem_limit_bytes=LIMIT),
         name="route",
     )(at, info, gathered)
 
 
-def low_kernel(rank, labels_ref, rows_ref, extra_ref, down_ref, low_ref, local_ref):
-    step = pl.program_id(0)
-    some = down_ref.shape[0] // rank
-    local = lane_as_row(extra_ref[...], 1)
-    wide = rows_by_rows(down_ref[...], rows_ref[...])
+def low_kernel(rank, labels_ref, rows_ref, down_ref, low_ref):
+    features = rows_ref.shape[1] - LANES
+    local = lane_as_row(rows_ref[:, features:], 1)
+    wide = rows_by_rows(down_ref[:, :features], rows_ref[:, :features])
     total = jnp.zeros(low_ref.shape, F32)
-    for i in range(some):
-        label = labels_ref[step * some + i]
-        total += jnp.where(local[0:1] == label, wide[i * rank : (i + 1) * rank], 0.0)
-
-    @pl.when(step == 0)
-    def _():
-        local_ref[...] = local
-        low_ref[...] = total
-
-    @pl.when(step != 0)
-    def _():
-        low_ref[...] += total
-
-
-def low_part(labels, rows, down, rank, limit):
+    for i in range(down_ref.shape[0] // rank):
+        total += jnp.where(local[0:1] == labels_ref[i], wide[i * rank : (i + 1) * rank], 0.0)
+    low_ref[...] = total
+
+
+def low_part(labels, rows, down, rank):
     count, wide = rows.shape
-    features = wide - LANES
-    steps = 4
     return pl.pallas_call(
         functools.partial(low_kernel, rank),
-        grid=(steps,),
-        in_specs=[
-            pl.BlockSpec(memory_space=pltpu.SMEM),
-            pl.BlockSpec((count, features), lambda i: (0, 0)),
-            pl.BlockSpec((count, LANES), lambda i: (0, features // LANES)),
-            pl.BlockSpec((down.shape[0] // steps, features), lambda i: (i, 0)),
-        ],
-        out_specs=(
-            pl.BlockSpec((rank, count), lambda i: (0, 0)),
-            pl.BlockSpec((8, count), lambda i: (0, 0)),
-        ),
-        out_shape=(
-            jax.ShapeDtypeStruct((rank, count), F32),
-            jax.ShapeDtypeStruct((8, count), I32),
-        ),
-        compiler_params=pltpu.CompilerParams(vmem_limit_bytes=limit),
+        out_shape=jax.ShapeDtypeStruct((rank, count), F32),
+        in_specs=[pl.BlockSpec(memory_space=pltpu.SMEM), VMEM, VMEM],
+        out_specs=VMEM,
+        compiler_params=pltpu.CompilerParams(vmem_limit_bytes=LIMIT),
         cost_estimate=pl.CostEstimate(
-            flops=2 * count * down.shape[0] * features,
-            bytes_accessed=2 * features * (count + down.shape[0]),
+            flops=2 * count * down.shape[0] * wide,
+            bytes_accessed=2 * wide * (count + down.shape[0]),
             transcendentals=0,
         ),
         name="low",
-    )(labels, rows, rows, down)
+    )(labels, rows, down)
 
 
 def spread(low, local, labels):
@@ -174,32 +149,26 @@
     return jnp.where(local == labels, values, 0.0).astype(BF16)
 
 
-def delta_kernel(low_ref, extra_ref, up_ref, out_ref, wide_ref):
-    rank, places = low_ref.shape[0], up_ref.shape[0]
-
-    @pl.when(pl.program_id(0) == 0)
-    def _():
-        local = extra_ref[:, 1:2].astype(F32).astype(I32)
-        wide_ref[...] = spread(low_ref[...], local, iota((1, places), 1) // rank)
-
-    out_ref[...] = (2.0 * jnp.dot(wide_ref[...], up_ref[...], preferred_element_type=F32)).astype(BF16)
-
-
-def delta_of(low, rows, up, tile):
-    count, wide = rows.shape
-    places, columns = up.shape
+def row_locals(rows_ref):
+    lane = rows_ref.shape[1] - LANES + 1
+    return rows_ref[:, lane : lane + 1].astype(F32).astype(I32)
+
+
+def delta_kernel(low_ref, rows_ref, up_ref, out_ref):
+    places = up_ref.shape[0]
+    labels = iota((1, places), 1) // low_ref.shape[0]
+    wide = spread(low_ref[...].astype(BF16), row_locals(rows_ref), labels)
+    out_ref[...] = (2.0 * jnp.dot(wide, up_ref[...], preferred_element_type=F32)).astype(BF16)
+
+
+def delta_of(low, rows, up):
+    count, columns = rows.shape[0], up.shape[1]
     return pl.pallas_call(
         delta_kernel,
-        grid=(columns // tile,),
-        in_specs=[
-            pl.BlockSpec(low.shape, lambda i: (0, 0)),
-            pl.BlockSpec((count, LANES), lambda i: (0, wide // LANES - 1)),
-            pl.BlockSpec((places, tile), lambda i: (0, i)),
-        ],
-        out_specs=pl.BlockSpec((count, tile), lambda i: (0, i)),
         out_shape=jax.ShapeDtypeStruct((count, columns), BF16),
-        scratch_shapes=[pltpu.VMEM((count, places), BF16)],
-        compiler_params=pltpu.CompilerParams(vmem_limit_bytes=SMALL),
+        in_specs=[VMEM] * 3,
+        out_specs=VMEM,
+        compiler_params=pltpu.CompilerParams(vmem_limit_bytes=LIMIT),
         cost_estimate=pl.CostEstimate(
             flops=2 * count * up.size, bytes_accessed=2 * (up.size + count * columns), transcendentals=0
         ),
@@ -207,65 +176,51 @@
     )(low, rows, up)
 
 
-def finish_kernel(
-    even,
-    full_ref,
-    labels_ref,
-    tall_ref,
-    low_ref,
-    extra_ref,
-    base_ref,
-    back_ref,
-    up_ref,
-    out_ref,
-    wide_ref,
-    main_ref,
-    rest_ref,
-):
-    @pl.when(pl.program_id(0) == 0)
-    def _():
-        owner, place = tall_ref[:, 0:1], tall_ref[:, 2:3]
-        target = jnp.where(place < even, owner * even + place, -1)
-        main_ref[...] = (iota(main_ref.shape, 1) == target).astype(BF16)
-        spare = jnp.where((owner == full_ref[0]) & (place >= even), place - even, -1)
-        rest_ref[...] = (iota(rest_ref.shape, 1) == spare).astype(BF16)
-        local = extra_ref[:, 1:2].astype(F32).astype(I32)
-        wide_ref[...] = spread(low_ref[...], local, labels_ref[0:1])
-
-    delta = (2.0 * jnp.dot(wide_ref[...], up_ref[...], preferred_element_type=F32)).astype(BF16)
-    total = base_ref[...] + jnp.dot(main_ref[...], back_ref[...], preferred_element_type=F32)
-    total += jnp.dot(rest_ref[...], delta, preferred_element_type=F32)
-    out_ref[...] = total.astype(BF16)
-
-
-def finish(full, labels, tall, low, rows, base, back, weights, even, tile):
-    group, columns = base.shape
-    skip = (weights.shape[1] - columns) // tile
-    whole = lambda a: pl.BlockSpec(a.shape, lambda i: (0, 0))
-    cut = lambda a: pl.BlockSpec((a.shape[0], tile), lambda i: (0, i))
+def add_kernel(even, tall_ref, base_ref, back_ref, out_ref):
+    owner, place = tall_ref[:, 0:1], tall_ref[:, 2:3]
+    target = jnp.where(place < even, owner * even + place, -1)
+    chosen = (iota((tall_ref.shape[0], back_ref.shape[0]), 1) == target).astype(BF16)
+    out_ref[...] = base_ref[...] + jnp.dot(chosen, back_ref[...], preferred_element_type=F32)
+
+
+def add_back(tall, base, back, even):
+    return pl.pallas_call(
+        functools.partial(add_kernel, even),
+        out_shape=jax.ShapeDtypeStruct(base.shape, F32),
+        in_specs=[VMEM] * 3,
+        out_specs=VMEM,
+        compiler_params=pltpu.CompilerParams(vmem_limit_bytes=LIMIT),
+        cost_estimate=pl.CostEstimate(
+            flops=2 * back.size * base.shape[0], bytes_accessed=8 * base.size + 2 * back.size, transcendentals=0
+        ),
+        name="add_back",
+    )(tall, base, back)
+
+
+def finish_kernel(even, full_ref, labels_ref, tall_ref, low_ref, rows_ref, base_ref, weights_ref, out_ref):
+    group, columns = base_ref.shape
+    owner, place = tall_ref[:, 0:1], tall_ref[:, 2:3]
+    spare = jnp.where((owner == full_ref[0]) & (place >= even), place - even, -1)
+    chosen = (iota((group, rows_ref.shape[0]), 1) == spare).astype(BF16)
+    wide = spread(low_ref[...].astype(BF16), row_locals(rows_ref), labels_ref[0:1])
+    up = weights_ref[:, weights_ref.shape[1] - columns :]
+    delta = (2.0 * jnp.dot(wide, up, preferred_element_type=F32)).astype(BF16)
+    added = jnp.dot(chosen, delta, preferred_element_type=F32)
+    out_ref[...] = (base_ref[...] + added).astype(BF16)
+
+
+def finish(full, labels, tall, low, rows, base, weights, even):
     return pl.pallas_call(
         functools.partial(finish_kernel, even),
-        grid=(columns // tile,),
-        in_specs=[
-            pl.BlockSpec(memory_space=pltpu.SMEM),
-            whole(labels),
-            whole(tall),
-            whole(low),
-            pl.BlockSpec((rows.shape[0], LANES), lambda i: (0, rows.shape[1] // LANES - 1)),
-            cut(base),
-            cut(back),
-            pl.BlockSpec((weights.shape[0], tile), lambda i: (0, i + skip)),
-        ],
-        out_specs=pl.BlockSpec((group, tile), lambda i: (0, i)),
-        out_shape=jax.ShapeDtypeStruct((group, columns), BF16),
-        scratch_shapes=[
-            pltpu.VMEM((low.shape[1], weights.shape[0]), BF16),
-            pltpu.VMEM((group, back.shape[0]), BF16),
-            pltpu.VMEM((group, low.shape[1]), BF16),
-        ],
-        compiler_params=pltpu.CompilerParams(vmem_limit_bytes=LIMIT),
+        out_shape=jax.ShapeDtypeStruct(base.shape, BF16),
+        in_specs=[pl.BlockSpec(memory_space=pltpu.SMEM)] + [VMEM] * 6,
+        out_specs=VMEM,
+        compiler_params=pltpu.CompilerParams(vmem_limit_bytes=LIMIT),
+        cost_estimate=pl.CostEstimate(
+            flops=4 * weights.size * rows.shape[0], bytes_accessed=6 * base.size, transcendentals=0
+        ),
         name="finish",
-    )(full, labels, tall, low, rows, base, back, weights)
+    )(full, labels, tall, low, rows, base, weights)
 
 
 def exchange(block, axis):
@@ -301,9 +256,12 @@
     return [send_ring(matrix[:half], 0), send_ring(matrix[half:], 1)]
 
 
-def scatter_end(started, root):
+def away_from(root):
     me = lax.axis_index("adapter").astype(I32)
-    away = ((me // SIDE - root // SIDE) % SIDE, (me % SIDE - root % SIDE) % SIDE)
+    return (me // SIDE - root // SIDE) % SIDE, (me % SIDE - root % SIDE) % SIDE
+
+
+def scatter_end(started, away):
     parts = []
     for first, got in enumerate(started):
         second = 1 - first
@@ -326,10 +284,11 @@
     return lax.ppermute(block, "tensor", [(i, i ^ bit) for i in range(members)])
 
 
-def total_over_tensor(part):
+def total_over_tensor(part, beside=None):
     part = part + swapped(part, 1)
     others = [swapped(part, bit) for bit in (2, 4, 6)]
-    return (part + others[0]) + (others[1] + others[2])
+    others, beside = lax.optimization_barrier((others, beside))
+    return (part + others[0]) + (others[1] + others[2]), beside
 
 
 def per_device(
@@ -348,14 +307,15 @@
     wide = features + LANES
 
     order = jnp.arange(held, dtype=I32)
+    started = scatter_start(jnp.concatenate([down, up], axis=1))
+
     gathered = lax.all_gather(tokens, "tensor", axis=0, tiled=True)
-    started = scatter_start(jnp.concatenate([down, up], axis=1))
     ids = lax.all_gather(token_adapter_index, "tensor", axis=0, tiled=True)
-    started, ids = lax.optimization_barrier((started, ids))
     info, tall = plan(ids, owners, held, even)
 
     named = info[3, 0]
-    piece = scatter_end(started, named)
+    started, away = lax.optimization_barrier((started, away_from(named)))
+    piece = scatter_end(started, away)
     weights = lax.all_gather(piece, "adapter", axis=0, tiled=True)
     labels = scattered_order(named, held)
 
@@ -373,11 +333,11 @@
     rows, base = lax.optimization_barrier((rows, base))
 
     rows = rows.reshape(owners * even, wide)
-    part, _ = low_part(order, rows, down, rank, SMALL)
-    low = total_over_tensor(part).astype(BF16)
-    delta = delta_of(low, rows, up, 256)
-    rest_rows, delta, full, turns, labels = lax.optimization_barrier(
-        (rest_rows, delta, full, turns, labels)
+    low, _ = total_over_tensor(low_part(order, rows, down, rank))
+    delta = delta_of(low, rows, up)
+    places = jnp.broadcast_to(jnp.repeat(labels, rank)[None], (8, held * rank))
+    rest_rows, delta, full, turns, labels, places = lax.optimization_barrier(
+        (rest_rows, delta, full, turns, labels, places)
     )
     back = exchange(delta.reshape(owners, even, columns), "adapter").reshape(owners * even, columns)
 
@@ -394,18 +354,17 @@
         mine = jnp.concatenate([mine, numbers], axis=1)
         moved = jnp.dot(chosen, mine, preferred_element_type=F32).astype(BF16)
         moved = exchange(moved.reshape(owners, even, wide), "adapter").reshape(owners * even, wide)
-        more_part, _ = low_part(order, moved, down, rank, SMALL)
-        more_low = total_over_tensor(more_part).astype(BF16)
-        more_delta = delta_of(more_low, moved, up, 256).reshape(owners, even, columns)
+        more_low, _ = total_over_tensor(low_part(order, moved, down, rank))
+        more_delta = delta_of(more_low, moved, up).reshape(owners, even, columns)
         more_back = exchange(more_delta, "adapter").reshape(owners * even, columns)
         return turn + 1, total + jnp.dot(chosen.T, more_back, preferred_element_type=F32)
 
     _, base = lax.while_loop(lambda carry: carry[0] < turns, more, (jnp.int32(1), base))
 
-    rest_part, _ = low_part(labels, rest_rows, weights, rank, LIMIT)
-    rest_low = total_over_tensor(rest_part).astype(BF16)
-    places = jnp.broadcast_to(jnp.repeat(labels, rank)[None], (8, held * rank))
-    return finish(full.reshape(1), places, tall, rest_low, rest_rows, base, back, weights, even, 256)
+    base = add_back(tall, base, back, even)
+
+    rest_low, base = total_over_tensor(low_part(labels, rest_rows, weights, rank), base)
+    return finish(full.reshape(1), places, tall, rest_low, rest_rows, base, weights, even)
 
 
 def solution(mesh):

time: 169 us -> 160 us (0.947)
  Pallas kernels: 23.2 us -> 17.6 us
  waiting for transfers between devices: 43.5 us -> 40.9 us
  other arithmetic: 11 us -> 8.86 us
    unnamed x0 -> x1, blocking collectives: none -> 9.6 us
    optimization_barrier x1 -> x0, blocking collectives: 9.6 us -> none  [per_device(): started, ids = lax.optimization_barrier((started, ids))]
    ppermute x12, waiting for transfers between devices: 21.7 us -> 15.1 us  [neighbour(): lax.ppermute(block, 'adapter', [(i, to(i)) for i in range(SIDE * SIDE)])]
    pallas_call x4 -> x5, Pallas kernels: 19.7 us -> 14 us  [the longest x1 4.75 us: delta_of(): pl.pallas_call(delta_kernel, out_shape=jax.ShapeDtypeStruct((count, colum...]
    all_gather x1, waiting for transfers between devices: 16.1 us -> 20 us  [per_device(): weights = lax.all_gather(piece, 'adapter', axis=0, tiled=True)]
    all_to_all x2, waiting for transfers between devices: 0.01 us -> 2.92 us  [exchange(): return lax.all_to_all(block, axis, split_axis=0, concat_axis=0, tiled=True)]
    ppermute x8, waiting for transfers between devices: 4.97 us -> 2.14 us  [swapped(): return lax.ppermute(block, 'tensor', [(i, i ^ bit) for i in range(members)])]
    unnamed x22 -> x18, local copies, waits for them, and re-layouts: 2.56 us -> 3.49 us
  transfers between devices with their start and end apart: 24 -> 24, of which waited for: 12 -> 10; matrix products, arithmetic and copies ran while one was open for 19% -> 19% of each run, Pallas kernels for 10% -> 10%
where the time goes in v3:
time: 160 us; the launch traced here: 159 us
  waiting for transfers between devices  40.9 us (26%)
  starting transfers between devices  39.2 us (25%)
  between operations  20 us (12%)
  matrix products  18.2 us (11%)
  Pallas kernels  17.6 us (11%)
  blocking collectives  9.6 us (6%)
  other arithmetic  8.86 us (6%)
  local copies, waits for them, and re-layouts  4.82 us (3%)
    all_gather x1, waiting for transfers between devices, per_device(): weights = lax.all_gather(piece, 'adapter', axis=0, tiled=True)  20 us
    dot_general x1, matrix products, per_device(): base = jnp.dot(gathered, joined_weight_matrix, preferred_element_type=F32)  18.2 us
    ppermute x12, starting transfers between devices, neighbour(): lax.ppermute(block, 'adapter', [(i, to(i)) for i in range(SIDE * SIDE)])  17.7 us
    ppermute x12, waiting for transfers between devices, neighbour(): lax.ppermute(block, 'adapter', [(i, to(i)) for i in range(SIDE * SIDE)])  15.1 us
    all_to_all x2, starting transfers between devices, exchange(): return lax.all_to_all(block, axis, split_axis=0, concat_axis=0, tiled=True)  13.1 us
    unnamed x1, blocking collectives  9.6 us
    ppermute x8, starting transfers between devices, swapped(): return lax.ppermute(block, 'tensor', [(i, i ^ bit) for i in range(members)])  8.43 us
    pallas_call x1, Pallas kernels, delta_of(): pl.pallas_call(delta_kernel, out_shape=jax.ShapeDtypeStruct((count, colum...  4.75 us
  transfers between devices with their start and end apart: 24, of which 10 were waited for; matrix products, arithmetic and copies ran while one was open for 19% of the time, Pallas kernels for 10%

profile of v3, /device:TPU:2, one launch (start us, length us, event | category | flops | bytes accessed | tf_op | source)
XLA Modules:
  0.0 159.2 jit_solution(13390242758810473133)
XLA Ops:
  6.5 0.7 all-gather.3.cloned.1.call-update
  7.3 0.0 all-gather.5.cloned.1.call-start
  7.3 0.0 copy-start.7
  7.3 3.5 %pad_maximum_fusion = (bf16[128,2304]{1,0:T(8,128)(2,1)S(1)}, bf16[128,2304]{1,0:T(8,128)(2,1)S(1)}, bf16[128,2304]{1,0:T(8,128)(2,1)}, bf16[128,2304]{1,0:T(8,1...) fusion(bf16[1024,1280]{1,0:T(8,128)(2,1)} %bitcast.44, ...), kind=kLoop, calls=%fused_computation.50 | loop fusion | flops 9437184 | bytes 9437184 | tf_op jit(solution)/shard_map/concatenate | solution.py:310
  10.8 4.1 %collective-permute-start.13 = (bf16[128,2304]{1,0:T(8,128)(2,1)S(1)}, bf16[128,2304]{1,0:T(8,128)(2,1)S(1)}, u32[]{:S(2)}, u32[]{:S(2)}) collective-permute-start(bf16[128,2304]{1,0:T(8,128)(2,1)S(1)} %get-tuple-element.463), channel_id=1, source_target_pairs={{0,24},{8,0},{16,8},{24,16},{32,56},{40,32},{48,40},{56,48},{64,88... | collective-permute-start | bytes 1769480 | tf_op jit(solution)/shard_map/ppermute | solution.py:239
  14.9 1.5 collective-permute-start.8
  16.4 1.1 collective-permute-start.9
  17.5 2.2 %collective-permute-start.10 = (bf16[128,2304]{1,0:T(8,128)(2,1)S(1)}, bf16[128,2304]{1,0:T(8,128)(2,1)}, u32[]{:S(2)}, u32[]{:S(2)}) collective-permute-start(bf16[128,2304]{1,0:T(8,128)(2,1)S(1)} %get-tuple-element.467), channel_id=1, source_target_pairs={{0,96},{8,104},{16,112},{24,120},{32,0},{40,8},{48,16},{56,24},{64... | collective-permute-start | bytes 1769480 | tf_op jit(solution)/shard_map/ppermute | solution.py:239
  19.6 7.8 %collective-permute-done.13 = bf16[128,2304]{1,0:T(8,128)(2,1)S(1)} collective-permute-done((bf16[128,2304]{1,0:T(8,128)(2,1)S(1)}, bf16[128,2304]{1,0:T(8,128)(2,1)S(1)}, u32[]{:S(2)}, u32[]{:S(2)}) %collective-permute-start.13) | collective-permute-done | bytes 589856 | tf_op jit(solution)/shard_map/ppermute | solution.py:239
  27.5 2.3 %collective-permute-start.12 = (bf16[128,2304]{1,0:T(8,128)(2,1)S(1)}, bf16[128,2304]{1,0:T(8,128)(2,1)}, u32[]{:S(2)}, u32[]{:S(2)}) collective-permute-start(bf16[128,2304]{1,0:T(8,128)(2,1)S(1)} %get-tuple-element.470), channel_id=1, source_target_pairs={{0,16},{8,24},{16,0},{24,8},{32,48},{40,56},{48,32},{56,40},{64,80... | collective-permute-start | bytes 1769480 | tf_op jit(solution)/shard_map/ppermute | solution.py:239
  29.8 0.6 dynamic-slice
  31.0 0.2 dynamic-update-slice
  31.3 9.6 %all-reduce.1 = s32[512]{0:T(512)S(1)} all-reduce(s32[512]{0:T(512)S(1)} %dynamic-update-slice), channel_id=1, replica_groups=mesh['adapter'=16,'tensor'=8] {'tensor'}, use_global_device_ids=true, to_apply=%add.1 | all-reduce | flops 512 | bytes 4096
  40.9 0.3 plan.1
  41.2 0.5 slice.94
  44.3 0.1 broadcast_in_dim.11
  44.4 0.1 broadcast_in_dim.22
  44.5 0.2 copy.14
  44.7 0.0 collective-permute-done.9
  44.7 0.0 collective-permute-done.10
  44.7 2.8 %collective-permute-done.11 = bf16[128,2304]{1,0:T(8,128)(2,1)} collective-permute-done((bf16[128,2304]{1,0:T(8,128)(2,1)S(1)}, bf16[128,2304]{1,0:T(8,128)(2,1)}, u32[]{:S(2)}, u32[]{:S(2)}) %collective-permute-start.11) | collective-permute-done | bytes 589856 | tf_op jit(solution)/shard_map/ppermute | solution.py:239
  47.5 0.0 collective-permute-done.12
  47.5 1.2 select_select_fusion.1
  48.8 0.1 collective-permute-start.16
  48.9 1.6 collective-permute-start.15
  50.5 0.5 collective-permute-start.14
  50.9 1.3 select_select_fusion
  52.2 1.7 %collective-permute-start.19 = (bf16[32,2304]{1,0:T(8,128)(2,1)S(1)}, bf16[32,2304]{1,0:T(8,128)(2,1)S(1)}, u32[]{:S(2)}, u32[]{:S(2)}) collective-permute-start(bf16[32,2304]{1,0:T(8,128)(2,1)S(1)} %get-tuple-element.474), channel_id=1, source_target_pairs={{0,96},{8,104},{16,112},{24,120},{32,0},{40,8},{48,16},{56,24},{64... | collective-permute-start | bytes 442376 | tf_op jit(solution)/shard_map/ppermute | solution.py:239
  54.0 0.8 collective-permute-start.18
  54.8 1.8 %collective-permute-start.17 = (bf16[32,2304]{1,0:T(8,128)(2,1)S(1)}, bf16[32,2304]{1,0:T(8,128)(2,1)S(1)}, u32[]{:S(2)}, u32[]{:S(2)}) collective-permute-start(bf16[32,2304]{1,0:T(8,128)(2,1)S(1)} %get-tuple-element.476), channel_id=1, source_target_pairs={{0,32},{8,40},{16,48},{24,56},{32,64},{40,72},{48,80},{56,88},{64,... | collective-permute-start | bytes 442376 | tf_op jit(solution)/shard_map/ppermute | solution.py:239
  56.6 1.0 collective-permute-done.14
  57.7 0.6 collective-permute-done.19
  58.3 2.3 %collective-permute-done.18 = bf16[32,2304]{1,0:T(8,128)(2,1)S(1)} collective-permute-done((bf16[32,2304]{1,0:T(8,128)(2,1)S(1)}, bf16[32,2304]{1,0:T(8,128)(2,1)S(1)}, u32[]{:S(2)}, u32[]{:S(2)}) %collective-permute-start.18) | collective-permute-done | bytes 147488 | tf_op jit(solution)/shard_map/ppermute | solution.py:239
  60.6 0.5 collective-permute-done.17
  61.1 0.7 pad_maximum_fusion.1
  61.9 0.0 all-gather.5.cloned.1.call-update
  61.9 0.0 all-gather.3.cloned.1.call-done.rows_ref
  61.9 3.2 %route.1 = (bf16[512,1152]{1,0:T(8,128)(2,1)}, bf16[128,1152]{1,0:T(8,128)(2,1)S(1)}) custom-call(s32[1]{0:T(128)} %bitcast.at_ref, s32[8,512]{1,0:T(8,128)S(1)} %get-tuple-element.325.info_ref, bf16[512,8192]{1,0:T(8,128)(2,1)} %all-gather.3.cloned.1.call-done.rows_ref), custom_call_target="tpu_custom_call" | custom-call | tf_op jit(solution)/shard_map/route/pallas_call | solution.py:95
  65.1 7.1 %all-to-all-start.2 = ((bf16[16,32,1152]{2,1,0:T(8,128)(2,1)}), bf16[16,32,1152]{2,1,0:T(8,128)(2,1)S(1)}, u32[]{:S(2)}, u32[]{:S(2)}) async-start(bf16[16,32,1152]{2,1,0:T(8,128)(2,1)} %bitcast.2), calls=%async_computation.2 | async-start | bytes 2359296 | tf_op jit(solution)/shard_map/all_to_all | solution.py:227
  72.2 18.2 %fusion.31 = f32[512,1280]{1,0:T(8,128)} fusion(bf16[512,8192]{1,0:T(8,128)(2,1)} %all-gather.3.cloned.1.call-done.rows_ref, bf16[8192,1280]{1,0:T(8,128)(2,1)} %param.9), kind=kOutput, calls=%fused_computation.87 | convolution fusion | flops 10737418240 | bytes 31981568 | tf_op jit(solution)/shard_map/dot_general | solution.py:332
  90.4 2.9 %all-to-all-done.2 = bf16[16,32,1152]{2,1,0:T(8,128)(2,1)S(1)} async-done(((bf16[16,32,1152]{2,1,0:T(8,128)(2,1)}), bf16[16,32,1152]{2,1,0:T(8,128)(2,1)S(1)}, u32[]{:S(2)}, u32[]{:S(2)}) %all-to-all-start.2) | async-done | bytes 1179680 | tf_op jit(solution)/shard_map/all_to_all | solution.py:227
  93.3 0.1 slice.114
  93.4 0.1 copy.16
  93.5 2.9 %low.8 = f32[16,512]{1,0:T(8,128)S(1)} custom-call(s32[64]{0:T(128)S(1)} %iota.30.labels_ref, bf16[512,1152]{1,0:T(8,128)(2,1)S(1)} %bitcast.41, bf16[1024,1024]{1,0:T(8,128)(2,1)} %bitcast.49), custom_call_target="tpu_custom_call" | custom-call | flops 1207959552 | bytes 3538944 | tf_op jit(solution)/shard_map/low/pallas_call | solution.py:130
  96.4 0.1 collective-permute-start.4
  96.5 0.7 slice_reduce_fusion
  97.2 0.5 slice.91
  97.8 0.1 collective-permute-start.7
  97.8 2.7 %collective-permute-start.6 = (f32[16,512]{1,0:T(8,128)S(1)}, f32[16,512]{1,0:T(8,128)S(1)}, u32[]{:S(2)}, u32[]{:S(2)}) collective-permute-start(f32[16,512]{1,0:T(8,128)S(1)} %add.175), channel_id=1, source_target_pairs={{0,4},{1,5},{2,6},{3,7},{4,0},{5,1},{6,2},{7,3},{8,12},{9,13},{10,... | collective-permute-start | bytes 98312 | tf_op jit(solution)/shard_map/ppermute | solution.py:284
  100.6 1.4 collective-permute-start.5
  101.9 1.3 compare_reduce_fusion.1
  106.5 4.7 %delta.7 = bf16[512,1280]{1,0:T(8,128)(2,1)} custom-call(f32[16,512]{1,0:T(8,128)S(1)} %add_add_fusion.1.low_ref, bf16[512,1152]{1,0:T(8,128)(2,1)S(1)} %bitcast.42, bf16[1024,1280]{1,0:T(8,128)(2,1)} %bitcast.45), custom_call_target="tpu_custom_call" | custom-call | flops 1342177280 | bytes 3932160 | tf_op jit(solution)/shard_map/delta/pallas_call | solution.py:166
  111.2 6.0 %all-to-all-start.3 = ((bf16[16,32,1280]{2,1,0:T(8,128)(2,1)}), bf16[16,32,1280]{2,1,0:T(8,128)(2,1)S(1)}, u32[]{:S(2)}, u32[]{:S(2)}) async-start(bf16[16,32,1280]{2,1,0:T(8,128)(2,1)} %bitcast.12), calls=%async_computation.3 | async-start | bytes 2621440 | tf_op jit(solution)/shard_map/all_to_all | solution.py:227
  117.2 20.0 %all-gather.5.cloned.1.call-done.down_ref.weights_ref = bf16[1024,2304]{1,0:T(8,128)(2,1)} async-done(((bf16[64,2304]{1,0:T(8,128)(2,1)}), bf16[1024,2304]{1,0:T(8,128)(2,1)}) %all-gather.5.cloned.1.call-update) | async-done | bytes 4718608 | tf_op jit(solution)/shard_map/all_gather | solution.py:319
  137.2 2.3 %copy-done = bf16[1024,2304]{1,0:T(8,128)(2,1)S(1)} copy-done((bf16[1024,2304]{1,0:T(8,128)(2,1)S(1)}, bf16[1024,2304]{1,0:T(8,128)(2,1)}, u32[]{:S(2)}) %copy-start) | copy-done | bytes 4718616
  139.6 1.3 low.9
  140.8 0.1 collective-permute-start.20
  140.9 1.2 collective-permute-done.20
  142.1 2.9 %collective-permute-start.23 = (f32[16,128]{1,0:T(8,128)S(1)}, f32[16,128]{1,0:T(8,128)S(1)}, u32[]{:S(2)}, u32[]{:S(2)}) collective-permute-start(f32[16,128]{1,0:T(8,128)S(1)} %add.193), channel_id=1, source_target_pairs={{0,6},{1,7},{2,4},{3,5},{4,2},{5,3},{6,0},{7,1},{8,14},{9,15},{10,... | collective-permute-start | bytes 24584 | tf_op jit(solution)/shard_map/ppermute | solution.py:284
  145.0 0.8 collective-permute-start.22
  145.8 0.3 collective-permute-start.21
  146.2 3.0 %add_back.1.base_ref = f32[512,1280]{1,0:T(8,128)S(1)} custom-call(s32[512,128]{1,0:T(8,128)S(1)} %get-tuple-element.334.tall_ref, f32[512,1280]{1,0:T(8,128)} %get-tuple-element.349.base_ref, bf16[512,1280]{1,0:T(8,128)(2,1)S(1)} %bitcast.40), custom_call_target="tpu_custom_call" | custom-call | flops 671088640 | bytes 6553600 | tf_op jit(solution)/shard_map/add_back/pallas_call | solution.py:187
  149.2 1.0 collective-permute-done.22
  150.2 2.1 %finish.1 = bf16[512,1280]{1,0:T(8,128)(2,1)} custom-call(s32[1]{0:T(128)} %bitcast.8.full_ref, s32[8,1024]{1,0:T(8,128)S(1)} %broadcast_in_dim.23.labels_ref, s32[512,128]{1,0:T(8,128)S(1)} %get-tuple-element.334.tall_ref, f32[16,128]{1,0:T(8,128)S(1)} %add_add_fusion.2.low_ref, bf16[128,1152]{1,0:T(8,128)(2,1)S(1)} %get-tuple-element.336.rows_ref, ...), custom_call_target="tpu_custom_call" | custom-call | flops 1207959552 | bytes 3932160 | tf_op jit(solution)/shard_map/finish/pallas_call | solution.py:213
  (40 shorter events, 0.3 us)
Async XLA Ops:
  6.5 55.4 %all-gather.3.cloned.1.call-start = ((), (), s32[]{:S(2)}) async-start(), calls=%async_computation.4 | async-start | bytes 9437184 | tf_op jit(solution)/shard_map/all_gather | solution.py:312
  7.3 130.0 %all-gather.5.cloned.1.call-start = ((), (), s32[]{:S(2)}) async-start(), calls=%async_computation.5 | async-start | bytes 5013504 | tf_op jit(solution)/shard_map/all_gather | solution.py:319
  7.3 22.5 %copy-start.7 = (u32[128]{0:T(128)S(1)}, u32[128]{0:T(128)}, u32[]{:S(2)}) copy-start(u32[128]{0:T(128)} %constant.217) | copy-start | bytes 1540
  7.3 23.7 %copy-start.6 = (s32[64]{0:T(128)S(1)}, s32[64]{0:T(128)}, u32[]{:S(2)}) copy-start(s32[64]{0:T(128)} %param.8) | copy-start | bytes 772
  10.8 16.7 %collective-permute-start.13 = (bf16[128,2304]{1,0:T(8,128)(2,1)S(1)}, bf16[128,2304]{1,0:T(8,128)(2,1)S(1)}, u32[]{:S(2)}, u32[]{:S(2)}) collective-permute-start(bf16[128,2304]{1,0:T(8,128)(2,1)S(1)} %get-tuple-element.463), channel_id=1, source_target_pairs={{0,24},{8,0},{16,8},{24,16},{32,56},{40,32},{48,40},{56,48},{64,88... | collective-permute-start | bytes 1769480 | tf_op jit(solution)/shard_map/ppermute | solution.py:239
  14.9 29.8 %collective-permute-start.8 = (bf16[128,2304]{1,0:T(8,128)(2,1)}, bf16[128,2304]{1,0:T(8,128)(2,1)}, u32[]{:S(2)}, u32[]{:S(2)}) collective-permute-start(bf16[128,2304]{1,0:T(8,128)(2,1)} %get-tuple-element.465), channel_id=1, source_target_pairs={{0,32},{8,40},{16,48},{24,56},{32,64},{40,72},{48,80},{56,88},{64,... | collective-permute-start | bytes 1769480 | tf_op jit(solution)/shard_map/ppermute | solution.py:239
  16.4 28.3 %collective-permute-start.9 = (bf16[128,2304]{1,0:T(8,128)(2,1)}, bf16[128,2304]{1,0:T(8,128)(2,1)}, u32[]{:S(2)}, u32[]{:S(2)}) collective-permute-start(bf16[128,2304]{1,0:T(8,128)(2,1)} %get-tuple-element.466), channel_id=1, source_target_pairs={{0,64},{8,72},{16,80},{24,88},{32,96},{40,104},{48,112},{56,120},{... | collective-permute-start | bytes 1769480 | tf_op jit(solution)/shard_map/ppermute | solution.py:239
  17.5 27.2 %collective-permute-start.10 = (bf16[128,2304]{1,0:T(8,128)(2,1)S(1)}, bf16[128,2304]{1,0:T(8,128)(2,1)}, u32[]{:S(2)}, u32[]{:S(2)}) collective-permute-start(bf16[128,2304]{1,0:T(8,128)(2,1)S(1)} %get-tuple-element.467), channel_id=1, source_target_pairs={{0,96},{8,104},{16,112},{24,120},{32,0},{40,8},{48,16},{56,24},{64... | collective-permute-start | bytes 1769480 | tf_op jit(solution)/shard_map/ppermute | solution.py:239
  19.6 27.9 %collective-permute-start.11 = (bf16[128,2304]{1,0:T(8,128)(2,1)S(1)}, bf16[128,2304]{1,0:T(8,128)(2,1)}, u32[]{:S(2)}, u32[]{:S(2)}) collective-permute-start(bf16[128,2304]{1,0:T(8,128)(2,1)S(1)} %get-tuple-element.469), channel_id=1, source_target_pairs={{0,8},{8,16},{16,24},{24,0},{32,40},{40,48},{48,56},{56,32},{64,72... | collective-permute-start | bytes 1769480 | tf_op jit(solution)/shard_map/ppermute | solution.py:239
  27.5 2.3 %copy-start.4 = (bf16[128,2304]{1,0:T(8,128)(2,1)}, bf16[128,2304]{1,0:T(8,128)(2,1)S(1)}, u32[]{:S(2)}) copy-start(bf16[128,2304]{1,0:T(8,128)(2,1)S(1)} %collective-permute-done.13) | copy-start | bytes 1769476
  27.5 20.1 %collective-permute-start.12 = (bf16[128,2304]{1,0:T(8,128)(2,1)S(1)}, bf16[128,2304]{1,0:T(8,128)(2,1)}, u32[]{:S(2)}, u32[]{:S(2)}) collective-permute-start(bf16[128,2304]{1,0:T(8,128)(2,1)S(1)} %get-tuple-element.470), channel_id=1, source_target_pairs={{0,16},{8,24},{16,0},{24,8},{32,48},{40,56},{48,32},{56,40},{64,80... | collective-permute-start | bytes 1769480 | tf_op jit(solution)/shard_map/ppermute | solution.py:239
  44.7 6.2 %copy-start.5 = (bf16[128,2304]{1,0:T(8,128)(2,1)S(1)}, bf16[128,2304]{1,0:T(8,128)(2,1)}, u32[]{:S(2)}) copy-start(bf16[128,2304]{1,0:T(8,128)(2,1)} %copy-done.4) | copy-start | bytes 1769476
  48.8 6.0 %collective-permute-start.16 = (bf16[32,2304]{1,0:T(8,128)(2,1)S(1)}, bf16[32,2304]{1,0:T(8,128)(2,1)S(1)}, u32[]{:S(2)}, u32[]{:S(2)}) collective-permute-start(bf16[32,2304]{1,0:T(8,128)(2,1)S(1)} %get-tuple-element.471), channel_id=1, source_target_pairs={{0,24},{8,0},{16,8},{24,16},{32,56},{40,32},{48,40},{56,48},{64,88... | collective-permute-start | bytes 442376 | tf_op jit(solution)/shard_map/ppermute | solution.py:239
  48.9 7.7 %collective-permute-start.15 = (bf16[32,2304]{1,0:T(8,128)(2,1)S(1)}, bf16[32,2304]{1,0:T(8,128)(2,1)S(1)}, u32[]{:S(2)}, u32[]{:S(2)}) collective-permute-start(bf16[32,2304]{1,0:T(8,128)(2,1)S(1)} %get-tuple-element.472), channel_id=1, source_target_pairs={{0,16},{8,24},{16,0},{24,8},{32,48},{40,56},{48,32},{56,40},{64,80... | collective-permute-start | bytes 442376 | tf_op jit(solution)/shard_map/ppermute | solution.py:239
  50.5 7.2 %collective-permute-start.14 = (bf16[32,2304]{1,0:T(8,128)(2,1)S(1)}, bf16[32,2304]{1,0:T(8,128)(2,1)S(1)}, u32[]{:S(2)}, u32[]{:S(2)}) collective-permute-start(bf16[32,2304]{1,0:T(8,128)(2,1)S(1)} %get-tuple-element.473), channel_id=1, source_target_pairs={{0,8},{8,16},{16,24},{24,0},{32,40},{40,48},{48,56},{56,32},{64,72... | collective-permute-start | bytes 442376 | tf_op jit(solution)/shard_map/ppermute | solution.py:239
  52.2 6.1 %collective-permute-start.19 = (bf16[32,2304]{1,0:T(8,128)(2,1)S(1)}, bf16[32,2304]{1,0:T(8,128)(2,1)S(1)}, u32[]{:S(2)}, u32[]{:S(2)}) collective-permute-start(bf16[32,2304]{1,0:T(8,128)(2,1)S(1)} %get-tuple-element.474), channel_id=1, source_target_pairs={{0,96},{8,104},{16,112},{24,120},{32,0},{40,8},{48,16},{56,24},{64... | collective-permute-start | bytes 442376 | tf_op jit(solution)/shard_map/ppermute | solution.py:239
  54.0 6.6 %collective-permute-start.18 = (bf16[32,2304]{1,0:T(8,128)(2,1)S(1)}, bf16[32,2304]{1,0:T(8,128)(2,1)S(1)}, u32[]{:S(2)}, u32[]{:S(2)}) collective-permute-start(bf16[32,2304]{1,0:T(8,128)(2,1)S(1)} %get-tuple-element.475), channel_id=1, source_target_pairs={{0,64},{8,72},{16,80},{24,88},{32,96},{40,104},{48,112},{56,120},{... | collective-permute-start | bytes 442376 | tf_op jit(solution)/shard_map/ppermute | solution.py:239
  54.8 6.3 %collective-permute-start.17 = (bf16[32,2304]{1,0:T(8,128)(2,1)S(1)}, bf16[32,2304]{1,0:T(8,128)(2,1)S(1)}, u32[]{:S(2)}, u32[]{:S(2)}) collective-permute-start(bf16[32,2304]{1,0:T(8,128)(2,1)S(1)} %get-tuple-element.476), channel_id=1, source_target_pairs={{0,32},{8,40},{16,48},{24,56},{32,64},{40,72},{48,80},{56,88},{64,... | collective-permute-start | bytes 442376 | tf_op jit(solution)/shard_map/ppermute | solution.py:239
  65.1 28.2 %all-to-all-start.2 = ((bf16[16,32,1152]{2,1,0:T(8,128)(2,1)}), bf16[16,32,1152]{2,1,0:T(8,128)(2,1)S(1)}, u32[]{:S(2)}, u32[]{:S(2)}) async-start(bf16[16,32,1152]{2,1,0:T(8,128)(2,1)} %bitcast.2), calls=%async_computation.2 | async-start | bytes 2359296 | tf_op jit(solution)/shard_map/all_to_all | solution.py:227
  96.4 1.3 collective-permute-start.4
  97.8 8.7 %collective-permute-start.7 = (f32[16,512]{1,0:T(8,128)S(1)}, f32[16,512]{1,0:T(8,128)S(1)}, u32[]{:S(2)}, u32[]{:S(2)}) collective-permute-start(f32[16,512]{1,0:T(8,128)S(1)} %add.175), channel_id=1, source_target_pairs={{0,6},{1,7},{2,4},{3,5},{4,2},{5,3},{6,0},{7,1},{8,14},{9,15},{10,... | collective-permute-start | bytes 98312 | tf_op jit(solution)/shard_map/ppermute | solution.py:284
  97.8 8.6 %collective-permute-start.6 = (f32[16,512]{1,0:T(8,128)S(1)}, f32[16,512]{1,0:T(8,128)S(1)}, u32[]{:S(2)}, u32[]{:S(2)}) collective-permute-start(f32[16,512]{1,0:T(8,128)S(1)} %add.175), channel_id=1, source_target_pairs={{0,4},{1,5},{2,6},{3,7},{4,0},{5,1},{6,2},{7,3},{8,12},{9,13},{10,... | collective-permute-start | bytes 98312 | tf_op jit(solution)/shard_map/ppermute | solution.py:284
  100.6 5.9 %collective-permute-start.5 = (f32[16,512]{1,0:T(8,128)S(1)}, f32[16,512]{1,0:T(8,128)S(1)}, u32[]{:S(2)}, u32[]{:S(2)}) collective-permute-start(f32[16,512]{1,0:T(8,128)S(1)} %add.175), channel_id=1, source_target_pairs={{0,2},{1,3},{2,0},{3,1},{4,6},{5,7},{6,4},{7,5},{8,10},{9,11},{10,... | collective-permute-start | bytes 98312 | tf_op jit(solution)/shard_map/ppermute | solution.py:284
  111.2 35.0 %all-to-all-start.3 = ((bf16[16,32,1280]{2,1,0:T(8,128)(2,1)}), bf16[16,32,1280]{2,1,0:T(8,128)(2,1)S(1)}, u32[]{:S(2)}, u32[]{:S(2)}) async-start(bf16[16,32,1280]{2,1,0:T(8,128)(2,1)} %bitcast.12), calls=%async_computation.3 | async-start | bytes 2621440 | tf_op jit(solution)/shard_map/all_to_all | solution.py:227
  137.2 2.3 %copy-start = (bf16[1024,2304]{1,0:T(8,128)(2,1)S(1)}, bf16[1024,2304]{1,0:T(8,128)(2,1)}, u32[]{:S(2)}) copy-start(bf16[1024,2304]{1,0:T(8,128)(2,1)} %all-gather.5.cloned.1.call-done.down_ref.weights_ref) | copy-start | bytes 14155780
  140.8 1.3 collective-permute-start.20
  142.1 7.1 %collective-permute-start.23 = (f32[16,128]{1,0:T(8,128)S(1)}, f32[16,128]{1,0:T(8,128)S(1)}, u32[]{:S(2)}, u32[]{:S(2)}) collective-permute-start(f32[16,128]{1,0:T(8,128)S(1)} %add.193), channel_id=1, source_target_pairs={{0,6},{1,7},{2,4},{3,5},{4,2},{5,3},{6,0},{7,1},{8,14},{9,15},{10,... | collective-permute-start | bytes 24584 | tf_op jit(solution)/shard_map/ppermute | solution.py:284
  145.0 5.2 %collective-permute-start.22 = (f32[16,128]{1,0:T(8,128)S(1)}, f32[16,128]{1,0:T(8,128)S(1)}, u32[]{:S(2)}, u32[]{:S(2)}) collective-permute-start(f32[16,128]{1,0:T(8,128)S(1)} %add.193), channel_id=1, source_target_pairs={{0,4},{1,5},{2,6},{3,7},{4,0},{5,1},{6,2},{7,3},{8,12},{9,13},{10,... | collective-permute-start | bytes 24584 | tf_op jit(solution)/shard_map/ppermute | solution.py:284
  145.8 4.3 %collective-permute-start.21 = (f32[16,128]{1,0:T(8,128)S(1)}, f32[16,128]{1,0:T(8,128)S(1)}, u32[]{:S(2)}, u32[]{:S(2)}) collective-permute-start(f32[16,128]{1,0:T(8,128)S(1)} %add.193), channel_id=1, source_target_pairs={{0,2},{1,3},{2,0},{3,1},{4,6},{5,7},{6,4},{7,5},{8,10},{9,11},{10,... | collective-permute-start | bytes 24584 | tf_op jit(solution)/shard_map/ppermute | solution.py:284
  146.2 4.0 %copy-start.1 = (bf16[1024,2304]{1,0:T(8,128)(2,1)S(1)}, bf16[1024,2304]{1,0:T(8,128)(2,1)}, u32[]{:S(2)}) copy-start(bf16[1024,2304]{1,0:T(8,128)(2,1)} %all-gather.5.cloned.1.call-done.down_ref.weights_ref) | copy-start | bytes 14155780
Sparse Core Ops, SparseCore 0:
  9.1 52.1 all-gather.2
  63.5 73.7 all-gather.4

commit v4 on v3

--- a/solution.py
+++ b/solution.py
@@ -323,23 +323,24 @@
     send, rest_rows = route(here, info, gathered, features, owners, even, capacity)
     rows = exchange(send.reshape(owners, even, wide), "adapter")
 
-    said = rows[:, 0, features + 3 : features + 6].astype(I32)
+    base = jnp.dot(gathered, joined_weight_matrix, preferred_element_type=F32)
+    rows, base = lax.optimization_barrier((rows, base))
+
+    rows = rows.reshape(owners * even, wide)
+    low, _ = total_over_tensor(low_part(order, rows, down, rank))
+    delta = delta_of(low, rows, up)
+    places = jnp.broadcast_to(jnp.repeat(labels, rank)[None], (8, held * rank))
+    said = rows.reshape(owners, even, wide)[:, 0, features + 3 : features + 6]
+    rest_rows, delta, said, labels, places = lax.optimization_barrier(
+        (rest_rows, delta, said, labels, places)
+    )
+    back = exchange(delta.reshape(owners, even, columns), "adapter").reshape(owners * even, columns)
+
+    said = said.astype(I32)
     same = jnp.all(said[:, 0] == said[0, 0])
     full = jnp.where(same, said[0, 0], -1)
     largest = jnp.where(same, jnp.max(said[:, 1]), jnp.max(said[:, 2]))
     turns = (largest + even - 1) // even
-
-    base = jnp.dot(gathered, joined_weight_matrix, preferred_element_type=F32)
-    rows, base = lax.optimization_barrier((rows, base))
-
-    rows = rows.reshape(owners * even, wide)
-    low, _ = total_over_tensor(low_part(order, rows, down, rank))
-    delta = delta_of(low, rows, up)
-    places = jnp.broadcast_to(jnp.repeat(labels, rank)[None], (8, held * rank))
-    rest_rows, delta, full, turns, labels, places = lax.optimization_barrier(
-        (rest_rows, delta, full, turns, labels, places)
-    )
-    back = exchange(delta.reshape(owners, even, columns), "adapter").reshape(owners * even, columns)
 
     owner, place = info[0], info[2]
 

time: 160 us -> 159 us (level)
  waiting for transfers between devices: 40.9 us -> 31.6 us
  starting transfers between devices: 39.2 us -> 48.2 us
    all_gather x1, waiting for transfers between devices: 20 us -> 6.56 us  [per_device(): weights = lax.all_gather(piece, 'adapter', axis=0, tiled=True)]
    ppermute x8, starting transfers between devices: 8.43 us -> 15.5 us  [swapped(): return lax.ppermute(block, 'tensor', [(i, i ^ bit) for i in range(members)])]
    ppermute x8, waiting for transfers between devices: 2.14 us -> 5.29 us  [swapped(): return lax.ppermute(block, 'tensor', [(i, i ^ bit) for i in range(members)])]
    all_to_all x2, starting transfers between devices: 13.1 us -> 15.7 us  [exchange(): return lax.all_to_all(block, axis, split_axis=0, concat_axis=0, tiled=True)]
    unnamed x18 -> x16, local copies, waits for them, and re-layouts: 3.49 us -> 3.38 us
  transfers between devices with their start and end apart: 24 -> 24, of which waited for: 10 -> 17; matrix products, arithmetic and copies ran while one was open for 19% -> 18% of each run, Pallas kernels for 10% -> 10%
where the time goes in v4:
time: 159 us; the launch traced here: 158 us
  starting transfers between devices  48.2 us (30%)
  waiting for transfers between devices  31.6 us (20%)
  between operations  19.9 us (13%)
  matrix products  18.1 us (11%)
  Pallas kernels  17.6 us (11%)
  blocking collectives  9.6 us (6%)
  other arithmetic  7.57 us (5%)
  local copies, waits for them, and re-layouts  4.85 us (3%)
    dot_general x1, matrix products, per_device(): base = jnp.dot(gathered, joined_weight_matrix, preferred_element_type=F32)  18.1 us
    ppermute x12, starting transfers between devices, neighbour(): lax.ppermute(block, 'adapter', [(i, to(i)) for i in range(SIDE * SIDE)])  16.9 us
    ppermute x12, waiting for transfers between devices, neighbour(): lax.ppermute(block, 'adapter', [(i, to(i)) for i in range(SIDE * SIDE)])  16.3 us
    all_to_all x2, starting transfers between devices, exchange(): return lax.all_to_all(block, axis, split_axis=0, concat_axis=0, tiled=True)  15.7 us
    ppermute x8, starting transfers between devices, swapped(): return lax.ppermute(block, 'tensor', [(i, i ^ bit) for i in range(members)])  15.5 us
    unnamed x1, blocking collectives  9.6 us
    all_gather x1, waiting for transfers between devices, per_device(): weights = lax.all_gather(piece, 'adapter', axis=0, tiled=True)  6.56 us
    ppermute x8, waiting for transfers between devices, swapped(): return lax.ppermute(block, 'tensor', [(i, i ^ bit) for i in range(members)])  5.29 us
  transfers between devices with their start and end apart: 24, of which 17 were waited for; matrix products, arithmetic and copies ran while one was open for 18% of the time, Pallas kernels for 10%

profile of v4, /device:TPU:2, one launch (start us, length us, event | category | flops | bytes accessed | tf_op | source)
XLA Modules:
  0.0 157.6 jit_solution(6508966480863850493)
XLA Ops:
  6.5 0.7 all-gather.3.cloned.1.call-update
  7.3 3.5 %pad_maximum_fusion = (bf16[128,2304]{1,0:T(8,128)(2,1)S(1)}, bf16[128,2304]{1,0:T(8,128)(2,1)S(1)}, bf16[128,2304]{1,0:T(8,128)(2,1)}, bf16[128,2304]{1,0:T(8,1...) fusion(bf16[1024,1280]{1,0:T(8,128)(2,1)} %bitcast.42, ...), kind=kLoop, calls=%fused_computation.50 | loop fusion | flops 9437184 | bytes 9437184 | tf_op jit(solution)/shard_map/concatenate | solution.py:310
  10.8 4.1 %collective-permute-start.13 = (bf16[128,2304]{1,0:T(8,128)(2,1)S(1)}, bf16[128,2304]{1,0:T(8,128)(2,1)S(1)}, u32[]{:S(2)}, u32[]{:S(2)}) collective-permute-start(bf16[128,2304]{1,0:T(8,128)(2,1)S(1)} %get-tuple-element.447), channel_id=1, source_target_pairs={{0,24},{8,0},{16,8},{24,16},{32,56},{40,32},{48,40},{56,48},{64,88... | collective-permute-start | bytes 1769480 | tf_op jit(solution)/shard_map/ppermute | solution.py:239
  14.9 1.5 collective-permute-start.8
  16.4 1.1 collective-permute-start.9
  17.5 2.2 %collective-permute-start.10 = (bf16[128,2304]{1,0:T(8,128)(2,1)S(1)}, bf16[128,2304]{1,0:T(8,128)(2,1)}, u32[]{:S(2)}, u32[]{:S(2)}) collective-permute-start(bf16[128,2304]{1,0:T(8,128)(2,1)S(1)} %get-tuple-element.451), channel_id=1, source_target_pairs={{0,96},{8,104},{16,112},{24,120},{32,0},{40,8},{48,16},{56,24},{64... | collective-permute-start | bytes 1769480 | tf_op jit(solution)/shard_map/ppermute | solution.py:239
  19.7 7.8 %collective-permute-done.13 = bf16[128,2304]{1,0:T(8,128)(2,1)S(1)} collective-permute-done((bf16[128,2304]{1,0:T(8,128)(2,1)S(1)}, bf16[128,2304]{1,0:T(8,128)(2,1)S(1)}, u32[]{:S(2)}, u32[]{:S(2)}) %collective-permute-start.13) | collective-permute-done | bytes 589856 | tf_op jit(solution)/shard_map/ppermute | solution.py:239
  27.5 2.3 %collective-permute-start.12 = (bf16[128,2304]{1,0:T(8,128)(2,1)S(1)}, bf16[128,2304]{1,0:T(8,128)(2,1)}, u32[]{:S(2)}, u32[]{:S(2)}) collective-permute-start(bf16[128,2304]{1,0:T(8,128)(2,1)S(1)} %get-tuple-element.454), channel_id=1, source_target_pairs={{0,16},{8,24},{16,0},{24,8},{32,48},{40,56},{48,32},{56,40},{64,80... | collective-permute-start | bytes 1769480 | tf_op jit(solution)/shard_map/ppermute | solution.py:239
  29.8 0.6 dynamic-slice
  31.0 0.2 dynamic-update-slice
  31.3 9.6 %all-reduce.1 = s32[512]{0:T(512)S(1)} all-reduce(s32[512]{0:T(512)S(1)} %dynamic-update-slice), channel_id=1, replica_groups=mesh['adapter'=16,'tensor'=8] {'tensor'}, use_global_device_ids=true, to_apply=%add.1 | all-reduce | flops 512 | bytes 4096
  40.9 0.3 plan.1
  41.2 0.5 slice.90
  44.3 0.2 collective-permute-done.10
  44.5 3.1 %collective-permute-done.11 = bf16[128,2304]{1,0:T(8,128)(2,1)} collective-permute-done((bf16[128,2304]{1,0:T(8,128)(2,1)S(1)}, bf16[128,2304]{1,0:T(8,128)(2,1)}, u32[]{:S(2)}, u32[]{:S(2)}) %collective-permute-start.11) | collective-permute-done | bytes 589856 | tf_op jit(solution)/shard_map/ppermute | solution.py:239
  47.6 1.2 select_select_fusion.1
  48.8 0.1 collective-permute-start.16
  48.9 1.1 collective-permute-start.15
  50.0 0.9 collective-permute-start.14
  50.9 0.1 select_select_fusion
  51.0 1.5 collective-permute-start.19
  52.5 0.8 collective-permute-start.18
  53.4 0.6 collective-permute-done.16
  54.0 1.3 collective-permute-start.17
  55.2 0.4 collective-permute-done.15
  55.7 1.5 collective-permute-done.14
  57.3 1.9 %collective-permute-done.18 = bf16[32,2304]{1,0:T(8,128)(2,1)S(1)} collective-permute-done((bf16[32,2304]{1,0:T(8,128)(2,1)S(1)}, bf16[32,2304]{1,0:T(8,128)(2,1)S(1)}, u32[]{:S(2)}, u32[]{:S(2)}) %collective-permute-start.18) | collective-permute-done | bytes 147488 | tf_op jit(solution)/shard_map/ppermute | solution.py:239
  59.2 0.7 collective-permute-done.17
  59.9 0.7 pad_maximum_fusion.1
  60.7 0.6 all-gather.3.cloned.1.call-done.rows_ref
  61.3 3.2 %route.1 = (bf16[512,1152]{1,0:T(8,128)(2,1)}, bf16[128,1152]{1,0:T(8,128)(2,1)S(1)}) custom-call(s32[1]{0:T(128)} %bitcast.at_ref, s32[8,512]{1,0:T(8,128)S(1)} %get-tuple-element.324.info_ref, bf16[512,8192]{1,0:T(8,128)(2,1)} %all-gather.3.cloned.1.call-done.rows_ref), custom_call_target="tpu_custom_call" | custom-call | tf_op jit(solution)/shard_map/route/pallas_call | solution.py:95
  64.5 8.6 %all-to-all-start.2 = ((bf16[16,32,1152]{2,1,0:T(8,128)(2,1)}), bf16[16,32,1152]{2,1,0:T(8,128)(2,1)S(1)}, u32[]{:S(2)}, u32[]{:S(2)}) async-start(bf16[16,32,1152]{2,1,0:T(8,128)(2,1)} %bitcast.2), calls=%async_computation.2 | async-start | bytes 2359296 | tf_op jit(solution)/shard_map/all_to_all | solution.py:227
  73.1 18.1 %fusion.31 = f32[512,1280]{1,0:T(8,128)} fusion(bf16[512,8192]{1,0:T(8,128)(2,1)} %all-gather.3.cloned.1.call-done.rows_ref, bf16[8192,1280]{1,0:T(8,128)(2,1)} %param.9), kind=kOutput, calls=%fused_computation.86 | convolution fusion | flops 10737418240 | bytes 31981568 | tf_op jit(solution)/shard_map/dot_general | solution.py:326
  91.2 2.2 %all-to-all-done.2 = bf16[16,32,1152]{2,1,0:T(8,128)(2,1)S(1)} async-done(((bf16[16,32,1152]{2,1,0:T(8,128)(2,1)}), bf16[16,32,1152]{2,1,0:T(8,128)(2,1)S(1)}, u32[]{:S(2)}, u32[]{:S(2)}) %all-to-all-start.2) | async-done | bytes 1179680 | tf_op jit(solution)/shard_map/all_to_all | solution.py:227
  93.4 2.9 %low.8 = f32[16,512]{1,0:T(8,128)S(1)} custom-call(s32[64]{0:T(128)S(1)} %iota.30.labels_ref, bf16[512,1152]{1,0:T(8,128)(2,1)S(1)} %bitcast.39, bf16[1024,1024]{1,0:T(8,128)(2,1)} %bitcast.47), custom_call_target="tpu_custom_call" | custom-call | flops 1207959552 | bytes 3538944 | tf_op jit(solution)/shard_map/low/pallas_call | solution.py:130
  96.3 0.1 collective-permute-start.4
  96.4 1.2 collective-permute-done.4
  97.6 0.7 collective-permute-start.7
  98.4 1.4 collective-permute-start.6
  99.7 2.0 %collective-permute-start.5 = (f32[16,512]{1,0:T(8,128)S(1)}, f32[16,512]{1,0:T(8,128)S(1)}, u32[]{:S(2)}, u32[]{:S(2)}) collective-permute-start(f32[16,512]{1,0:T(8,128)S(1)} %add.175), channel_id=1, source_target_pairs={{0,2},{1,3},{2,0},{3,1},{4,6},{5,7},{6,4},{7,5},{8,10},{9,11},{10,... | collective-permute-start | bytes 98312 | tf_op jit(solution)/shard_map/ppermute | solution.py:284
  101.8 0.1 broadcast_in_dim.22
  101.9 0.2 copy.12
  102.1 0.1 slice.89
  102.2 0.1 copy.11
  102.3 0.8 collective-permute-done.7
  103.0 0.8 collective-permute-done.6
  103.9 0.1 collective-permute-done.5
  104.0 4.7 %delta.7 = bf16[512,1280]{1,0:T(8,128)(2,1)} custom-call(f32[16,512]{1,0:T(8,128)S(1)} %add_add_fusion.1.low_ref, bf16[512,1152]{1,0:T(8,128)(2,1)S(1)} %bitcast.40, bf16[1024,1280]{1,0:T(8,128)(2,1)} %bitcast.43), custom_call_target="tpu_custom_call" | custom-call | flops 1342177280 | bytes 3932160 | tf_op jit(solution)/shard_map/delta/pallas_call | solution.py:166
  108.7 0.5 slice.92
  109.3 1.3 compare_reduce_fusion.1
  111.8 0.7 slice_reduce_fusion
  114.3 0.2 while.15
  114.5 7.1 %all-to-all-start.3 = ((bf16[16,32,1280]{2,1,0:T(8,128)(2,1)}), bf16[16,32,1280]{2,1,0:T(8,128)(2,1)S(1)}, u32[]{:S(2)}, u32[]{:S(2)}) async-start(bf16[16,32,1280]{2,1,0:T(8,128)(2,1)} %bitcast.13), calls=%async_computation.3 | async-start | bytes 2621440 | tf_op jit(solution)/shard_map/all_to_all | solution.py:227
  121.6 6.6 %all-gather.5.cloned.1.call-done.down_ref.weights_ref = bf16[1024,2304]{1,0:T(8,128)(2,1)} async-done(((bf16[64,2304]{1,0:T(8,128)(2,1)}), bf16[1024,2304]{1,0:T(8,128)(2,1)}) %all-gather.5.cloned.1.call-update) | async-done | bytes 4718608 | tf_op jit(solution)/shard_map/all_gather | solution.py:319
  128.2 2.3 %copy-done = bf16[1024,2304]{1,0:T(8,128)(2,1)S(1)} copy-done((bf16[1024,2304]{1,0:T(8,128)(2,1)S(1)}, bf16[1024,2304]{1,0:T(8,128)(2,1)}, u32[]{:S(2)}) %copy-start) | copy-done | bytes 4718616
  130.5 1.3 low.9
  131.8 0.1 collective-permute-start.20
  131.9 1.2 collective-permute-done.20
  133.1 10.4 %collective-permute-start.23 = (f32[16,128]{1,0:T(8,128)S(1)}, f32[16,128]{1,0:T(8,128)S(1)}, u32[]{:S(2)}, u32[]{:S(2)}) collective-permute-start(f32[16,128]{1,0:T(8,128)S(1)} %add.193), channel_id=1, source_target_pairs={{0,6},{1,7},{2,4},{3,5},{4,2},{5,3},{6,0},{7,1},{8,14},{9,15},{10,... | collective-permute-start | bytes 24584 | tf_op jit(solution)/shard_map/ppermute | solution.py:284
  143.5 0.2 collective-permute-start.22
  143.7 0.6 collective-permute-start.21
  144.3 3.0 %add_back.1.base_ref = f32[512,1280]{1,0:T(8,128)S(1)} custom-call(s32[512,128]{1,0:T(8,128)S(1)} %get-tuple-element.333.tall_ref, f32[512,1280]{1,0:T(8,128)} %get-tuple-element.347.base_ref, bf16[512,1280]{1,0:T(8,128)(2,1)S(1)} %bitcast.38), custom_call_target="tpu_custom_call" | custom-call | flops 671088640 | bytes 6553600 | tf_op jit(solution)/shard_map/add_back/pallas_call | solution.py:187
  147.3 1.3 collective-permute-done.22
  148.6 2.1 %finish.1 = bf16[512,1280]{1,0:T(8,128)(2,1)} custom-call(s32[1]{0:T(128)} %bitcast.9.full_ref, s32[8,1024]{1,0:T(8,128)S(1)} %broadcast_in_dim.23.labels_ref, s32[512,128]{1,0:T(8,128)S(1)} %get-tuple-element.333.tall_ref, f32[16,128]{1,0:T(8,128)S(1)} %add_add_fusion.2.low_ref, bf16[128,1152]{1,0:T(8,128)(2,1)S(1)} %get-tuple-element.335.rows_ref, ...), custom_call_target="tpu_custom_call" | custom-call | flops 1207959552 | bytes 3932160 | tf_op jit(solution)/shard_map/finish/pallas_call | solution.py:213
  (39 shorter events, 0.4 us)
Async XLA Ops:
  6.5 54.8 %all-gather.3.cloned.1.call-start = ((), (), s32[]{:S(2)}) async-start(), calls=%async_computation.4 | async-start | bytes 9437184 | tf_op jit(solution)/shard_map/all_gather | solution.py:312
  7.3 120.9 %all-gather.5.cloned.1.call-start = ((), (), s32[]{:S(2)}) async-start(), calls=%async_computation.5 | async-start | bytes 5013504 | tf_op jit(solution)/shard_map/all_gather | solution.py:319
  7.3 22.5 %copy-start.7 = (u32[128]{0:T(128)S(1)}, u32[128]{0:T(128)}, u32[]{:S(2)}) copy-start(u32[128]{0:T(128)} %constant.217) | copy-start | bytes 1540
  7.3 23.7 %copy-start.6 = (s32[64]{0:T(128)S(1)}, s32[64]{0:T(128)}, u32[]{:S(2)}) copy-start(s32[64]{0:T(128)} %param.8) | copy-start | bytes 772
  10.8 16.7 %collective-permute-start.13 = (bf16[128,2304]{1,0:T(8,128)(2,1)S(1)}, bf16[128,2304]{1,0:T(8,128)(2,1)S(1)}, u32[]{:S(2)}, u32[]{:S(2)}) collective-permute-start(bf16[128,2304]{1,0:T(8,128)(2,1)S(1)} %get-tuple-element.447), channel_id=1, source_target_pairs={{0,24},{8,0},{16,8},{24,16},{32,56},{40,32},{48,40},{56,48},{64,88... | collective-permute-start | bytes 1769480 | tf_op jit(solution)/shard_map/ppermute | solution.py:239
  14.9 29.4 %collective-permute-start.8 = (bf16[128,2304]{1,0:T(8,128)(2,1)}, bf16[128,2304]{1,0:T(8,128)(2,1)}, u32[]{:S(2)}, u32[]{:S(2)}) collective-permute-start(bf16[128,2304]{1,0:T(8,128)(2,1)} %get-tuple-element.449), channel_id=1, source_target_pairs={{0,32},{8,40},{16,48},{24,56},{32,64},{40,72},{48,80},{56,88},{64,... | collective-permute-start | bytes 1769480 | tf_op jit(solution)/shard_map/ppermute | solution.py:239
  16.4 27.9 %collective-permute-start.9 = (bf16[128,2304]{1,0:T(8,128)(2,1)}, bf16[128,2304]{1,0:T(8,128)(2,1)}, u32[]{:S(2)}, u32[]{:S(2)}) collective-permute-start(bf16[128,2304]{1,0:T(8,128)(2,1)} %get-tuple-element.450), channel_id=1, source_target_pairs={{0,64},{8,72},{16,80},{24,88},{32,96},{40,104},{48,112},{56,120},{... | collective-permute-start | bytes 1769480 | tf_op jit(solution)/shard_map/ppermute | solution.py:239
  17.5 27.0 %collective-permute-start.10 = (bf16[128,2304]{1,0:T(8,128)(2,1)S(1)}, bf16[128,2304]{1,0:T(8,128)(2,1)}, u32[]{:S(2)}, u32[]{:S(2)}) collective-permute-start(bf16[128,2304]{1,0:T(8,128)(2,1)S(1)} %get-tuple-element.451), channel_id=1, source_target_pairs={{0,96},{8,104},{16,112},{24,120},{32,0},{40,8},{48,16},{56,24},{64... | collective-permute-start | bytes 1769480 | tf_op jit(solution)/shard_map/ppermute | solution.py:239
  19.6 27.9 %collective-permute-start.11 = (bf16[128,2304]{1,0:T(8,128)(2,1)S(1)}, bf16[128,2304]{1,0:T(8,128)(2,1)}, u32[]{:S(2)}, u32[]{:S(2)}) collective-permute-start(bf16[128,2304]{1,0:T(8,128)(2,1)S(1)} %get-tuple-element.453), channel_id=1, source_target_pairs={{0,8},{8,16},{16,24},{24,0},{32,40},{40,48},{48,56},{56,32},{64,72... | collective-permute-start | bytes 1769480 | tf_op jit(solution)/shard_map/ppermute | solution.py:239
  27.5 2.3 %copy-start.4 = (bf16[128,2304]{1,0:T(8,128)(2,1)}, bf16[128,2304]{1,0:T(8,128)(2,1)S(1)}, u32[]{:S(2)}) copy-start(bf16[128,2304]{1,0:T(8,128)(2,1)S(1)} %collective-permute-done.13) | copy-start | bytes 1769476
  27.5 20.1 %collective-permute-start.12 = (bf16[128,2304]{1,0:T(8,128)(2,1)S(1)}, bf16[128,2304]{1,0:T(8,128)(2,1)}, u32[]{:S(2)}, u32[]{:S(2)}) collective-permute-start(bf16[128,2304]{1,0:T(8,128)(2,1)S(1)} %get-tuple-element.454), channel_id=1, source_target_pairs={{0,16},{8,24},{16,0},{24,8},{32,48},{40,56},{48,32},{56,40},{64,80... | collective-permute-start | bytes 1769480 | tf_op jit(solution)/shard_map/ppermute | solution.py:239
  44.5 6.4 %copy-start.5 = (bf16[128,2304]{1,0:T(8,128)(2,1)S(1)}, bf16[128,2304]{1,0:T(8,128)(2,1)}, u32[]{:S(2)}) copy-start(bf16[128,2304]{1,0:T(8,128)(2,1)} %copy-done.4) | copy-start | bytes 1769476
  48.8 5.2 %collective-permute-start.16 = (bf16[32,2304]{1,0:T(8,128)(2,1)S(1)}, bf16[32,2304]{1,0:T(8,128)(2,1)S(1)}, u32[]{:S(2)}, u32[]{:S(2)}) collective-permute-start(bf16[32,2304]{1,0:T(8,128)(2,1)S(1)} %get-tuple-element.455), channel_id=1, source_target_pairs={{0,24},{8,0},{16,8},{24,16},{32,56},{40,32},{48,40},{56,48},{64,88... | collective-permute-start | bytes 442376 | tf_op jit(solution)/shard_map/ppermute | solution.py:239
  48.9 6.8 %collective-permute-start.15 = (bf16[32,2304]{1,0:T(8,128)(2,1)S(1)}, bf16[32,2304]{1,0:T(8,128)(2,1)S(1)}, u32[]{:S(2)}, u32[]{:S(2)}) collective-permute-start(bf16[32,2304]{1,0:T(8,128)(2,1)S(1)} %get-tuple-element.456), channel_id=1, source_target_pairs={{0,16},{8,24},{16,0},{24,8},{32,48},{40,56},{48,32},{56,40},{64,80... | collective-permute-start | bytes 442376 | tf_op jit(solution)/shard_map/ppermute | solution.py:239
  50.0 7.2 %collective-permute-start.14 = (bf16[32,2304]{1,0:T(8,128)(2,1)S(1)}, bf16[32,2304]{1,0:T(8,128)(2,1)S(1)}, u32[]{:S(2)}, u32[]{:S(2)}) collective-permute-start(bf16[32,2304]{1,0:T(8,128)(2,1)S(1)} %get-tuple-element.457), channel_id=1, source_target_pairs={{0,8},{8,16},{16,24},{24,0},{32,40},{40,48},{48,56},{56,32},{64,72... | collective-permute-start | bytes 442376 | tf_op jit(solution)/shard_map/ppermute | solution.py:239
  51.0 6.2 %collective-permute-start.19 = (bf16[32,2304]{1,0:T(8,128)(2,1)S(1)}, bf16[32,2304]{1,0:T(8,128)(2,1)S(1)}, u32[]{:S(2)}, u32[]{:S(2)}) collective-permute-start(bf16[32,2304]{1,0:T(8,128)(2,1)S(1)} %get-tuple-element.458), channel_id=1, source_target_pairs={{0,96},{8,104},{16,112},{24,120},{32,0},{40,8},{48,16},{56,24},{64... | collective-permute-start | bytes 442376 | tf_op jit(solution)/shard_map/ppermute | solution.py:239
  52.5 6.6 %collective-permute-start.18 = (bf16[32,2304]{1,0:T(8,128)(2,1)S(1)}, bf16[32,2304]{1,0:T(8,128)(2,1)S(1)}, u32[]{:S(2)}, u32[]{:S(2)}) collective-permute-start(bf16[32,2304]{1,0:T(8,128)(2,1)S(1)} %get-tuple-element.459), channel_id=1, source_target_pairs={{0,64},{8,72},{16,80},{24,88},{32,96},{40,104},{48,112},{56,120},{... | collective-permute-start | bytes 442376 | tf_op jit(solution)/shard_map/ppermute | solution.py:239
  54.0 5.9 %collective-permute-start.17 = (bf16[32,2304]{1,0:T(8,128)(2,1)S(1)}, bf16[32,2304]{1,0:T(8,128)(2,1)S(1)}, u32[]{:S(2)}, u32[]{:S(2)}) collective-permute-start(bf16[32,2304]{1,0:T(8,128)(2,1)S(1)} %get-tuple-element.460), channel_id=1, source_target_pairs={{0,32},{8,40},{16,48},{24,56},{32,64},{40,72},{48,80},{56,88},{64,... | collective-permute-start | bytes 442376 | tf_op jit(solution)/shard_map/ppermute | solution.py:239
  64.5 28.9 %all-to-all-start.2 = ((bf16[16,32,1152]{2,1,0:T(8,128)(2,1)}), bf16[16,32,1152]{2,1,0:T(8,128)(2,1)S(1)}, u32[]{:S(2)}, u32[]{:S(2)}) async-start(bf16[16,32,1152]{2,1,0:T(8,128)(2,1)} %bitcast.2), calls=%async_computation.2 | async-start | bytes 2359296 | tf_op jit(solution)/shard_map/all_to_all | solution.py:227
  96.3 1.3 collective-permute-start.4
  97.6 5.4 %collective-permute-start.7 = (f32[16,512]{1,0:T(8,128)S(1)}, f32[16,512]{1,0:T(8,128)S(1)}, u32[]{:S(2)}, u32[]{:S(2)}) collective-permute-start(f32[16,512]{1,0:T(8,128)S(1)} %add.175), channel_id=1, source_target_pairs={{0,6},{1,7},{2,4},{3,5},{4,2},{5,3},{6,0},{7,1},{8,14},{9,15},{10,... | collective-permute-start | bytes 98312 | tf_op jit(solution)/shard_map/ppermute | solution.py:284
  98.4 5.5 %collective-permute-start.6 = (f32[16,512]{1,0:T(8,128)S(1)}, f32[16,512]{1,0:T(8,128)S(1)}, u32[]{:S(2)}, u32[]{:S(2)}) collective-permute-start(f32[16,512]{1,0:T(8,128)S(1)} %add.175), channel_id=1, source_target_pairs={{0,4},{1,5},{2,6},{3,7},{4,0},{5,1},{6,2},{7,3},{8,12},{9,13},{10,... | collective-permute-start | bytes 98312 | tf_op jit(solution)/shard_map/ppermute | solution.py:284
  99.7 4.2 %collective-permute-start.5 = (f32[16,512]{1,0:T(8,128)S(1)}, f32[16,512]{1,0:T(8,128)S(1)}, u32[]{:S(2)}, u32[]{:S(2)}) collective-permute-start(f32[16,512]{1,0:T(8,128)S(1)} %add.175), channel_id=1, source_target_pairs={{0,2},{1,3},{2,0},{3,1},{4,6},{5,7},{6,4},{7,5},{8,10},{9,11},{10,... | collective-permute-start | bytes 98312 | tf_op jit(solution)/shard_map/ppermute | solution.py:284
  114.5 29.8 %all-to-all-start.3 = ((bf16[16,32,1280]{2,1,0:T(8,128)(2,1)}), bf16[16,32,1280]{2,1,0:T(8,128)(2,1)S(1)}, u32[]{:S(2)}, u32[]{:S(2)}) async-start(bf16[16,32,1280]{2,1,0:T(8,128)(2,1)} %bitcast.13), calls=%async_computation.3 | async-start | bytes 2621440 | tf_op jit(solution)/shard_map/all_to_all | solution.py:227
  128.2 2.3 %copy-start = (bf16[1024,2304]{1,0:T(8,128)(2,1)S(1)}, bf16[1024,2304]{1,0:T(8,128)(2,1)}, u32[]{:S(2)}) copy-start(bf16[1024,2304]{1,0:T(8,128)(2,1)} %all-gather.5.cloned.1.call-done.down_ref.weights_ref) | copy-start | bytes 14155780
  131.8 1.3 collective-permute-start.20
  133.1 14.3 %collective-permute-start.23 = (f32[16,128]{1,0:T(8,128)S(1)}, f32[16,128]{1,0:T(8,128)S(1)}, u32[]{:S(2)}, u32[]{:S(2)}) collective-permute-start(f32[16,128]{1,0:T(8,128)S(1)} %add.193), channel_id=1, source_target_pairs={{0,6},{1,7},{2,4},{3,5},{4,2},{5,3},{6,0},{7,1},{8,14},{9,15},{10,... | collective-permute-start | bytes 24584 | tf_op jit(solution)/shard_map/ppermute | solution.py:284
  143.5 5.2 %collective-permute-start.22 = (f32[16,128]{1,0:T(8,128)S(1)}, f32[16,128]{1,0:T(8,128)S(1)}, u32[]{:S(2)}, u32[]{:S(2)}) collective-permute-start(f32[16,128]{1,0:T(8,128)S(1)} %add.193), channel_id=1, source_target_pairs={{0,4},{1,5},{2,6},{3,7},{4,0},{5,1},{6,2},{7,3},{8,12},{9,13},{10,... | collective-permute-start | bytes 24584 | tf_op jit(solution)/shard_map/ppermute | solution.py:284
  143.7 4.9 %collective-permute-start.21 = (f32[16,128]{1,0:T(8,128)S(1)}, f32[16,128]{1,0:T(8,128)S(1)}, u32[]{:S(2)}, u32[]{:S(2)}) collective-permute-start(f32[16,128]{1,0:T(8,128)S(1)} %add.193), channel_id=1, source_target_pairs={{0,2},{1,3},{2,0},{3,1},{4,6},{5,7},{6,4},{7,5},{8,10},{9,11},{10,... | collective-permute-start | bytes 24584 | tf_op jit(solution)/shard_map/ppermute | solution.py:284
  144.3 4.3 %copy-start.1 = (bf16[1024,2304]{1,0:T(8,128)(2,1)S(1)}, bf16[1024,2304]{1,0:T(8,128)(2,1)}, u32[]{:S(2)}) copy-start(bf16[1024,2304]{1,0:T(8,128)(2,1)} %all-gather.5.cloned.1.call-done.down_ref.weights_ref) | copy-start | bytes 14155780
Sparse Core Ops, SparseCore 0:
  9.1 52.1 all-gather.2
  63.5 64.6 all-gather.4

commit v5 on v4

--- a/solution.py
+++ b/solution.py
@@ -176,28 +176,9 @@
     )(low, rows, up)
 
 
-def add_kernel(even, tall_ref, base_ref, back_ref, out_ref):
-    owner, place = tall_ref[:, 0:1], tall_ref[:, 2:3]
-    target = jnp.where(place < even, owner * even + place, -1)
-    chosen = (iota((tall_ref.shape[0], back_ref.shape[0]), 1) == target).astype(BF16)
-    out_ref[...] = base_ref[...] + jnp.dot(chosen, back_ref[...], preferred_element_type=F32)
-
-
-def add_back(tall, base, back, even):
-    return pl.pallas_call(
-        functools.partial(add_kernel, even),
-        out_shape=jax.ShapeDtypeStruct(base.shape, F32),
-        in_specs=[VMEM] * 3,
-        out_specs=VMEM,
-        compiler_params=pltpu.CompilerParams(vmem_limit_bytes=LIMIT),
-        cost_estimate=pl.CostEstimate(
-            flops=2 * back.size * base.shape[0], bytes_accessed=8 * base.size + 2 * back.size, transcendentals=0
-        ),
-        name="add_back",
-    )(tall, base, back)
-
-
-def finish_kernel(even, full_ref, labels_ref, tall_ref, low_ref, rows_ref, base_ref, weights_ref, out_ref):
+def finish_kernel(
+    even, full_ref, labels_ref, tall_ref, low_ref, rows_ref, base_ref, back_ref, weights_ref, out_ref
+):
     group, columns = base_ref.shape
     owner, place = tall_ref[:, 0:1], tall_ref[:, 2:3]
     spare = jnp.where((owner == full_ref[0]) & (place >= even), place - even, -1)
@@ -206,21 +187,24 @@
     up = weights_ref[:, weights_ref.shape[1] - columns :]
     delta = (2.0 * jnp.dot(wide, up, preferred_element_type=F32)).astype(BF16)
     added = jnp.dot(chosen, delta, preferred_element_type=F32)
+    target = jnp.where(place < even, owner * even + place, -1)
+    main = (iota((group, back_ref.shape[0]), 1) == target).astype(BF16)
+    added += jnp.dot(main, back_ref[...], preferred_element_type=F32)
     out_ref[...] = (base_ref[...] + added).astype(BF16)
 
 
-def finish(full, labels, tall, low, rows, base, weights, even):
+def finish(full, labels, tall, low, rows, base, back, weights, even):
     return pl.pallas_call(
         functools.partial(finish_kernel, even),
         out_shape=jax.ShapeDtypeStruct(base.shape, BF16),
-        in_specs=[pl.BlockSpec(memory_space=pltpu.SMEM)] + [VMEM] * 6,
+        in_specs=[pl.BlockSpec(memory_space=pltpu.SMEM)] + [VMEM] * 7,
         out_specs=VMEM,
         compiler_params=pltpu.CompilerParams(vmem_limit_bytes=LIMIT),
         cost_estimate=pl.CostEstimate(
             flops=4 * weights.size * rows.shape[0], bytes_accessed=6 * base.size, transcendentals=0
         ),
         name="finish",
-    )(full, labels, tall, low, rows, base, weights)
+    )(full, labels, tall, low, rows, base, back, weights)
 
 
 def exchange(block, axis):
@@ -362,10 +346,9 @@
 
     _, base = lax.while_loop(lambda carry: carry[0] < turns, more, (jnp.int32(1), base))
 
-    base = add_back(tall, base, back, even)
-
-    rest_low, base = total_over_tensor(low_part(labels, rest_rows, weights, rank), base)
-    return finish(full.reshape(1), places, tall, rest_low, rest_rows, base, weights, even)
+
+    rest_low, back = total_over_tensor(low_part(labels, rest_rows, weights, rank), back)
+    return finish(full.reshape(1), places, tall, rest_low, rest_rows, base, back, weights, even)
 
 
 def solution(mesh):

time: 159 us -> 166 us (1.044)
  waiting for transfers between devices: 31.6 us -> 45 us
  starting transfers between devices: 48.2 us -> 39.2 us
  local copies, waits for them, and re-layouts: 4.85 us -> 7.13 us
    all_gather x1, waiting for transfers between devices: 6.56 us -> 22.2 us  [per_device(): weights = lax.all_gather(piece, 'adapter', axis=0, tiled=True)]
    ppermute x8, starting transfers between devices: 15.5 us -> 8.36 us  [swapped(): return lax.ppermute(block, 'tensor', [(i, i ^ bit) for i in range(members)])]
    pallas_call x1 -> x0, Pallas kernels: 2.99 us -> none  [add_back(): pl.pallas_call(functools.partial(add_kernel, even), out_shape=jax.ShapeDt...]
    pallas_call x1, Pallas kernels: 2.11 us -> 4.53 us  [finish(): pl.pallas_call(functools.partial(finish_kernel, even), out_shape=jax.Shap...]
    all_to_all x2, starting transfers between devices: 15.7 us -> 13.3 us  [exchange(): return lax.all_to_all(block, axis, split_axis=0, concat_axis=0, tiled=True)]
    unnamed x16, local copies, waits for them, and re-layouts: 3.38 us -> 5.7 us
    ppermute x8, waiting for transfers between devices: 5.29 us -> 3.4 us  [swapped(): return lax.ppermute(block, 'tensor', [(i, i ^ bit) for i in range(members)])]
  transfers between devices with their start and end apart: 24 -> 24, of which waited for: 17 -> 13; matrix products, arithmetic and copies ran while one was open for 18% -> 18% of each run, Pallas kernels for 10% -> 8%
where the time goes in v5:
time: 166 us; the launch traced here: 165 us
  waiting for transfers between devices  45 us (27%)
  starting transfers between devices  39.2 us (24%)
  between operations  19.9 us (12%)
  matrix products  18.2 us (11%)
  Pallas kernels  17 us (10%)
  blocking collectives  9.6 us (6%)
  other arithmetic  8.63 us (5%)
  local copies, waits for them, and re-layouts  7.13 us (4%)
    all_gather x1, waiting for transfers between devices, per_device(): weights = lax.all_gather(piece, 'adapter', axis=0, tiled=True)  22.2 us
    dot_general x1, matrix products, per_device(): base = jnp.dot(gathered, joined_weight_matrix, preferred_element_type=F32)  18.2 us
    ppermute x12, starting transfers between devices, neighbour(): lax.ppermute(block, 'adapter', [(i, to(i)) for i in range(SIDE * SIDE)])  17.4 us
    ppermute x12, waiting for transfers between devices, neighbour(): lax.ppermute(block, 'adapter', [(i, to(i)) for i in range(SIDE * SIDE)])  15.8 us
    all_to_all x2, starting transfers between devices, exchange(): return lax.all_to_all(block, axis, split_axis=0, concat_axis=0, tiled=True)  13.3 us
    unnamed x1, blocking collectives  9.6 us
    ppermute x8, starting transfers between devices, swapped(): return lax.ppermute(block, 'tensor', [(i, i ^ bit) for i in range(members)])  8.36 us
    unnamed x16, local copies, waits for them, and re-layouts  5.7 us
  transfers between devices with their start and end apart: 24, of which 13 were waited for; matrix products, arithmetic and copies ran while one was open for 18% of the time, Pallas kernels for 8%

profile of v5, /device:TPU:2, one launch (start us, length us, event | category | flops | bytes accessed | tf_op | source)
XLA Modules:
  0.0 164.7 jit_solution(8633150827188333399)
XLA Ops:
  6.5 0.7 all-gather.3.cloned.1.call-update
  7.3 0.0 all-gather.5.cloned.1.call-start
  7.3 3.5 %pad_maximum_fusion = (bf16[128,2304]{1,0:T(8,128)(2,1)S(1)}, bf16[128,2304]{1,0:T(8,128)(2,1)S(1)}, bf16[128,2304]{1,0:T(8,128)(2,1)}, bf16[128,2304]{1,0:T(8,1...) fusion(bf16[1024,1280]{1,0:T(8,128)(2,1)} %bitcast.42, ...), kind=kLoop, calls=%fused_computation.50 | loop fusion | flops 9437184 | bytes 9437184 | tf_op jit(solution)/shard_map/concatenate | solution.py:294
  10.8 4.1 %collective-permute-start.13 = (bf16[128,2304]{1,0:T(8,128)(2,1)S(1)}, bf16[128,2304]{1,0:T(8,128)(2,1)S(1)}, u32[]{:S(2)}, u32[]{:S(2)}) collective-permute-start(bf16[128,2304]{1,0:T(8,128)(2,1)S(1)} %get-tuple-element.447), channel_id=1, source_target_pairs={{0,24},{8,0},{16,8},{24,16},{32,56},{40,32},{48,40},{56,48},{64,88... | collective-permute-start | bytes 1769480 | tf_op jit(solution)/shard_map/ppermute | solution.py:223
  14.9 1.5 collective-permute-start.8
  16.4 1.1 collective-permute-start.9
  17.5 2.2 %collective-permute-start.10 = (bf16[128,2304]{1,0:T(8,128)(2,1)S(1)}, bf16[128,2304]{1,0:T(8,128)(2,1)}, u32[]{:S(2)}, u32[]{:S(2)}) collective-permute-start(bf16[128,2304]{1,0:T(8,128)(2,1)S(1)} %get-tuple-element.451), channel_id=1, source_target_pairs={{0,96},{8,104},{16,112},{24,120},{32,0},{40,8},{48,16},{56,24},{64... | collective-permute-start | bytes 1769480 | tf_op jit(solution)/shard_map/ppermute | solution.py:223
  19.7 7.8 %collective-permute-done.13 = bf16[128,2304]{1,0:T(8,128)(2,1)S(1)} collective-permute-done((bf16[128,2304]{1,0:T(8,128)(2,1)S(1)}, bf16[128,2304]{1,0:T(8,128)(2,1)S(1)}, u32[]{:S(2)}, u32[]{:S(2)}) %collective-permute-start.13) | collective-permute-done | bytes 589856 | tf_op jit(solution)/shard_map/ppermute | solution.py:223
  27.5 2.3 %collective-permute-start.12 = (bf16[128,2304]{1,0:T(8,128)(2,1)S(1)}, bf16[128,2304]{1,0:T(8,128)(2,1)}, u32[]{:S(2)}, u32[]{:S(2)}) collective-permute-start(bf16[128,2304]{1,0:T(8,128)(2,1)S(1)} %get-tuple-element.454), channel_id=1, source_target_pairs={{0,16},{8,24},{16,0},{24,8},{32,48},{40,56},{48,32},{56,40},{64,80... | collective-permute-start | bytes 1769480 | tf_op jit(solution)/shard_map/ppermute | solution.py:223
  29.8 0.6 dynamic-slice
  31.0 0.2 dynamic-update-slice
  31.3 9.6 %all-reduce.1 = s32[512]{0:T(512)S(1)} all-reduce(s32[512]{0:T(512)S(1)} %dynamic-update-slice), channel_id=1, replica_groups=mesh['adapter'=16,'tensor'=8] {'tensor'}, use_global_device_ids=true, to_apply=%add.1 | all-reduce | flops 512 | bytes 4096
  40.9 0.3 plan.1
  41.2 0.5 slice.90
  44.3 0.2 collective-permute-done.10
  44.5 3.1 %collective-permute-done.11 = bf16[128,2304]{1,0:T(8,128)(2,1)} collective-permute-done((bf16[128,2304]{1,0:T(8,128)(2,1)S(1)}, bf16[128,2304]{1,0:T(8,128)(2,1)}, u32[]{:S(2)}, u32[]{:S(2)}) %collective-permute-start.11) | collective-permute-done | bytes 589856 | tf_op jit(solution)/shard_map/ppermute | solution.py:223
  47.6 1.2 select_select_fusion.1
  48.8 0.1 collective-permute-start.16
  48.9 1.1 collective-permute-start.15
  50.0 0.9 collective-permute-start.14
  50.9 1.2 select_select_fusion
  52.1 1.6 collective-permute-start.19
  53.6 0.6 collective-permute-start.18
  54.3 2.0 %collective-permute-start.17 = (bf16[32,2304]{1,0:T(8,128)(2,1)S(1)}, bf16[32,2304]{1,0:T(8,128)(2,1)S(1)}, u32[]{:S(2)}, u32[]{:S(2)}) collective-permute-start(bf16[32,2304]{1,0:T(8,128)(2,1)S(1)} %get-tuple-element.460), channel_id=1, source_target_pairs={{0,32},{8,40},{16,48},{24,56},{32,64},{40,72},{48,80},{56,88},{64,... | collective-permute-start | bytes 442376 | tf_op jit(solution)/shard_map/ppermute | solution.py:223
  56.2 1.0 collective-permute-done.14
  57.3 0.5 collective-permute-done.19
  57.8 2.5 %collective-permute-done.18 = bf16[32,2304]{1,0:T(8,128)(2,1)S(1)} collective-permute-done((bf16[32,2304]{1,0:T(8,128)(2,1)S(1)}, bf16[32,2304]{1,0:T(8,128)(2,1)S(1)}, u32[]{:S(2)}, u32[]{:S(2)}) %collective-permute-start.18) | collective-permute-done | bytes 147488 | tf_op jit(solution)/shard_map/ppermute | solution.py:223
  60.3 0.7 collective-permute-done.17
  60.9 0.1 slice_select_fusion
  61.0 0.7 pad_maximum_fusion.1
  61.7 0.0 all-gather.5.cloned.1.call-update
  61.8 0.0 all-gather.3.cloned.1.call-done.rows_ref
  61.8 3.2 %route.1 = (bf16[512,1152]{1,0:T(8,128)(2,1)}, bf16[128,1152]{1,0:T(8,128)(2,1)S(1)}) custom-call(s32[1]{0:T(128)} %bitcast.at_ref, s32[8,512]{1,0:T(8,128)S(1)} %get-tuple-element.324.info_ref, bf16[512,8192]{1,0:T(8,128)(2,1)} %all-gather.3.cloned.1.call-done.rows_ref), custom_call_target="tpu_custom_call" | custom-call | tf_op jit(solution)/shard_map/route/pallas_call | solution.py:95
  65.0 7.3 %all-to-all-start.2 = ((bf16[16,32,1152]{2,1,0:T(8,128)(2,1)}), bf16[16,32,1152]{2,1,0:T(8,128)(2,1)S(1)}, u32[]{:S(2)}, u32[]{:S(2)}) async-start(bf16[16,32,1152]{2,1,0:T(8,128)(2,1)} %bitcast.2), calls=%async_computation.2 | async-start | bytes 2359296 | tf_op jit(solution)/shard_map/all_to_all | solution.py:211
  72.3 18.2 %fusion.31 = f32[512,1280]{1,0:T(8,128)} fusion(bf16[512,8192]{1,0:T(8,128)(2,1)} %all-gather.3.cloned.1.call-done.rows_ref, bf16[8192,1280]{1,0:T(8,128)(2,1)} %param.9), kind=kOutput, calls=%fused_computation.86 | convolution fusion | flops 10737418240 | bytes 31981568 | tf_op jit(solution)/shard_map/dot_general | solution.py:310
  90.4 2.9 %all-to-all-done.2 = bf16[16,32,1152]{2,1,0:T(8,128)(2,1)S(1)} async-done(((bf16[16,32,1152]{2,1,0:T(8,128)(2,1)}), bf16[16,32,1152]{2,1,0:T(8,128)(2,1)S(1)}, u32[]{:S(2)}, u32[]{:S(2)}) %all-to-all-start.2) | async-done | bytes 1179680 | tf_op jit(solution)/shard_map/all_to_all | solution.py:211
  93.3 2.9 %low.8 = f32[16,512]{1,0:T(8,128)S(1)} custom-call(s32[64]{0:T(128)S(1)} %iota.30.labels_ref, bf16[512,1152]{1,0:T(8,128)(2,1)S(1)} %bitcast.39, bf16[1024,1024]{1,0:T(8,128)(2,1)} %bitcast.47), custom_call_target="tpu_custom_call" | custom-call | flops 1207959552 | bytes 3538944 | tf_op jit(solution)/shard_map/low/pallas_call | solution.py:130
  96.2 0.1 collective-permute-start.4
  96.3 1.2 collective-permute-done.4
  97.6 2.7 %collective-permute-start.6 = (f32[16,512]{1,0:T(8,128)S(1)}, f32[16,512]{1,0:T(8,128)S(1)}, u32[]{:S(2)}, u32[]{:S(2)}) collective-permute-start(f32[16,512]{1,0:T(8,128)S(1)} %add.175), channel_id=1, source_target_pairs={{0,4},{1,5},{2,6},{3,7},{4,0},{5,1},{6,2},{7,3},{8,12},{9,13},{10,... | collective-permute-start | bytes 98312 | tf_op jit(solution)/shard_map/ppermute | solution.py:268
  100.3 1.4 collective-permute-start.5
  101.7 0.1 broadcast_in_dim.11
  101.7 0.1 broadcast_in_dim.22
  101.8 0.1 slice.89
  101.9 0.1 copy.11
  102.0 0.7 collective-permute-done.7
  102.7 0.4 collective-permute-done.6
  103.0 1.1 collective-permute-done.5
  104.2 4.7 %delta.7 = bf16[512,1280]{1,0:T(8,128)(2,1)} custom-call(f32[16,512]{1,0:T(8,128)S(1)} %add_add_fusion.1.low_ref, bf16[512,1152]{1,0:T(8,128)(2,1)S(1)} %bitcast.40, bf16[1024,1280]{1,0:T(8,128)(2,1)} %bitcast.43), custom_call_target="tpu_custom_call" | custom-call | flops 1342177280 | bytes 3932160 | tf_op jit(solution)/shard_map/delta/pallas_call | solution.py:166
  108.9 6.1 %all-to-all-start.3 = ((bf16[16,32,1280]{2,1,0:T(8,128)(2,1)}), bf16[16,32,1280]{2,1,0:T(8,128)(2,1)S(1)}, u32[]{:S(2)}, u32[]{:S(2)}) async-start(bf16[16,32,1280]{2,1,0:T(8,128)(2,1)} %bitcast.10), calls=%async_computation.3 | async-start | bytes 2621440 | tf_op jit(solution)/shard_map/all_to_all | solution.py:211
  115.0 0.2 copy.12
  115.2 22.2 %all-gather.5.cloned.1.call-done.down_ref.weights_ref = bf16[1024,2304]{1,0:T(8,128)(2,1)} async-done(((bf16[64,2304]{1,0:T(8,128)(2,1)}), bf16[1024,2304]{1,0:T(8,128)(2,1)}) %all-gather.5.cloned.1.call-update) | async-done | bytes 4718608 | tf_op jit(solution)/shard_map/all_gather | solution.py:303
  137.4 2.3 %copy-done = bf16[1024,2304]{1,0:T(8,128)(2,1)S(1)} copy-done((bf16[1024,2304]{1,0:T(8,128)(2,1)S(1)}, bf16[1024,2304]{1,0:T(8,128)(2,1)}, u32[]{:S(2)}) %copy-start) | copy-done | bytes 4718616
  139.7 1.3 low.9
  141.0 0.1 collective-permute-start.20
  141.1 0.7 slice_reduce_fusion
  141.8 0.5 slice.92
  142.3 2.7 %collective-permute-start.23 = (f32[16,128]{1,0:T(8,128)S(1)}, f32[16,128]{1,0:T(8,128)S(1)}, u32[]{:S(2)}, u32[]{:S(2)}) collective-permute-start(f32[16,128]{1,0:T(8,128)S(1)} %add.193), channel_id=1, source_target_pairs={{0,6},{1,7},{2,4},{3,5},{4,2},{5,3},{6,0},{7,1},{8,14},{9,15},{10,... | collective-permute-start | bytes 24584 | tf_op jit(solution)/shard_map/ppermute | solution.py:268
  145.0 0.8 collective-permute-start.22
  145.9 0.5 collective-permute-start.21
  146.4 1.2 compare_reduce_fusion.1
  150.8 0.2 while.15
  151.0 2.3 %copy-done.1 = bf16[1024,2304]{1,0:T(8,128)(2,1)S(1)} copy-done((bf16[1024,2304]{1,0:T(8,128)(2,1)S(1)}, bf16[1024,2304]{1,0:T(8,128)(2,1)}, u32[]{:S(2)}) %copy-start.1) | copy-done | bytes 4718616
  153.3 4.5 %finish.1 = bf16[512,1280]{1,0:T(8,128)(2,1)} custom-call(s32[1]{0:T(128)} %bitcast.9.full_ref, s32[8,1024]{1,0:T(8,128)S(1)} %broadcast_in_dim.23.labels_ref, s32[512,128]{1,0:T(8,128)S(1)} %get-tuple-element.333.tall_ref, f32[16,128]{1,0:T(8,128)S(1)} %add_add_fusion.2.low_ref, bf16[128,1152]{1,0:T(8,128)(2,1)S(1)} %get-tuple-element.335.rows_ref, ...), custom_call_target="tpu_custom_call" | custom-call | flops 1207959552 | bytes 3932160 | tf_op jit(solution)/shard_map/finish/pallas_call | solution.py:197
  (38 shorter events, 0.3 us)
Async XLA Ops:
  6.5 55.2 %all-gather.3.cloned.1.call-start = ((), (), s32[]{:S(2)}) async-start(), calls=%async_computation.4 | async-start | bytes 9437184 | tf_op jit(solution)/shard_map/all_gather | solution.py:296
  7.3 130.2 %all-gather.5.cloned.1.call-start = ((), (), s32[]{:S(2)}) async-start(), calls=%async_computation.5 | async-start | bytes 5013504 | tf_op jit(solution)/shard_map/all_gather | solution.py:303
  7.3 22.5 %copy-start.7 = (u32[128]{0:T(128)S(1)}, u32[128]{0:T(128)}, u32[]{:S(2)}) copy-start(u32[128]{0:T(128)} %constant.217) | copy-start | bytes 1540
  7.3 23.7 %copy-start.6 = (s32[64]{0:T(128)S(1)}, s32[64]{0:T(128)}, u32[]{:S(2)}) copy-start(s32[64]{0:T(128)} %param.8) | copy-start | bytes 772
  10.8 16.7 %collective-permute-start.13 = (bf16[128,2304]{1,0:T(8,128)(2,1)S(1)}, bf16[128,2304]{1,0:T(8,128)(2,1)S(1)}, u32[]{:S(2)}, u32[]{:S(2)}) collective-permute-start(bf16[128,2304]{1,0:T(8,128)(2,1)S(1)} %get-tuple-element.447), channel_id=1, source_target_pairs={{0,24},{8,0},{16,8},{24,16},{32,56},{40,32},{48,40},{56,48},{64,88... | collective-permute-start | bytes 1769480 | tf_op jit(solution)/shard_map/ppermute | solution.py:223
  14.9 29.4 %collective-permute-start.8 = (bf16[128,2304]{1,0:T(8,128)(2,1)}, bf16[128,2304]{1,0:T(8,128)(2,1)}, u32[]{:S(2)}, u32[]{:S(2)}) collective-permute-start(bf16[128,2304]{1,0:T(8,128)(2,1)} %get-tuple-element.449), channel_id=1, source_target_pairs={{0,32},{8,40},{16,48},{24,56},{32,64},{40,72},{48,80},{56,88},{64,... | collective-permute-start | bytes 1769480 | tf_op jit(solution)/shard_map/ppermute | solution.py:223
  16.4 27.9 %collective-permute-start.9 = (bf16[128,2304]{1,0:T(8,128)(2,1)}, bf16[128,2304]{1,0:T(8,128)(2,1)}, u32[]{:S(2)}, u32[]{:S(2)}) collective-permute-start(bf16[128,2304]{1,0:T(8,128)(2,1)} %get-tuple-element.450), channel_id=1, source_target_pairs={{0,64},{8,72},{16,80},{24,88},{32,96},{40,104},{48,112},{56,120},{... | collective-permute-start | bytes 1769480 | tf_op jit(solution)/shard_map/ppermute | solution.py:223
  17.5 27.0 %collective-permute-start.10 = (bf16[128,2304]{1,0:T(8,128)(2,1)S(1)}, bf16[128,2304]{1,0:T(8,128)(2,1)}, u32[]{:S(2)}, u32[]{:S(2)}) collective-permute-start(bf16[128,2304]{1,0:T(8,128)(2,1)S(1)} %get-tuple-element.451), channel_id=1, source_target_pairs={{0,96},{8,104},{16,112},{24,120},{32,0},{40,8},{48,16},{56,24},{64... | collective-permute-start | bytes 1769480 | tf_op jit(solution)/shard_map/ppermute | solution.py:223
  19.6 27.9 %collective-permute-start.11 = (bf16[128,2304]{1,0:T(8,128)(2,1)S(1)}, bf16[128,2304]{1,0:T(8,128)(2,1)}, u32[]{:S(2)}, u32[]{:S(2)}) collective-permute-start(bf16[128,2304]{1,0:T(8,128)(2,1)S(1)} %get-tuple-element.453), channel_id=1, source_target_pairs={{0,8},{8,16},{16,24},{24,0},{32,40},{40,48},{48,56},{56,32},{64,72... | collective-permute-start | bytes 1769480 | tf_op jit(solution)/shard_map/ppermute | solution.py:223
  27.5 2.3 %copy-start.4 = (bf16[128,2304]{1,0:T(8,128)(2,1)}, bf16[128,2304]{1,0:T(8,128)(2,1)S(1)}, u32[]{:S(2)}) copy-start(bf16[128,2304]{1,0:T(8,128)(2,1)S(1)} %collective-permute-done.13) | copy-start | bytes 1769476
  27.5 20.1 %collective-permute-start.12 = (bf16[128,2304]{1,0:T(8,128)(2,1)S(1)}, bf16[128,2304]{1,0:T(8,128)(2,1)}, u32[]{:S(2)}, u32[]{:S(2)}) collective-permute-start(bf16[128,2304]{1,0:T(8,128)(2,1)S(1)} %get-tuple-element.454), channel_id=1, source_target_pairs={{0,16},{8,24},{16,0},{24,8},{32,48},{40,56},{48,32},{56,40},{64,80... | collective-permute-start | bytes 1769480 | tf_op jit(solution)/shard_map/ppermute | solution.py:223
  44.5 6.4 %copy-start.5 = (bf16[128,2304]{1,0:T(8,128)(2,1)S(1)}, bf16[128,2304]{1,0:T(8,128)(2,1)}, u32[]{:S(2)}) copy-start(bf16[128,2304]{1,0:T(8,128)(2,1)} %copy-done.4) | copy-start | bytes 1769476
  48.8 5.5 %collective-permute-start.16 = (bf16[32,2304]{1,0:T(8,128)(2,1)S(1)}, bf16[32,2304]{1,0:T(8,128)(2,1)S(1)}, u32[]{:S(2)}, u32[]{:S(2)}) collective-permute-start(bf16[32,2304]{1,0:T(8,128)(2,1)S(1)} %get-tuple-element.455), channel_id=1, source_target_pairs={{0,24},{8,0},{16,8},{24,16},{32,56},{40,32},{48,40},{56,48},{64,88... | collective-permute-start | bytes 442376 | tf_op jit(solution)/shard_map/ppermute | solution.py:223
  48.9 7.4 %collective-permute-start.15 = (bf16[32,2304]{1,0:T(8,128)(2,1)S(1)}, bf16[32,2304]{1,0:T(8,128)(2,1)S(1)}, u32[]{:S(2)}, u32[]{:S(2)}) collective-permute-start(bf16[32,2304]{1,0:T(8,128)(2,1)S(1)} %get-tuple-element.456), channel_id=1, source_target_pairs={{0,16},{8,24},{16,0},{24,8},{32,48},{40,56},{48,32},{56,40},{64,80... | collective-permute-start | bytes 442376 | tf_op jit(solution)/shard_map/ppermute | solution.py:223
  50.0 7.2 %collective-permute-start.14 = (bf16[32,2304]{1,0:T(8,128)(2,1)S(1)}, bf16[32,2304]{1,0:T(8,128)(2,1)S(1)}, u32[]{:S(2)}, u32[]{:S(2)}) collective-permute-start(bf16[32,2304]{1,0:T(8,128)(2,1)S(1)} %get-tuple-element.457), channel_id=1, source_target_pairs={{0,8},{8,16},{16,24},{24,0},{32,40},{40,48},{48,56},{56,32},{64,72... | collective-permute-start | bytes 442376 | tf_op jit(solution)/shard_map/ppermute | solution.py:223
  52.1 5.7 %collective-permute-start.19 = (bf16[32,2304]{1,0:T(8,128)(2,1)S(1)}, bf16[32,2304]{1,0:T(8,128)(2,1)S(1)}, u32[]{:S(2)}, u32[]{:S(2)}) collective-permute-start(bf16[32,2304]{1,0:T(8,128)(2,1)S(1)} %get-tuple-element.458), channel_id=1, source_target_pairs={{0,96},{8,104},{16,112},{24,120},{32,0},{40,8},{48,16},{56,24},{64... | collective-permute-start | bytes 442376 | tf_op jit(solution)/shard_map/ppermute | solution.py:223
  53.6 6.6 %collective-permute-start.18 = (bf16[32,2304]{1,0:T(8,128)(2,1)S(1)}, bf16[32,2304]{1,0:T(8,128)(2,1)S(1)}, u32[]{:S(2)}, u32[]{:S(2)}) collective-permute-start(bf16[32,2304]{1,0:T(8,128)(2,1)S(1)} %get-tuple-element.459), channel_id=1, source_target_pairs={{0,64},{8,72},{16,80},{24,88},{32,96},{40,104},{48,112},{56,120},{... | collective-permute-start | bytes 442376 | tf_op jit(solution)/shard_map/ppermute | solution.py:223
  54.3 6.7 %collective-permute-start.17 = (bf16[32,2304]{1,0:T(8,128)(2,1)S(1)}, bf16[32,2304]{1,0:T(8,128)(2,1)S(1)}, u32[]{:S(2)}, u32[]{:S(2)}) collective-permute-start(bf16[32,2304]{1,0:T(8,128)(2,1)S(1)} %get-tuple-element.460), channel_id=1, source_target_pairs={{0,32},{8,40},{16,48},{24,56},{32,64},{40,72},{48,80},{56,88},{64,... | collective-permute-start | bytes 442376 | tf_op jit(solution)/shard_map/ppermute | solution.py:223
  65.0 28.3 %all-to-all-start.2 = ((bf16[16,32,1152]{2,1,0:T(8,128)(2,1)}), bf16[16,32,1152]{2,1,0:T(8,128)(2,1)S(1)}, u32[]{:S(2)}, u32[]{:S(2)}) async-start(bf16[16,32,1152]{2,1,0:T(8,128)(2,1)} %bitcast.2), calls=%async_computation.2 | async-start | bytes 2359296 | tf_op jit(solution)/shard_map/all_to_all | solution.py:211
  96.2 1.3 collective-permute-start.4
  97.5 5.1 %collective-permute-start.7 = (f32[16,512]{1,0:T(8,128)S(1)}, f32[16,512]{1,0:T(8,128)S(1)}, u32[]{:S(2)}, u32[]{:S(2)}) collective-permute-start(f32[16,512]{1,0:T(8,128)S(1)} %add.175), channel_id=1, source_target_pairs={{0,6},{1,7},{2,4},{3,5},{4,2},{5,3},{6,0},{7,1},{8,14},{9,15},{10,... | collective-permute-start | bytes 98312 | tf_op jit(solution)/shard_map/ppermute | solution.py:268
  97.6 5.5 %collective-permute-start.6 = (f32[16,512]{1,0:T(8,128)S(1)}, f32[16,512]{1,0:T(8,128)S(1)}, u32[]{:S(2)}, u32[]{:S(2)}) collective-permute-start(f32[16,512]{1,0:T(8,128)S(1)} %add.175), channel_id=1, source_target_pairs={{0,4},{1,5},{2,6},{3,7},{4,0},{5,1},{6,2},{7,3},{8,12},{9,13},{10,... | collective-permute-start | bytes 98312 | tf_op jit(solution)/shard_map/ppermute | solution.py:268
  100.3 3.9 %collective-permute-start.5 = (f32[16,512]{1,0:T(8,128)S(1)}, f32[16,512]{1,0:T(8,128)S(1)}, u32[]{:S(2)}, u32[]{:S(2)}) collective-permute-start(f32[16,512]{1,0:T(8,128)S(1)} %add.175), channel_id=1, source_target_pairs={{0,2},{1,3},{2,0},{3,1},{4,6},{5,7},{6,4},{7,5},{8,10},{9,11},{10,... | collective-permute-start | bytes 98312 | tf_op jit(solution)/shard_map/ppermute | solution.py:268
  108.9 41.8 %all-to-all-start.3 = ((bf16[16,32,1280]{2,1,0:T(8,128)(2,1)}), bf16[16,32,1280]{2,1,0:T(8,128)(2,1)S(1)}, u32[]{:S(2)}, u32[]{:S(2)}) async-start(bf16[16,32,1280]{2,1,0:T(8,128)(2,1)} %bitcast.10), calls=%async_computation.3 | async-start | bytes 2621440 | tf_op jit(solution)/shard_map/all_to_all | solution.py:211
  137.4 2.3 %copy-start = (bf16[1024,2304]{1,0:T(8,128)(2,1)S(1)}, bf16[1024,2304]{1,0:T(8,128)(2,1)}, u32[]{:S(2)}) copy-start(bf16[1024,2304]{1,0:T(8,128)(2,1)} %all-gather.5.cloned.1.call-done.down_ref.weights_ref) | copy-start | bytes 14155780
  141.0 1.3 collective-permute-start.20
  142.3 8.4 %collective-permute-start.23 = (f32[16,128]{1,0:T(8,128)S(1)}, f32[16,128]{1,0:T(8,128)S(1)}, u32[]{:S(2)}, u32[]{:S(2)}) collective-permute-start(f32[16,128]{1,0:T(8,128)S(1)} %add.193), channel_id=1, source_target_pairs={{0,6},{1,7},{2,4},{3,5},{4,2},{5,3},{6,0},{7,1},{8,14},{9,15},{10,... | collective-permute-start | bytes 24584 | tf_op jit(solution)/shard_map/ppermute | solution.py:268
  145.0 5.7 %collective-permute-start.22 = (f32[16,128]{1,0:T(8,128)S(1)}, f32[16,128]{1,0:T(8,128)S(1)}, u32[]{:S(2)}, u32[]{:S(2)}) collective-permute-start(f32[16,128]{1,0:T(8,128)S(1)} %add.193), channel_id=1, source_target_pairs={{0,4},{1,5},{2,6},{3,7},{4,0},{5,1},{6,2},{7,3},{8,12},{9,13},{10,... | collective-permute-start | bytes 24584 | tf_op jit(solution)/shard_map/ppermute | solution.py:268
  145.9 4.8 %collective-permute-start.21 = (f32[16,128]{1,0:T(8,128)S(1)}, f32[16,128]{1,0:T(8,128)S(1)}, u32[]{:S(2)}, u32[]{:S(2)}) collective-permute-start(f32[16,128]{1,0:T(8,128)S(1)} %add.193), channel_id=1, source_target_pairs={{0,2},{1,3},{2,0},{3,1},{4,6},{5,7},{6,4},{7,5},{8,10},{9,11},{10,... | collective-permute-start | bytes 24584 | tf_op jit(solution)/shard_map/ppermute | solution.py:268
  151.0 2.3 %copy-start.1 = (bf16[1024,2304]{1,0:T(8,128)(2,1)S(1)}, bf16[1024,2304]{1,0:T(8,128)(2,1)}, u32[]{:S(2)}) copy-start(bf16[1024,2304]{1,0:T(8,128)(2,1)} %all-gather.5.cloned.1.call-done.down_ref.weights_ref) | copy-start | bytes 14155780
Sparse Core Ops, SparseCore 0:
  9.1 52.1 all-gather.2
  63.5 73.8 all-gather.4
